TPU v7x, 32 devices: a whole 2x2x4 slice. The times are simulated.
32 devices in a mesh: fsdp: 8 (over z, x), tp: 4 (over y, core).
Axes of the slice: x: 2, y: 2, z: 4, core: 2. Of those that a mesh axis runs over, the one named last changes fastest.
Arguments:
- layer_input: bfloat16 [8192, 2048], P(('fsdp', 'tp')), may hold values from -6 to 6
- out_cotangent: bfloat16 [8192, 2048], P(('fsdp', 'tp')), may hold values from -6 to 6
- segments: int32 [8, 1024], P('fsdp'), may hold values from 0 to 2, as said below
- qkv_weight: float32 [1, 3, 2048, 2048], P(None, None, 'fsdp', 'tp'), may hold values from -0.125 to 0.125
- qkv_first: float32 [1, 3, 2048, 2048], P(None, None, 'fsdp', 'tp'), may hold values from -16 to 16
- qkv_second: float32 [1, 3, 2048, 2048], P(None, None, 'fsdp', 'tp'), may hold values from 19.6608 to 311.296
- out_weight: float32 [1, 2048, 2048], P(None, ('tp', 'fsdp')), may hold values from -0.5 to 0.5
- out_first: float32 [1, 2048, 2048], P(None, ('tp', 'fsdp')), may hold values from -6 to 6
- out_second: float32 [1, 2048, 2048], P(None, ('tp', 'fsdp')), may hold values from 2.12992 to 34.4064
- up_weight: float32 [1, 2048, 8192], P(None, 'fsdp', 'tp'), may hold values from -0.125 to 0.125
- up_first: float32 [1, 2048, 8192], P(None, 'fsdp', 'tp'), may hold values from -16 to 16
- up_second: float32 [1, 2048, 8192], P(None, 'fsdp', 'tp'), may hold values from 19.6608 to 311.296
- down_weight: float32 [1, 8192, 2048], P(None, ('tp', 'fsdp')), may hold values from -0.0625 to 0.0625
- down_first: float32 [1, 8192, 2048], P(None, ('tp', 'fsdp')), may hold values from -32 to 32
- down_second: float32 [1, 8192, 2048], P(None, ('tp', 'fsdp')), may hold values from 77.824 to 1228.8
- small_params: float32 [1, 26624], replicated
- small_first: float32 [1, 26624], replicated, may hold values from -32 to 32
- small_second: float32 [1, 26624], replicated, may hold values from 54.0672 to 860.16
Outputs:
- layer_output: float32 [8192, 2048], P(('fsdp', 'tp'))
- input_grad: float32 [8192, 2048], P(('fsdp', 'tp'))
- qkv_first_new: float32 [1, 3, 2048, 2048], P(None, None, 'fsdp', 'tp')
- qkv_second_new: float32 [1, 3, 2048, 2048], P(None, None, 'fsdp', 'tp')
- qkv_new: float32 [1, 3, 2048, 2048], P(None, None, 'fsdp', 'tp')
- out_first_new: float32 [1, 2048, 2048], P(None, ('tp', 'fsdp'))
- out_second_new: float32 [1, 2048, 2048], P(None, ('tp', 'fsdp'))
- out_new: float32 [1, 2048, 2048], P(None, ('tp', 'fsdp'))
- up_first_new: float32 [1, 2048, 8192], P(None, 'fsdp', 'tp')
- up_second_new: float32 [1, 2048, 8192], P(None, 'fsdp', 'tp')
- up_new: float32 [1, 2048, 8192], P(None, 'fsdp', 'tp')
- down_first_new: float32 [1, 8192, 2048], P(None, ('tp', 'fsdp'))
- down_second_new: float32 [1, 8192, 2048], P(None, ('tp', 'fsdp'))
- down_new: float32 [1, 8192, 2048], P(None, ('tp', 'fsdp'))
- small_first_new: float32 [1, 26624], replicated
- small_second_new: float32 [1, 26624], replicated
- small_new: float32 [1, 26624], replicated
Inputs may be any that keep to these rules, and one draw needn't show every extreme that they name: `segments`: each sequence holds two or three documents numbered from 0 in order, none empty. One of them, the middle one, begins within the first 256 positions and ends within the last 256 positions. Before it there may be one document that starts the sequence; after it there is always one document that ends the sequence, of fewer than 256 tokens.
All inputs are finite; a program needn't handle non-finite values.
Results may differ from a plain program's by a relative error of at most 0.019.
Values may be sent and summed in bfloat16 or wider, within the bound.
A program may use at most 192 MiB of HBM per device.

v0:
```python
import jax
import jax.numpy as jnp
from jax import lax
from jax.sharding import PartitionSpec as P

HD = 256
ROT = 64
STEP = 10


norm_eps = 1e-05
beta_one = 0.9
beta_two = 0.95
adam_eps = 1e-08
decay_rate = 0.01
rate_vector = 0.2
masked_score = -1e30


def norm_forward(stream, gain, shift):
    mean_row = jnp.mean(stream, axis=-1, keepdims=True)
    centred = stream - mean_row
    spread = jnp.mean(centred * centred, axis=-1, keepdims=True)
    inverse = lax.rsqrt(spread + norm_eps)
    normal = centred * inverse
    return (normal * gain + shift, normal, inverse)


def norm_backward(grad_out, normal, inverse, gain):
    gain_grad = jnp.sum(grad_out * normal, axis=0)
    shift_grad = jnp.sum(grad_out, axis=0)
    scaled = grad_out * gain
    inner = (
        scaled
        - jnp.mean(scaled, axis=-1, keepdims=True)
        - normal * jnp.mean(scaled * normal, axis=-1, keepdims=True)
    )
    return (inner * inverse, gain_grad, shift_grad)


def rotary_tables(seg_ids):
    length = seg_ids.shape[0]
    indices = jnp.arange(length, dtype=jnp.int32)
    earlier = jnp.sum((seg_ids[None, :] < seg_ids[:, None]).astype(jnp.int32), axis=1)
    position = (indices - earlier).astype(jnp.float32)
    inverse_freq = 10000.0 ** (-jnp.arange(0, ROT, 2).astype(jnp.float32) / ROT)
    angle = position[:, None] * inverse_freq[None, :]
    return (jnp.cos(angle), jnp.sin(angle))


def rotate(values, cosine, sine):
    half_dims = cosine.shape[-1]
    first_half = values[..., :half_dims]
    second_half = values[..., half_dims : 2 * half_dims]
    remainder = values[..., 2 * half_dims :]
    cosine = cosine[:, None, :]
    sine = sine[:, None, :]
    return jnp.concatenate(
        [
            first_half * cosine - second_half * sine,
            second_half * cosine + first_half * sine,
            remainder,
        ],
        axis=-1,
    )


def gelu_slope(pre_act):
    normal_cdf = 0.5 * lax.erfc(-pre_act * 0.7071067811865476)
    density = jnp.exp(-0.5 * pre_act * pre_act) * 0.3989422804014327
    return normal_cdf + pre_act * density


def allowed_block(seg_ids, offset, count):
    length = seg_ids.shape[0]
    query_idx = offset + jnp.arange(count, dtype=jnp.int32)
    key_idx = jnp.arange(length, dtype=jnp.int32)
    query_seg = seg_ids[offset : offset + count]
    return (key_idx[None, :] <= query_idx[:, None]) & (seg_ids[None, :] == query_seg[:, None])


def block_scores(query_rows, key_rows, seg_ids, offset, count):
    scores = jnp.einsum(
        "qhd,khd->hqk", query_rows, key_rows, preferred_element_type=jnp.float32
    ) * HD ** (-0.5)
    allowed = allowed_block(seg_ids, offset, count)
    return jnp.where(allowed[None], scores, masked_score)


def attend(query_rows, key_rows, value_rows, seg_ids, block_rows):
    length = key_rows.shape[0]
    outputs = []
    totals = []
    for offset in range(0, length, block_rows):
        scores = block_scores(
            query_rows[offset : offset + block_rows], key_rows, seg_ids, offset, block_rows
        )
        peak = jnp.max(scores, axis=-1, keepdims=True)
        total = jnp.log(jnp.sum(jnp.exp(scores - peak), axis=-1, keepdims=True)) + peak
        weights = jnp.exp(scores - total).astype(jnp.bfloat16)
        outputs.append(
            jnp.einsum("hqk,khd->qhd", weights, value_rows, preferred_element_type=jnp.float32)
        )
        totals.append(total)
    return (jnp.concatenate(outputs, axis=0), jnp.concatenate(totals, axis=1))


def attend_back(query_rows, key_rows, value_rows, out_grad, totals, seg_ids, block_rows):
    length = key_rows.shape[0]
    query_parts = []
    key_grad = jnp.zeros(key_rows.shape, jnp.float32)
    value_grad = jnp.zeros(value_rows.shape, jnp.float32)
    for offset in range(0, length, block_rows):
        rows_now = query_rows[offset : offset + block_rows]
        back_now = out_grad[offset : offset + block_rows]
        scores = block_scores(rows_now, key_rows, seg_ids, offset, block_rows)
        probs = jnp.exp(scores - totals[:, offset : offset + block_rows])
        weights = probs.astype(jnp.bfloat16)
        prob_grad = jnp.einsum(
            "qhd,khd->hqk", back_now, value_rows, preferred_element_type=jnp.float32
        )
        inner = jnp.sum(probs * prob_grad, axis=-1, keepdims=True)
        score_grad = (probs * (prob_grad - inner)).astype(jnp.bfloat16)
        query_parts.append(
            jnp.einsum("hqk,khd->qhd", score_grad, key_rows, preferred_element_type=jnp.float32)
            * HD ** (-0.5)
        )
        key_grad = key_grad + jnp.einsum(
            "hqk,qhd->khd", score_grad, rows_now, preferred_element_type=jnp.float32
        ) * HD ** (-0.5)
        value_grad = value_grad + jnp.einsum(
            "hqk,qhd->khd", weights, back_now, preferred_element_type=jnp.float32
        )
    return (jnp.concatenate(query_parts, axis=0), key_grad, value_grad)


def branch_term(mixed_rows, active, out_full, down_full):
    return jnp.dot(mixed_rows, out_full, preferred_element_type=jnp.float32) + jnp.dot(
        active, down_full, preferred_element_type=jnp.float32
    )


def adam_step(weight, first, second, grad, rate, decay):
    first_new = beta_one * first + (1.0 - beta_one) * grad
    second_new = beta_two * second + (1.0 - beta_two) * grad * grad
    first_hat = first_new / (1.0 - beta_one**STEP)
    second_hat = second_new / (1.0 - beta_two**STEP)
    weight_new = weight - rate * (first_hat / (jnp.sqrt(second_hat) + adam_eps) + decay * weight)
    return (first_new, second_new, weight_new)


def local(
    layer_input,
    out_cotangent,
    segments,
    qkv_weight,
    qkv_first,
    qkv_second,
    out_weight,
    out_first,
    out_second,
    up_weight,
    up_first,
    up_second,
    down_weight,
    down_first,
    down_second,
    small_params,
    small_first,
    small_second,
):
    tp_rank = lax.axis_index("tp")
    model_width = layer_input.shape[1]
    layer_count = qkv_weight.shape[0]
    local_width = qkv_weight.shape[3]
    local_hidden = up_weight.shape[2]
    hidden_all = small_params.shape[1] - 9 * model_width
    local_heads = local_width // HD
    seg_ids = segments[0]
    length = seg_ids.shape[0]
    block_rows = min(length, 512)
    cosine, sine = rotary_tables(seg_ids)
    rate_matrix = model_width ** (-0.5)
    rate_output = 4.0 * model_width ** (-0.5)

    def weight_shards(layer_idx):
        return (
            qkv_weight[layer_idx].astype(jnp.bfloat16),
            out_weight[layer_idx].astype(jnp.bfloat16),
            up_weight[layer_idx].astype(jnp.bfloat16),
            down_weight[layer_idx].astype(jnp.bfloat16),
        )

    def unpack(layer_idx):
        vector = small_params[layer_idx]
        qkv_bias = lax.dynamic_slice_in_dim(
            vector[6 * model_width : 9 * model_width].reshape(3, model_width),
            tp_rank * local_width,
            local_width,
            1,
        )
        up_bias = lax.dynamic_slice_in_dim(
            vector[9 * model_width :], tp_rank * local_hidden, local_hidden, 0
        )
        return (
            vector[0:model_width],
            vector[model_width : 2 * model_width],
            vector[2 * model_width : 3 * model_width],
            vector[3 * model_width : 4 * model_width],
            vector[4 * model_width : 5 * model_width],
            vector[5 * model_width : 6 * model_width],
            qkv_bias,
            up_bias,
        )

    stream = layer_input.astype(jnp.float32)
    layer_idx = 0
    gain_one, shift_one, gain_two, shift_two, bias_out, bias_down, qkv_bias, up_bias = unpack(
        layer_idx
    )
    qkv_shard, out_shard, up_shard, down_shard = weight_shards(layer_idx)
    qkv_full = lax.all_gather(qkv_shard, "fsdp", axis=1, tiled=True)
    out_full = lax.all_gather(out_shard, "fsdp", axis=0, tiled=True)
    up_full = lax.all_gather(up_shard, "fsdp", axis=0, tiled=True)
    down_full = lax.all_gather(down_shard, "fsdp", axis=0, tiled=True)
    normed_one, normal_one, inverse_one = norm_forward(stream, gain_one, shift_one)
    normed_two, normal_two, inverse_two = norm_forward(stream, gain_two, shift_two)
    rows_one = lax.all_gather(normed_one.astype(jnp.bfloat16), "tp", axis=0, tiled=True)
    rows_two = lax.all_gather(normed_two.astype(jnp.bfloat16), "tp", axis=0, tiled=True)
    projected = (
        jnp.einsum("sd,cdh->csh", rows_one, qkv_full, preferred_element_type=jnp.float32)
        + qkv_bias[:, None, :]
    )
    query_rows = rotate(projected[0].reshape(length, local_heads, HD), cosine, sine).astype(
        jnp.bfloat16
    )
    key_rows = rotate(projected[1].reshape(length, local_heads, HD), cosine, sine).astype(
        jnp.bfloat16
    )
    value_rows = projected[2].reshape(length, local_heads, HD).astype(jnp.bfloat16)
    attended, totals = attend(query_rows, key_rows, value_rows, seg_ids, block_rows)
    mixed_rows = attended.astype(jnp.bfloat16).reshape(length, local_width)
    pre_act = jnp.dot(rows_two, up_full, preferred_element_type=jnp.float32) + up_bias
    active = jax.nn.gelu(pre_act, approximate=False).astype(jnp.bfloat16)
    branch = lax.psum_scatter(
        branch_term(mixed_rows, active, out_full, down_full).astype(jnp.bfloat16),
        "tp",
        scatter_dimension=0,
        tiled=True,
    ).astype(jnp.float32)
    saved = [
        (
            normal_one,
            inverse_one,
            normal_two,
            inverse_two,
            rows_one,
            rows_two,
            query_rows,
            key_rows,
            value_rows,
            totals,
            mixed_rows,
            pre_act,
            active,
            (qkv_full, out_full, up_full, down_full),
        )
    ]
    stream = stream + branch + bias_out + bias_down
    gradient = out_cotangent.astype(jnp.float32)
    weight_grads = [None] * layer_count
    small_grads = [None] * layer_count
    for layer_idx in reversed(range(layer_count)):
        (
            normal_one,
            inverse_one,
            normal_two,
            inverse_two,
            rows_one,
            rows_two,
            query_rows,
            key_rows,
            value_rows,
            totals,
            mixed_rows,
            pre_act,
            active,
            kept_weights,
        ) = saved[layer_idx]
        gain_one, shift_one, gain_two, shift_two, bias_out, bias_down, qkv_bias, up_bias = unpack(
            layer_idx
        )
        qkv_shard, out_shard, up_shard, down_shard = weight_shards(layer_idx)
        qkv_full, out_full, up_full, down_full = (
            lax.all_gather(qkv_shard, "fsdp", axis=1, tiled=True),
            lax.all_gather(out_shard, "fsdp", axis=0, tiled=True),
            lax.all_gather(up_shard, "fsdp", axis=0, tiled=True),
            lax.all_gather(down_shard, "fsdp", axis=0, tiled=True),
        )
        bias_grad = jnp.sum(gradient, axis=0)
        back_rows = lax.all_gather(gradient.astype(jnp.bfloat16), "tp", axis=0, tiled=True)
        out_grad = jnp.einsum(
            "sh,sd->hd", mixed_rows, back_rows, preferred_element_type=jnp.float32
        )
        down_grad = jnp.einsum("sf,sd->fd", active, back_rows, preferred_element_type=jnp.float32)
        active_grad = jnp.einsum(
            "sd,fd->sf", back_rows, down_full, preferred_element_type=jnp.float32
        )
        pre_grad = (active_grad * gelu_slope(pre_act)).astype(jnp.bfloat16)
        up_grad = jnp.einsum("sd,sf->df", rows_two, pre_grad, preferred_element_type=jnp.float32)
        up_bias_grad = jnp.sum(pre_grad, axis=0, dtype=jnp.float32)
        mixed_grad = (
            jnp.einsum("sd,hd->sh", back_rows, out_full, preferred_element_type=jnp.float32)
            .astype(jnp.bfloat16)
            .reshape(length, local_heads, HD)
        )
        query_grad, key_grad, value_grad = attend_back(
            query_rows, key_rows, value_rows, mixed_grad, totals, seg_ids, block_rows
        )
        query_grad = rotate(query_grad, cosine, -sine)
        key_grad = rotate(key_grad, cosine, -sine)
        proj_grad = (
            jnp.stack([query_grad, key_grad, value_grad])
            .reshape(3, length, local_width)
            .astype(jnp.bfloat16)
        )
        qkv_grad = jnp.einsum(
            "sd,csh->cdh", rows_one, proj_grad, preferred_element_type=jnp.float32
        )
        qkv_bias_grad = jnp.sum(proj_grad, axis=1, dtype=jnp.float32)
        first_norm = jnp.einsum(
            "csh,cdh->sd", proj_grad, qkv_full, preferred_element_type=jnp.float32
        )
        second_norm = jnp.einsum("sf,df->sd", pre_grad, up_full, preferred_element_type=jnp.float32)
        first_local, second_local = (
            lax.psum_scatter(
                first_norm.astype(jnp.bfloat16), "tp", scatter_dimension=0, tiled=True
            ).astype(jnp.float32),
            lax.psum_scatter(
                second_norm.astype(jnp.bfloat16), "tp", scatter_dimension=0, tiled=True
            ).astype(jnp.float32),
        )
        qkv_part, out_part, down_part, up_part = (
            lax.psum_scatter(
                qkv_grad.astype(jnp.bfloat16), "fsdp", scatter_dimension=1, tiled=True
            ).astype(jnp.float32),
            lax.psum_scatter(
                out_grad.astype(jnp.bfloat16), "fsdp", scatter_dimension=0, tiled=True
            ).astype(jnp.float32),
            lax.psum_scatter(
                down_grad.astype(jnp.bfloat16), "fsdp", scatter_dimension=0, tiled=True
            ).astype(jnp.float32),
            lax.psum_scatter(
                up_grad.astype(jnp.bfloat16), "fsdp", scatter_dimension=0, tiled=True
            ).astype(jnp.float32),
        )
        input_one, gain_one_grad, shift_one_grad = norm_backward(
            first_local, normal_one, inverse_one, gain_one
        )
        input_two, gain_two_grad, shift_two_grad = norm_backward(
            second_local, normal_two, inverse_two, gain_two
        )
        gradient = gradient + input_one + input_two
        qkv_spread = lax.dynamic_update_slice_in_dim(
            jnp.zeros((3, model_width), jnp.float32), qkv_bias_grad, tp_rank * local_width, 1
        )
        up_spread = lax.dynamic_update_slice_in_dim(
            jnp.zeros((hidden_all,), jnp.float32), up_bias_grad, tp_rank * local_hidden, 0
        )
        small_grads[layer_idx] = jnp.concatenate(
            [
                gain_one_grad,
                shift_one_grad,
                gain_two_grad,
                shift_two_grad,
                bias_grad,
                bias_grad,
                qkv_spread.reshape(-1),
                up_spread,
            ]
        )
        weight_grads[layer_idx] = (qkv_part, out_part, up_part, down_part)
    summed_small = lax.psum(jnp.stack(small_grads), ("fsdp", "tp"))
    qkv_total = jnp.stack([entry[0] for entry in weight_grads])
    out_total = jnp.stack([entry[1] for entry in weight_grads])
    up_total = jnp.stack([entry[2] for entry in weight_grads])
    down_total = jnp.stack([entry[3] for entry in weight_grads])
    qkv_m, qkv_v, qkv_w = adam_step(
        qkv_weight, qkv_first, qkv_second, qkv_total, rate_matrix, decay_rate
    )
    out_m, out_v, out_w = adam_step(
        out_weight, out_first, out_second, out_total, rate_output, decay_rate
    )
    up_m, up_v, up_w = adam_step(up_weight, up_first, up_second, up_total, rate_matrix, decay_rate)
    down_m, down_v, down_w = adam_step(
        down_weight, down_first, down_second, down_total, rate_matrix, decay_rate
    )
    small_m, small_v, small_w = adam_step(
        small_params, small_first, small_second, summed_small, rate_vector, 0.0
    )
    return (
        stream,
        gradient,
        qkv_m,
        qkv_v,
        qkv_w,
        out_m,
        out_v,
        out_w,
        up_m,
        up_v,
        up_w,
        down_m,
        down_v,
        down_w,
        small_m,
        small_v,
        small_w,
    )


def solution(mesh):
    in_specs = (
        P(("fsdp", "tp"), None),
        P(("fsdp", "tp"), None),
        P("fsdp", None),
        P(None, None, "fsdp", "tp"),
        P(None, None, "fsdp", "tp"),
        P(None, None, "fsdp", "tp"),
        P(None, ("tp", "fsdp"), None),
        P(None, ("tp", "fsdp"), None),
        P(None, ("tp", "fsdp"), None),
        P(None, "fsdp", "tp"),
        P(None, "fsdp", "tp"),
        P(None, "fsdp", "tp"),
        P(None, ("tp", "fsdp"), None),
        P(None, ("tp", "fsdp"), None),
        P(None, ("tp", "fsdp"), None),
        P(),
        P(),
        P(),
    )
    out_specs = (
        P(("fsdp", "tp"), None),
        P(("fsdp", "tp"), None),
        P(None, None, "fsdp", "tp"),
        P(None, None, "fsdp", "tp"),
        P(None, None, "fsdp", "tp"),
        P(None, ("tp", "fsdp"), None),
        P(None, ("tp", "fsdp"), None),
        P(None, ("tp", "fsdp"), None),
        P(None, "fsdp", "tp"),
        P(None, "fsdp", "tp"),
        P(None, "fsdp", "tp"),
        P(None, ("tp", "fsdp"), None),
        P(None, ("tp", "fsdp"), None),
        P(None, ("tp", "fsdp"), None),
        P(),
        P(),
        P(),
    )
    return jax.shard_map(local, mesh=mesh, in_specs=in_specs, out_specs=out_specs, check_vma=False)
```

profile of v0, /device:TPU:30, one launch (start us, length us, event | category | flops | bytes accessed | tf_op | source)
XLA Modules:
  0.0 1302.7 jit_solution(9884035956678403936)
XLA Ops:
  11.9 3.3 fusion.59
  25.9 24.0 %all-gather.12.cloned.1.call-done = bf16[1024,2048]{1,0:T(8,128)(2,1)} async-done(((bf16[256,2048]{1,0:T(8,128)(2,1)}), bf16[1024,2048]{1,0:T(8,128)(2,1)}) %all-gather.12.cloned.1.call-update) | async-done | bytes 4194320 | tf_op jit(solution)/shard_map/all_gather | solution.py:228
  49.8 100.7 %all-gather.18.cloned.1.call-done = bf16[1,3,2048,512]{2,3,1,0:T(8,128)(2,1)} async-done(((bf16[1,3,256,512]{2,3,1,0:T(8,128)(2,1)}), bf16[1,3,2048,512]{2,3,1,0:T(8,128)(2,1)}) %all-gather.18.cloned.1.call-update) | async-done | bytes 6291472 | tf_op jit(solution)/shard_map/all_gather | solution.py:222
  150.5 10.1 add_bitcast_fusion
  195.0 6.7 convolution_convert_fusion.2
  201.8 21.4 %all-gather.14.cloned.1.call-done = bf16[1024,2048]{1,0:T(8,128)(2,1)} async-done(((bf16[256,2048]{1,0:T(8,128)(2,1)}), bf16[1024,2048]{1,0:T(8,128)(2,1)}) %all-gather.14.cloned.1.call-update) | async-done | bytes 4194320 | tf_op jit(solution)/shard_map/all_gather | solution.py:229
  223.2 125.6 %all-gather.22.cloned.1.call-done = bf16[1,2048,2048]{2,1,0:T(8,128)(2,1)} async-done(((bf16[1,256,2048]{2,1,0:T(8,128)(2,1)}), bf16[1,2048,2048]{2,1,0:T(8,128)(2,1)}) %all-gather.22.cloned.1.call-update) | async-done | bytes 8388624 | tf_op jit(solution)/shard_map/all_gather | solution.py:224
  348.8 43.2 %multiply_convert_fusion = (bf16[1024,2048]{1,0:T(8,128)(2,1)S(1)}, f32[1024,2048]{1,0:T(8,128)}, f32[1024,2048]{1,0:T(8,128)}) fusion(f32[2048]{0:T(1024)S(1)} %bitcast.178, bf16[1024,2048]{1,0:T(8,128)(2,1)} %all-gather.14.cloned.1.call-done, bf16[1,2048,2048]{2,1,0:T(8,128)(2,1)} %all-gather.22.cloned.1.call-done), kind=kOutput, calls=%fused_computation.20 | convolution fusion | flops 8728346624 | bytes 33562624 | tf_op jit(solution)/shard_map/dot_general | solution.py:243
  394.0 11.4 convolution_convert_fusion
  405.5 13.7 %reduce-scatter.16.cloned.1.call-done = bf16[64,2048]{1,0:T(8,128)(2,1)} async-done(((bf16[512,2048]{1,0:T(8,128)(2,1)}), bf16[64,2048]{1,0:T(8,128)(2,1)}) %reduce-scatter.16.cloned.1.call-update) | async-done | bytes 262160 | tf_op jit(solution)/shard_map/reduce_scatter | solution.py:347
  422.3 148.8 %reduce-scatter.20.cloned.1.call-done = bf16[256,2048]{1,0:T(8,128)(2,1)} async-done(((bf16[2048,2048]{1,0:T(8,128)(2,1)}), bf16[256,2048]{1,0:T(8,128)(2,1)}) %reduce-scatter.20.cloned.1.call-update) | async-done | bytes 1048592 | tf_op jit(solution)/shard_map/reduce_scatter | solution.py:350
  571.1 8.0 multiply_subtract_fusion
  579.2 42.6 %all-gather.20.cloned.1.call-done = bf16[1,512,2048]{2,1,0:T(8,128)(2,1)} async-done(((bf16[1,64,2048]{2,1,0:T(8,128)(2,1)}), bf16[1,512,2048]{2,1,0:T(8,128)(2,1)}) %all-gather.20.cloned.1.call-update) | async-done | bytes 2097168 | tf_op jit(solution)/shard_map/all_gather | solution.py:223
  621.8 5.4 fusion.91
  635.2 4.5 multiply_reduce_fusion
  659.8 11.4 bitcast_convert_fusion
  671.2 76.6 %all-gather.24.cloned.1.call-done = bf16[1,2048,2048]{2,1,0:T(8,128)(2,1)} async-done(((bf16[1,256,2048]{2,1,0:T(8,128)(2,1)}), bf16[1,2048,2048]{2,1,0:T(8,128)(2,1)}) %all-gather.24.cloned.1.call-update) | async-done | bytes 8388624 | tf_op jit(solution)/shard_map/all_gather | solution.py:225
  747.8 17.8 %convert_reduce_fusion = (f32[2048]{0:T(1024)S(1)}, bf16[1024,2048]{1,0:T(8,128)(2,1)S(1)}) fusion(f32[1024,2048]{1,0:T(8,128)} %get-tuple-element.136, f32[2048]{0:T(1024)S(1)} %bitcast.179, f32[1024,2048]{1,0:T(8,128)} %get-tuple-element.95, bf16[1024,2048]{1,0:T(8,128)(2,1)} %all-gather.16.cloned.1.call-done, ...), kind=kOutput, calls=%fused_computation.18 | convolution fusion | flops 8613001216 | bytes 33570816 | tf_op jit(solution)/shard_map/sd,fd->sf/dot_general | solution.py:306
  767.6 12.6 fusion.33
  780.5 4.4 fusion.83
  785.0 12.6 add_convert_fusion
  797.7 10.9 convert_bitcast_fusion
  811.0 31.1 %reduce-scatter.12.cloned.1.call-done = bf16[256,2048]{1,0:T(8,128)(2,1)} async-done(((bf16[1024,2048]{1,0:T(8,128)(2,1)}), bf16[256,2048]{1,0:T(8,128)(2,1)}) %reduce-scatter.12.cloned.1.call-update) | async-done | bytes 1048592 | tf_op jit(solution)/shard_map/reduce_scatter | solution.py:339
  842.1 3.4 fusion.75
  845.6 43.6 %reduce-scatter.8.cloned.1.call-done = bf16[256,2048]{1,0:T(8,128)(2,1)} async-done(((bf16[1024,2048]{1,0:T(8,128)(2,1)}), bf16[256,2048]{1,0:T(8,128)(2,1)}) %reduce-scatter.8.cloned.1.call-update) | async-done | bytes 1048592 | tf_op jit(solution)/shard_map/reduce_scatter | solution.py:245
  889.2 5.0 convert_reduce_fusion.6
  895.3 14.1 %convolution_convert_fusion.1 = bf16[2048,2048]{1,0:T(8,128)(2,1)} fusion(bf16[1024,2048]{1,0:T(8,128)(2,1)} %all-gather.14.cloned.1.call-done, bf16[1024,2048]{1,0:T(8,128)(2,1)} %copy-done.43), kind=kOutput, calls=%fused_computation.36 | convolution fusion | flops 8594128896 | bytes 16777216 | tf_op jit(solution)/shard_map/sd,sf->df/dot_general | solution.py:310
  914.5 95.9 %reduce-scatter.14.cloned.1.call-done = bf16[3,256,512]{1,2,0:T(8,128)(2,1)} async-done(((bf16[3,2048,512]{1,2,0:T(8,128)(2,1)}), bf16[3,256,512]{1,2,0:T(8,128)(2,1)}) %reduce-scatter.14.cloned.1.call-update) | async-done | bytes 786448 | tf_op jit(solution)/shard_map/reduce_scatter | solution.py:344
  1010.3 4.6 multiply_subtract_fusion.2
  1024.2 113.6 %all-reduce.2.cloned.1.call-done = f32[1,26624]{1,0:T(1,128)} async-done(((f32[1,26624]{1,0:T(1,128)}), f32[1,26624]{1,0:T(1,128)}) %all-reduce.2.cloned.1.call-update) | async-done | bytes 106512 | tf_op jit(solution)/shard_map/psum | solution.py:383
  1140.1 149.2 %reduce-scatter.18.cloned.1.call-done = bf16[256,2048]{1,0:T(8,128)(2,1)} async-done(((bf16[2048,2048]{1,0:T(8,128)(2,1)}), bf16[256,2048]{1,0:T(8,128)(2,1)}) %reduce-scatter.18.cloned.1.call-update) | async-done | bytes 1048592 | tf_op jit(solution)/shard_map/reduce_scatter | solution.py:353
  1289.3 6.4 multiply_subtract_fusion.1
  (208 shorter events, 104.8 us)
Async XLA Ops:
  7.2 8.1 copy-start.23
  7.2 42.6 %all-gather.12.cloned.1.call-start = ((), (), s32[]{:S(2)}) async-start(), calls=%async_computation.7 | async-start | bytes 5242880 | tf_op jit(solution)/shard_map/all_gather | solution.py:228
  8.7 6.4 copy-start.28
  15.2 135.3 %all-gather.18.cloned.1.call-start = ((), (), s32[]{:S(2)}) async-start(), calls=%async_computation.18 | async-start | bytes 7077888 | tf_op jit(solution)/shard_map/all_gather | solution.py:222
  16.7 178.3 %all-gather.16.cloned.1.call-start = ((), (), s32[]{:S(2)}) async-start(), calls=%async_computation.10 | async-start | bytes 5242880 | tf_op jit(solution)/shard_map/all_gather | solution.py:301
  17.5 205.7 %all-gather.14.cloned.1.call-start = ((), (), s32[]{:S(2)}) async-start(), calls=%async_computation.8 | async-start | bytes 5242880 | tf_op jit(solution)/shard_map/all_gather | solution.py:229
  18.1 330.7 %all-gather.22.cloned.1.call-start = ((), (), s32[]{:S(2)}) async-start(), calls=%async_computation.20 | async-start | bytes 9437184 | tf_op jit(solution)/shard_map/all_gather | solution.py:224
  20.8 398.3 %reduce-scatter.16.cloned.1.call-start = ((), (), s32[]{:S(2)}) async-start(), calls=%async_computation.14 | async-start | bytes 2359296 | tf_op jit(solution)/shard_map/reduce_scatter | solution.py:347
  24.7 156.4 %copy-start.11 = (f32[1024,32]{1,0:T(8,128)}, f32[1024,32]{1,0:T(8,128)S(1)}, u32[]{:S(2)}) copy-start(f32[1024,32]{1,0:T(8,128)S(1)} %get-tuple-element.131) | copy-start | bytes 393220
  201.7 369.4 %reduce-scatter.20.cloned.1.call-start = ((), (), s32[]{:S(2)}) async-start(), calls=%async_computation.16 | async-start | bytes 9437184 | tf_op jit(solution)/shard_map/reduce_scatter | solution.py:350
  348.8 45.2 %copy-start.40 = (bf16[1024,2048]{1,0:T(8,128)(2,1)S(1)}, bf16[1024,2048]{1,0:T(8,128)(2,1)}, u32[]{:S(2)}) copy-start(bf16[1024,2048]{1,0:T(8,128)(2,1)} %all-gather.16.cloned.1.call-done) | copy-start | bytes 12582916
  405.4 216.4 %all-gather.20.cloned.1.call-start = ((), (), s32[]{:S(2)}) async-start(), calls=%async_computation.19 | async-start | bytes 2359296 | tf_op jit(solution)/shard_map/all_gather | solution.py:223
  422.3 325.5 %all-gather.24.cloned.1.call-start = ((), (), s32[]{:S(2)}) async-start(), calls=%async_computation.21 | async-start | bytes 9437184 | tf_op jit(solution)/shard_map/all_gather | solution.py:225
  579.2 231.8 %reduce-scatter.10.cloned.1.call-start = ((), (), s32[]{:S(2)}) async-start(), calls=%async_computation.11 | async-start | bytes 5242880 | tf_op jit(solution)/shard_map/reduce_scatter | solution.py:336
  659.7 137.9 %copy-start.16 = (bf16[1,1024,512]{2,1,0:T(8,128)(2,1)}, bf16[1,1024,512]{2,1,0:T(8,128)(2,1)S(1)}, u32[]{:S(2)}) copy-start(bf16[1,1024,512]{2,1,0:T(8,128)(2,1)S(1)} %copy.118) | copy-start | bytes 3145732
  671.2 170.9 %reduce-scatter.12.cloned.1.call-start = ((), (), s32[]{:S(2)}) async-start(), calls=%async_computation.12 | async-start | bytes 5242880 | tf_op jit(solution)/shard_map/reduce_scatter | solution.py:339
  780.2 109.0 %reduce-scatter.8.cloned.1.call-start = ((), (), s32[]{:S(2)}) async-start(), calls=%async_computation.9 | async-start | bytes 5242880 | tf_op jit(solution)/shard_map/reduce_scatter | solution.py:245
  797.6 212.7 %reduce-scatter.14.cloned.1.call-start = ((), (), s32[]{:S(2)}) async-start(), calls=%async_computation.13 | async-start | bytes 7077888 | tf_op jit(solution)/shard_map/reduce_scatter | solution.py:344
  808.6 33.5 %copy-start.6 = (bf16[256,2048]{1,0:T(8,128)(2,1)S(1)}, bf16[256,2048]{1,0:T(8,128)(2,1)}, u32[]{:S(2)}) copy-start(bf16[256,2048]{1,0:T(8,128)(2,1)} %param.18) | copy-start | bytes 3145732
  808.6 33.5 %copy-start.27 = (f32[1,2048]{1,0:T(1,128)S(1)}, f32[1,2048]{1,0:T(1,128)}, u32[]{:S(2)}) copy-start(f32[1,2048]{1,0:T(1,128)} %copy-done.26) | copy-start | bytes 24580
  808.6 33.5 %copy-start.29 = (f32[1,2048]{1,0:T(1,128)S(1)}, f32[1,2048]{1,0:T(1,128)}, u32[]{:S(2)}) copy-start(f32[1,2048]{1,0:T(1,128)} %copy-done.28) | copy-start | bytes 24580
  808.6 33.5 %copy-start.37 = (f32[256]{0:T(256)S(1)}, f32[256]{0:T(256)}, u32[]{:S(2)}) copy-start(f32[256]{0:T(256)} %copy-done.36) | copy-start | bytes 3076
  808.6 33.5 %copy-start.39 = (f32[256]{0:T(256)S(1)}, f32[256]{0:T(256)}, u32[]{:S(2)}) copy-start(f32[256]{0:T(256)} %copy-done.38) | copy-start | bytes 3076
  808.6 80.6 %copy-start.34 = (f32[1,2048]{1,0:T(1,128)S(1)}, f32[1,2048]{1,0:T(1,128)}, u32[]{:S(2)}) copy-start(f32[1,2048]{1,0:T(1,128)} %get-tuple-element.123) | copy-start | bytes 24580
  808.6 80.6 %copy-start.35 = (f32[1,2048]{1,0:T(1,128)S(1)}, f32[1,2048]{1,0:T(1,128)}, u32[]{:S(2)}) copy-start(f32[1,2048]{1,0:T(1,128)} %get-tuple-element.128) | copy-start | bytes 24580
  808.6 329.1 %all-reduce.2.cloned.1.call-start = ((), (), s32[]{:S(2)}) async-start(), calls=%async_computation.17 | async-start | bytes 212992 | tf_op jit(solution)/shard_map/psum | solution.py:383
  895.0 394.3 %reduce-scatter.18.cloned.1.call-start = ((), (), s32[]{:S(2)}) async-start(), calls=%async_computation.15 | async-start | bytes 9437184 | tf_op jit(solution)/shard_map/reduce_scatter | solution.py:353
  909.4 100.9 %copy-start.8 = (f32[1,3,256,512]{2,3,1,0:T(8,128)S(1)}, f32[1,3,256,512]{2,3,1,0:T(8,128)}, u32[]{:S(2)}) copy-start(f32[1,3,256,512]{2,3,1,0:T(8,128)} %copy-done.7) | copy-start | bytes 4718596
  1014.9 122.8 %copy-start.25 = (f32[1,26624]{1,0:T(1,128)S(1)}, f32[1,26624]{1,0:T(1,128)}, u32[]{:S(2)}) copy-start(f32[1,26624]{1,0:T(1,128)} %param.33) | copy-start | bytes 319492
  1014.9 122.8 %copy-start.31 = (f32[1,26624]{1,0:T(1,128)S(1)}, f32[1,26624]{1,0:T(1,128)}, u32[]{:S(2)}) copy-start(f32[1,26624]{1,0:T(1,128)} %param.35) | copy-start | bytes 319492
  1014.9 122.8 %copy-start.32 = (f32[1,26624]{1,0:T(1,128)S(1)}, f32[1,26624]{1,0:T(1,128)}, u32[]{:S(2)}) copy-start(f32[1,26624]{1,0:T(1,128)} %param.34) | copy-start | bytes 319492
  1018.0 271.3 %copy-start.9 = (f32[1,256,2048]{2,1,0:T(8,128)S(1)}, f32[1,256,2048]{2,1,0:T(8,128)}, u32[]{:S(2)}) copy-start(f32[1,256,2048]{2,1,0:T(8,128)} %param.27) | copy-start | bytes 6291460
  (28 other events, 94.3 us)
Sparse Core Ops, SparseCore 0:
  15.3 34.4 all-gather.11
  52.4 98.0 all-gather.17
  152.1 34.5 all-gather.15
  188.7 34.4 all-gather.13
  225.7 122.9 all-gather.21
  352.7 66.3 reduce-scatter.15
  422.8 148.2 reduce-scatter.19
  574.0 47.7 all-gather.19
  624.8 122.9 all-gather.23
  750.3 44.6 reduce-scatter.9
  797.5 44.5 reduce-scatter.11
  844.6 44.5 reduce-scatter.7
  892.8 117.4 reduce-scatter.13
  1016.3 121.4 all-reduce.1
  1141.3 147.9 reduce-scatter.17
where the time goes:
time: 1310 us; the launch traced here: 1300 us
  waiting for transfers between devices  988 us (75%)
  matrix products  181 us (14%)
  other arithmetic  65 us (5%)
  local copies, waits for them, and re-layouts  52.3 us (4%)
  between operations  15.2 us (1%)
    reduce_scatter x1, waiting for transfers between devices, local(): lax.psum_scatter(up_grad.astype(jnp.bfloat16), 'fsdp', scatter_dimension=...  149 us
    reduce_scatter x1, waiting for transfers between devices, local(): lax.psum_scatter(down_grad.astype(jnp.bfloat16), 'fsdp', scatter_dimensio...  149 us
    all_gather x1, waiting for transfers between devices, local(): up_full = lax.all_gather(up_shard, 'fsdp', axis=0, tiled=True)  126 us
    psum x1, waiting for transfers between devices, local(): summed_small = lax.psum(jnp.stack(small_grads), ('fsdp', 'tp'))  114 us
    all_gather x1, waiting for transfers between devices, local(): qkv_full = lax.all_gather(qkv_shard, 'fsdp', axis=1, tiled=True)  101 us
    reduce_scatter x1, waiting for transfers between devices, local(): lax.psum_scatter(qkv_grad.astype(jnp.bfloat16), 'fsdp', scatter_dimension...  95.9 us
    all_gather x1, waiting for transfers between devices, local(): down_full = lax.all_gather(down_shard, 'fsdp', axis=0, tiled=True)  76.6 us
    reduce_scatter x1, waiting for transfers between devices, local(): lax.psum_scatter(branch_term(mixed_rows, active, out_full, down_full).ast...  43.6 us
  transfers between devices with their start and end apart: 15, of which 13 were waited for; matrix products, arithmetic and copies ran while one was open for 21% of the time, Pallas kernels for 0%

commit v1 on v0

v1 whole, which is shorter than its diff:
```python
import jax
import jax.numpy as jnp
from jax import lax
from jax.sharding import PartitionSpec as P

HD = 256
ROT = 64
STEP = 10

norm_eps = 1e-05
beta_one = 0.9
beta_two = 0.95
adam_eps = 1e-08
decay_rate = 0.01
rate_vector = 0.2
masked_score = -1e30
f32 = jnp.float32
bf16 = jnp.bfloat16


def rotary_tables(seg_ids):
    length = seg_ids.shape[0]
    indices = jnp.arange(length, dtype=jnp.int32)
    earlier = jnp.sum((seg_ids[None, :] < seg_ids[:, None]).astype(jnp.int32), axis=1)
    position = (indices - earlier).astype(f32)
    inverse_freq = 10000.0 ** (-jnp.arange(0, ROT, 2).astype(f32) / ROT)
    angle = position[:, None] * inverse_freq[None, :]
    return (jnp.cos(angle), jnp.sin(angle))


def rotate(values, cosine, sine):
    half_dims = cosine.shape[-1]
    first_half = values[..., :half_dims]
    second_half = values[..., half_dims : 2 * half_dims]
    remainder = values[..., 2 * half_dims :]
    return jnp.concatenate(
        [
            first_half * cosine - second_half * sine,
            second_half * cosine + first_half * sine,
            remainder,
        ],
        axis=-1,
    )


def adam_step(weight, first, second, grad, rate, decay):
    first_new = beta_one * first + (1.0 - beta_one) * grad
    second_new = beta_two * second + (1.0 - beta_two) * grad * grad
    first_hat = first_new / (1.0 - beta_one**STEP)
    second_hat = second_new / (1.0 - beta_two**STEP)
    weight_new = weight - rate * (first_hat / (jnp.sqrt(second_hat) + adam_eps) + decay * weight)
    return (first_new, second_new, weight_new)


def dot(a, b, dims, out=f32):
    return lax.dot_general(a, b, (dims, ((), ())), preferred_element_type=out)


def make_local(fsdp, tp):
    lo_n = 2
    mid_n = 2
    hi_n = fsdp // (lo_n * mid_n)
    hi_bits = [1 << b for b in range(2, fsdp.bit_length() - 1)]
    top = hi_bits[-1]

    def swap_top(i):
        a, b = (i & 2) // 2, (i & top) // top
        return (i & ~(2 | top)) | (2 * b) | (top * a)

    def px(v, mask):
        return lax.ppermute(v, "fsdp", [(i, i ^ mask) for i in range(fsdp)])

    def pt(v, mask):
        return lax.ppermute(v, "tp", [(i, i ^ mask) for i in range(tp)])

    def local(
        layer_input,
        out_cotangent,
        segments,
        qkv_weight,
        qkv_first,
        qkv_second,
        out_weight,
        out_first,
        out_second,
        up_weight,
        up_first,
        up_second,
        down_weight,
        down_first,
        down_second,
        small_params,
        small_first,
        small_second,
    ):
        f = lax.axis_index("fsdp")
        t = lax.axis_index("tp")
        mid = (f // 2) % 2
        hi = f // 4
        lo = f % 2
        core = t % 2
        half_t = t // 2
        rows, d = layer_input.shape
        length = segments.shape[1]
        width = qkv_weight.shape[3]
        hidden = up_weight.shape[2]
        hidden_all = small_params.shape[1] - 9 * d
        sub = hidden // fsdp
        feat = d // fsdp
        mine = hidden // 2
        orow = width // fsdp
        vector = small_params[0]

        up16 = up_weight[0].astype(bf16).reshape(feat, hi_n, 2, lo_n * sub)
        down16 = down_weight[0].astype(bf16)
        qkv16 = qkv_weight[0].astype(bf16).reshape(3, feat, 2, HD)
        out16 = out_weight[0].astype(bf16)

        def pick(v, index, axis):
            return lax.dynamic_index_in_dim(v, index, axis, keepdims=False)

        def gather_tokens(own):
            mid_block = px(own, 2)
            y_own = pt(own, 2)
            y_mid = pt(mid_block, 2)
            blocks = {(0, 0): own, (2, 0): mid_block, (0, 2): y_own, (2, 2): y_mid}
            for key in list(blocks):
                blocks[(key[0], 1 ^ key[1])] = pt(blocks[key], 1)
            whole = jnp.zeros((2, tp, rows, d), own.dtype)
            for (a, b), block in blocks.items():
                whole = lax.dynamic_update_slice(
                    whole, block[None, None], ((mid ^ (a // 2)), t ^ b, 0, 0)
                )
            return whole.reshape(2 * tp * rows, d)

        def scatter_tokens(part):
            part = part.reshape(2, tp // 2, 2, rows, d)
            keep = pick(part, core, 2)
            give = pick(part, 1 - core, 2)
            part = (keep.astype(f32) + pt(give, 1).astype(f32)).astype(bf16)
            keep = pick(part, half_t, 1)
            give = pick(part, 1 - half_t, 1)
            part = (keep.astype(f32) + pt(give, 2).astype(f32)).astype(bf16)
            keep = pick(part, mid, 0)
            give = pick(part, 1 - mid, 0)
            return keep.astype(f32) + px(give, 2).astype(f32)

        def gather_group(block):
            blocks = {0: block}
            for mask in hi_bits + [1]:
                for key in list(blocks):
                    blocks[key | mask] = px(blocks[key], mask)
            return blocks

        def scatter_group(part):
            keep = pick(part, lo, 1)
            give = pick(part, 1 - lo, 1)
            got = px(give, 1)
            index = hi
            total = keep.astype(f32) + got.astype(f32)
            for mask in reversed(hi_bits):
                total = total.astype(bf16)
                bit = mask // 4
                n = total.shape[0] // 2
                upper = (index & bit) // bit
                shaped = total.reshape((2, n) + total.shape[1:])
                keep = pick(shaped, upper, 0)
                give = pick(shaped, 1 - upper, 0)
                total = keep.astype(f32) + px(give, mask).astype(f32)
            return total[0]

        def halves(v, axis):
            return pick(v, mid, axis), pick(v, 1 - mid, axis)

        own, other = halves(up16, 2)
        from_mid = px(other, 2)
        up_whole = jnp.zeros((hi_n, 2, lo_n, feat, hi_n, lo_n * sub), bf16)
        for a, block in ((0, own), (2, from_mid)):
            for mask, piece in gather_group(block).items():
                g = f ^ a ^ mask
                up_whole = lax.dynamic_update_slice(
                    up_whole, piece[None, None, None], (g // 4, (g // 2) % 2, g % 2, 0, 0, 0)
                )
        up_full = up_whole.reshape(d, mine)
        x_all = gather_tokens(layer_input)
        own, other = halves(qkv16, 2)
        from_mid = px(other, 2)
        qkv_whole = jnp.zeros((3, hi_n, 2, lo_n, feat, HD), bf16)
        for a, block in ((0, own), (2, from_mid)):
            for mask, piece in gather_group(block).items():
                g = f ^ a ^ mask
                qkv_whole = lax.dynamic_update_slice(
                    qkv_whole,
                    piece[:, None, None, None],
                    (0, g // 4, (g // 2) % 2, g % 2, 0, 0),
                )
        qkv_full = qkv_whole.reshape(3, d, HD)
        e_all = gather_tokens(out_cotangent)
        down_whole = jnp.zeros((hi_n, lo_n, sub, d), bf16)
        for mask, piece in gather_group(down16).items():
            g = f ^ mask
            down_whole = lax.dynamic_update_slice(down_whole, piece[None, None], (g // 4, g % 2, 0, 0))
        down_full = down_whole.reshape(mine, d)

        swap_perm = [(i, swap_top(i)) for i in range(fsdp)]
        out_block = lax.ppermute(out16, "fsdp", swap_perm)
        out_whole = jnp.zeros((hi_n, lo_n, orow, d), bf16)
        n_top = top // 4
        hi_rest = hi % n_top if n_top > 1 else 0
        for mask, piece in gather_group(out_block).items():
            g = f ^ mask
            g_top = g // top
            g_rest = (g // 4) % n_top if n_top > 1 else 0
            place = g_rest * 2 + g_top
            out_whole = lax.dynamic_update_slice(out_whole, piece[None, None], (place, g % 2, 0, 0))
        out_full = out_whole.reshape(HD, d)

        seg_other = px(segments.astype(f32), 2).astype(jnp.int32)
        seg = jnp.where(mid == 0, jnp.concatenate([segments, seg_other]), jnp.concatenate([seg_other, segments]))
        cosine, sine = jax.vmap(rotary_tables)(seg)
        idx = jnp.arange(length, dtype=jnp.int32)
        allowed = (idx[None, :] <= idx[:, None])[None] & (seg[:, :, None] == seg[:, None, :])

        stream = layer_input.astype(f32)
        x32 = x_all.astype(f32)
        mean_row = jnp.mean(x32, axis=-1, keepdims=True)
        centred = x32 - mean_row
        inverse = lax.rsqrt(jnp.mean(centred * centred, axis=-1, keepdims=True) + norm_eps)
        normal = centred * inverse
        gain_one, shift_one = vector[0:d], vector[d : 2 * d]
        gain_two, shift_two = vector[2 * d : 3 * d], vector[3 * d : 4 * d]
        bias_out, bias_down = vector[4 * d : 5 * d], vector[5 * d : 6 * d]
        qkv_bias = lax.dynamic_slice_in_dim(
            vector[6 * d : 9 * d].reshape(3, d), t * width + mid * HD, HD, 1
        )
        up_bias = pick(
            pick(vector[9 * d :].reshape(tp, hi_n, 2, lo_n * sub), t, 0), mid, 1
        ).reshape(mine)
        rows_one = (normal * gain_one + shift_one).astype(bf16)
        rows_two = (normal * gain_two + shift_two).astype(bf16)

        pre_act = dot(rows_two, up_full, ((1,), (0,))) + up_bias
        cdf = 0.5 * (1.0 + lax.erf(pre_act * 0.7071067811865476))
        active = (pre_act * cdf).astype(bf16)
        slope = (cdf + pre_act * (jnp.exp(-0.5 * pre_act * pre_act) * 0.3989422804014327)).astype(bf16)
        down_grad = dot(active, e_all, ((0,), (0,)), bf16)
        down_sum = scatter_group(down_grad.reshape(hi_n, lo_n, sub, d))
        active_grad = dot(e_all, down_full, ((1,), (1,)))
        pre_grad = (active_grad * slope.astype(f32)).astype(bf16)
        up_grad = dot(rows_two, pre_grad, ((0,), (0,)), bf16)
        up_bias_grad = jnp.sum(pre_grad, axis=0, dtype=f32)

        def scatter_cols(grad, tail):
            pass

        up_sum = scatter_group(
            up_grad.reshape(hi_n, 2, lo_n, feat, mine).transpose(0, 2, 1, 3, 4)
        ).astype(bf16)
        keep, give = halves(up_sum, 0)
        got = px(give, 2)
        up_total = jnp.where(
            mid == 0,
            jnp.stack([keep.reshape(feat, hi_n, lo_n * sub), got.reshape(feat, hi_n, lo_n * sub)], 2),
            jnp.stack([got.reshape(feat, hi_n, lo_n * sub), keep.reshape(feat, hi_n, lo_n * sub)], 2),
        ).reshape(1, feat, hidden)

        proj = dot(rows_one, qkv_full, ((1,), (1,))) + qkv_bias[None]
        proj = proj.reshape(2, length, 3, HD)
        query = rotate(proj[:, :, 0], cosine, sine).astype(bf16)
        key = rotate(proj[:, :, 1], cosine, sine).astype(bf16)
        value = proj[:, :, 2].astype(bf16)
        scale = HD ** (-0.5)
        scores = jnp.einsum("bqd,bkd->bqk", query, key, preferred_element_type=f32) * scale
        scores = jnp.where(allowed, scores, masked_score)
        peak = jnp.max(scores, axis=-1, keepdims=True)
        total = jnp.log(jnp.sum(jnp.exp(scores - peak), axis=-1, keepdims=True)) + peak
        probs = jnp.exp(scores - total)
        weights = probs.astype(bf16)
        mixed = jnp.einsum("bqk,bkd->bqd", weights, value, preferred_element_type=f32)
        mixed = mixed.astype(bf16).reshape(2 * length, HD)
        out_grad = dot(mixed, e_all, ((0,), (0,)), bf16)
        out_sum = scatter_group(
            jnp.moveaxis(
                out_grad.reshape(hi_n // 2, 2, lo_n, orow, d), 1, 0
            ).reshape(hi_n, lo_n, orow, d)
        ).astype(bf16)
        out_total = lax.ppermute(out_sum, "fsdp", swap_perm)[None].astype(f32)
        mixed_grad = dot(e_all, out_full, ((1,), (1,)), bf16).reshape(2, length, HD)
        prob_grad = jnp.einsum("bqd,bkd->bqk", mixed_grad, value, preferred_element_type=f32)
        inner = jnp.sum(probs * prob_grad, axis=-1, keepdims=True)
        score_grad = (probs * (prob_grad - inner)).astype(bf16)
        query_grad = jnp.einsum("bqk,bkd->bqd", score_grad, key, preferred_element_type=f32) * scale
        key_grad = jnp.einsum("bqk,bqd->bkd", score_grad, query, preferred_element_type=f32) * scale
        value_grad = jnp.einsum("bqk,bqd->bkd", weights, mixed_grad, preferred_element_type=f32)
        proj_grad = jnp.stack(
            [rotate(query_grad, cosine, -sine), rotate(key_grad, cosine, -sine), value_grad], 0
        ).astype(bf16).reshape(3, 2 * length, HD)
        qkv_grad = dot(rows_one, proj_grad, ((0,), (1,)), bf16)
        qkv_bias_grad = jnp.sum(proj_grad, axis=1, dtype=f32)
        qkv_sum = scatter_group(
            qkv_grad.reshape(hi_n, 2, lo_n, feat, 3, HD).transpose(0, 2, 1, 4, 3, 5)
        ).astype(bf16)
        keep, give = halves(qkv_sum, 0)
        got = px(give, 2)
        qkv_total = jnp.where(
            mid == 0, jnp.concatenate([keep, got], -1), jnp.concatenate([got, keep], -1)
        )[None].astype(f32)

        branch = dot(mixed, out_full, ((1,), (0,))) + dot(active, down_full, ((1,), (0,)))
        layer_output = stream + scatter_tokens(branch.astype(bf16)) + bias_out + bias_down

        first_norm = lax.dot_general(
            proj_grad, qkv_full, (((0, 2), (0, 2)), ((), ())), preferred_element_type=f32
        )
        second_norm = dot(pre_grad, up_full, ((1,), (1,)))
        gain_one_grad = jnp.sum(first_norm * normal, axis=0)
        shift_one_grad = jnp.sum(first_norm, axis=0)
        gain_two_grad = jnp.sum(second_norm * normal, axis=0)
        shift_two_grad = jnp.sum(second_norm, axis=0)
        scaled = scatter_tokens((first_norm * gain_one + second_norm * gain_two).astype(bf16))
        own_mean = jnp.mean(stream, axis=-1, keepdims=True)
        own_centred = stream - own_mean
        own_inverse = lax.rsqrt(jnp.mean(own_centred * own_centred, axis=-1, keepdims=True) + norm_eps)
        own_normal = own_centred * own_inverse
        gradient = out_cotangent.astype(f32)
        input_grad = gradient + own_inverse * (
            scaled
            - jnp.mean(scaled, axis=-1, keepdims=True)
            - own_normal * jnp.mean(scaled * own_normal, axis=-1, keepdims=True)
        )

        bias_grad = jnp.sum(gradient, axis=0)
        qkv_spread = lax.dynamic_update_slice(
            jnp.zeros((3, d), f32), qkv_bias_grad, (0, t * width + mid * HD)
        )
        up_spread = lax.dynamic_update_slice(
            jnp.zeros((tp, hi_n, 2, lo_n * sub), f32),
            up_bias_grad.reshape(1, hi_n, 1, lo_n * sub),
            (t, 0, mid, 0),
        )
        small_grad = jnp.concatenate(
            [
                gain_one_grad,
                shift_one_grad,
                gain_two_grad,
                shift_two_grad,
                bias_grad,
                bias_grad,
                qkv_spread.reshape(-1),
                up_spread.reshape(-1),
            ]
        )
        small_total = lax.psum(small_grad[None], ("fsdp", "tp"))
        rate_matrix = d ** (-0.5)
        rate_output = 4.0 * d ** (-0.5)
        down_total = down_sum[None]
        up_total = up_total.astype(f32)
        results = [layer_output, input_grad]
        for weight, first, second, grad, rate, decay in (
            (qkv_weight, qkv_first, qkv_second, qkv_total, rate_matrix, decay_rate),
            (out_weight, out_first, out_second, out_total, rate_output, decay_rate),
            (up_weight, up_first, up_second, up_total, rate_matrix, decay_rate),
            (down_weight, down_first, down_second, down_total, rate_matrix, decay_rate),
            (small_params, small_first, small_second, small_total, rate_vector, 0.0),
        ):
            results.extend(adam_step(weight, first, second, grad, rate, decay))
        return tuple(results)

    return local


def solution(mesh):
    tokens = P(("fsdp", "tp"), None)
    inner = P(None, ("tp", "fsdp"), None)
    qkv = P(None, None, "fsdp", "tp")
    up = P(None, "fsdp", "tp")
    weights = (qkv,) * 3 + (inner,) * 3 + (up,) * 3 + (inner,) * 3 + (P(),) * 3
    return jax.shard_map(
        make_local(mesh.shape["fsdp"], mesh.shape["tp"]),
        mesh=mesh,
        in_specs=(tokens, tokens, P("fsdp", None)) + weights,
        out_specs=(tokens, tokens) + weights,
        check_vma=False,
    )
```

time: 1310 us -> 1030 us (0.79)
  waiting for transfers between devices: 988 us -> 510 us
  local copies, waits for them, and re-layouts: 52.3 us -> 186 us
  starting transfers between devices: 1.08 us -> 57.4 us
  other arithmetic: 65 us -> 85.5 us
  matrix products: 181 us -> 161 us
    reduce_scatter x7 -> x0, waiting for transfers between devices: 482 us -> none  [the longest x1 149 us: local(): lax.psum_scatter(up_grad.astype(jnp.bfloat16), 'fsdp', scatter_dimension=...]
    ppermute x0 -> x53, waiting for transfers between devices: none -> 396 us  [the longest x35 333 us: px(): return lax.ppermute(v, 'fsdp', [(i, i ^ mask) for i in range(fsdp)])]
    all_gather x7 -> x0, waiting for transfers between devices: 391 us -> none  [the longest x1 126 us: local(): up_full = lax.all_gather(up_shard, 'fsdp', axis=0, tiled=True)]
    ppermute x0 -> x53, starting transfers between devices: none -> 57.3 us  [the longest x35 49.7 us: px(): return lax.ppermute(v, 'fsdp', [(i, i ^ mask) for i in range(fsdp)])]
    dynamic_update_slice x2 -> x41, local copies, waits for them, and re-layouts: 0.34 us -> 50.2 us  [the longest x16 17.6 us: gather_tokens(): lax.dynamic_update_slice(whole, block[None, None], (mid ^ a // 2, t ^ b,...]
    dynamic_slice x2 -> x17, local copies, waits for them, and re-layouts: 0.02 us -> 29.2 us  [the longest x16 28.6 us: pick(): return lax.dynamic_index_in_dim(v, index, axis, keepdims=False)]
    dot_general x0 -> x3, local copies, waits for them, and re-layouts: none -> 25.3 us  [dot(): return lax.dot_general(a, b, (dims, ((), ())), preferred_element_type=out)]
    convert_element_type x5 -> x17, other arithmetic: 9.6 us -> 34.8 us  [the longest x2 8.18 us: scatter_tokens(): part = (keep.astype(f32) + pt(give, 1).astype(f32)).astype(bf16)]
  transfers between devices with their start and end apart: 15 -> 54, of which waited for: 13 -> 22; matrix products, arithmetic and copies ran while one was open for 21% -> 34% of each run, Pallas kernels for 0% -> 0%
where the time goes in v1:
time: 1030 us; the launch traced here: 1020 us
  waiting for transfers between devices  510 us (50%)
  local copies, waits for them, and re-layouts  186 us (18%)
  matrix products  161 us (16%)
  other arithmetic  85.5 us (8%)
  starting transfers between devices  57.4 us (6%)
  between operations  16 us (2%)
    ppermute x35, waiting for transfers between devices, px(): return lax.ppermute(v, 'fsdp', [(i, i ^ mask) for i in range(fsdp)])  333 us
    dot_general x11, matrix products, dot(): return lax.dot_general(a, b, (dims, ((), ())), preferred_element_type=out)  125 us
    psum x1, waiting for transfers between devices, local(): small_total = lax.psum(small_grad[None], ('fsdp', 'tp'))  114 us
    ppermute x16, waiting for transfers between devices, pt(): return lax.ppermute(v, 'tp', [(i, i ^ mask) for i in range(tp)])  63 us
    ppermute x35, starting transfers between devices, px(): return lax.ppermute(v, 'fsdp', [(i, i ^ mask) for i in range(fsdp)])  49.7 us
    unnamed x161, local copies, waits for them, and re-layouts  34.6 us
    dynamic_slice x16, local copies, waits for them, and re-layouts, pick(): return lax.dynamic_index_in_dim(v, index, axis, keepdims=False)  28.6 us
    dot_general x3, local copies, waits for them, and re-layouts, dot(): return lax.dot_general(a, b, (dims, ((), ())), preferred_element_type=out)  25.3 us
  transfers between devices with their start and end apart: 54, of which 22 were waited for; matrix products, arithmetic and copies ran while one was open for 34% of the time, Pallas kernels for 0%

profile of v1, /device:TPU:30, one launch (start us, length us, event | category | flops | bytes accessed | tf_op | source)
XLA Modules:
  0.0 1016.3 jit_solution(16908562107191132542)
XLA Ops:
  57.9 26.8 %collective-permute-done.11 = bf16[3,256,256]{2,1,0:T(8,128)(2,1)S(1)} collective-permute-done((bf16[3,256,256]{2,1,0:T(8,128)(2,1)S(1)}, bf16[3,256,256]{2,1,0:T(8,128)(2,1)S(1)}, u32[]{:S(2)}, u32[]{:S(2)}) %collective-permute-start.11) | collective-permute-done | bytes 393248 | tf_op jit(solution)/shard_map/ppermute | solution.py:71
  91.1 24.9 %collective-permute-done.12 = bf16[3,256,256]{2,1,0:T(8,128)(2,1)S(1)} collective-permute-done((bf16[3,256,256]{2,1,0:T(8,128)(2,1)S(1)}, bf16[3,256,256]{2,1,0:T(8,128)(2,1)S(1)}, u32[]{:S(2)}, u32[]{:S(2)}) %collective-permute-start.12) | collective-permute-done | bytes 393248 | tf_op jit(solution)/shard_map/ppermute | solution.py:71
  123.2 9.4 collective-permute-done.22
  134.0 29.1 %collective-permute-done.2 = bf16[256,2048]{1,0:T(8,128)(2,1)S(1)} collective-permute-done((bf16[256,2048]{1,0:T(8,128)(2,1)S(1)}, bf16[256,2048]{1,0:T(8,128)(2,1)S(1)}, u32[]{:S(2)}, u32[]{:S(2)}) %collective-permute-start.2) | collective-permute-done | bytes 1048608 | tf_op jit(solution)/shard_map/ppermute | solution.py:74
  171.5 12.6 %collective-permute-done.14 = bf16[3,256,256]{2,1,0:T(8,128)(2,1)S(1)} collective-permute-done((bf16[3,256,256]{2,1,0:T(8,128)(2,1)S(1)}, bf16[3,256,256]{2,1,0:T(8,128)(2,1)S(1)}, u32[]{:S(2)}, u32[]{:S(2)}) %collective-permute-start.14) | collective-permute-done | bytes 393248 | tf_op jit(solution)/shard_map/ppermute | solution.py:71
  196.0 15.5 %collective-permute-done.34 = bf16[256,2048]{1,0:T(8,128)(2,1)} collective-permute-done((bf16[256,2048]{1,0:T(8,128)(2,1)S(1)}, bf16[256,2048]{1,0:T(8,128)(2,1)}, u32[]{:S(2)}, u32[]{:S(2)}) %collective-permute-start.34) | collective-permute-done | bytes 1048608 | tf_op jit(solution)/shard_map/ppermute | solution.py:74
  229.7 7.2 add_convert_fusion.4
  237.0 8.8 convolution_add_fusion
  297.8 15.0 %fusion.14 = (bf16[1024,2048]{1,0:T(8,128)(2,1)}, f32[2048,1024]{0,1:T(8,128)}) fusion(f32[1024]{0:T(1024)S(1)} %bitcast.376, bf16[2048,2048]{1,0:T(8,128)(2,1)S(1)} %bitcast.318, bf16[2048,1024]{1,0:T(8,128)(2,1)} %bitcast.337), kind=kOutput, calls=%fused_computation.41 | convolution fusion | flops 8602517504 | bytes 25169920 | tf_op jit(solution)/shard_map/dot_general | solution.py:56
  313.6 12.6 %fusion.109 = bf16[2,2,256,2048]{3,2,1,0:T(8,128)(2,1)S(1)} fusion(bf16[2,2,256,2048]{3,2,1,0:T(8,128)(2,1)} %bitcast.380, bf16[2048,2048,1,1]{1,0,3,2:T(8,128)(2,1)} %bitcast.326), kind=kOutput, calls=%fused_computation.271 | convolution fusion | flops 8589934592 | bytes 16777216 | tf_op jit(solution)/shard_map/dot_general | solution.py:56
  330.7 9.2 collective-permute-start.16
  340.1 10.1 collective-permute-done.16
  351.6 31.2 %collective-permute-done.17 = bf16[64,2048]{1,0:T(8,128)(2,1)S(1)} collective-permute-done((bf16[64,2048]{1,0:T(8,128)(2,1)S(1)}, bf16[64,2048]{1,0:T(8,128)(2,1)S(1)}, u32[]{:S(2)}, u32[]{:S(2)}) %collective-permute-start.17) | collective-permute-done | bytes 262176 | tf_op jit(solution)/shard_map/ppermute | solution.py:71
  407.6 39.5 %collective-permute-done.52 = bf16[1,256,2048]{2,1,0:T(8,128)(2,1)S(1)} collective-permute-done((bf16[1,256,2048]{2,1,0:T(8,128)(2,1)}, bf16[1,256,2048]{2,1,0:T(8,128)(2,1)S(1)}, u32[]{:S(2)}, u32[]{:S(2)}) %collective-permute-start.52) | collective-permute-done | bytes 1048608 | tf_op jit(solution)/shard_map/ppermute | solution.py:71
  457.9 40.8 %collective-permute-done.26 = bf16[256,2048]{1,0:T(8,128)(2,1)} collective-permute-done((bf16[256,2048]{1,0:T(8,128)(2,1)}, bf16[256,2048]{1,0:T(8,128)(2,1)}, u32[]{:S(2)}, u32[]{:S(2)}) %collective-permute-start.26) | collective-permute-done | bytes 1048608 | tf_op jit(solution)/shard_map/ppermute | solution.py:71
  509.3 14.8 %collective-permute-done.28 = bf16[256,2048]{1,0:T(8,128)(2,1)} collective-permute-done((bf16[256,2048]{1,0:T(8,128)(2,1)}, bf16[256,2048]{1,0:T(8,128)(2,1)}, u32[]{:S(2)}, u32[]{:S(2)}) %collective-permute-start.28) | collective-permute-done | bytes 1048608 | tf_op jit(solution)/shard_map/ppermute | solution.py:71
  526.4 16.5 %fusion.16 = f32[2048,2048]{1,0:T(8,128)} fusion(bf16[1024,2048]{1,0:T(8,128)(2,1)} %bitcast.62, f32[2048,1024]{0,1:T(8,128)} %get-tuple-element.87, f32[1024]{0:T(1024)S(1)} %bitcast.377), kind=kOutput, calls=%fused_computation.44 | convolution fusion | flops 8602517504 | bytes 29364224 | tf_op jit(solution)/shard_map/dot_general | solution.py:56
  543.0 14.3 %convert_reduce_fusion.1 = (f32[1024]{0:T(1024)S(1)}, bf16[2048,1024]{0,1:T(8,128)(2,1)}) fusion(f32[2048,1024]{0,1:T(8,128)S(1)} %bitcast.382, f32[1024]{0:T(1024)S(1)} %bitcast.378, bf16[2048,2048]{1,0:T(8,128)(2,1)S(1)} %bitcast.330, bf16[1024,2048]{1,0:T(8,128)(2,1)} %bitcast.62), kind=kOutput, calls=%fused_computation.31 | convolution fusion | flops 8621390848 | bytes 25174016 | tf_op jit(solution)/shard_map/dot_general | solution.py:56
  557.3 8.5 add_convert_fusion.2
  575.0 14.2 %fusion.107 = f32[2048,2048]{1,0:T(8,128)} fusion(bf16[2048,1024]{0,1:T(8,128)(2,1)} %get-tuple-element.93, bf16[2048,1024]{1,0:T(8,128)(2,1)S(1)} %bitcast.338), kind=kOutput, calls=%fused_computation.269 | convolution fusion | flops 8589934592 | bytes 25165824 | tf_op jit(solution)/shard_map/dot_general | solution.py:56
  589.3 21.1 %fusion.95 = (f32[2048]{0:T(1024)S(1)}, f32[2048]{0:T(1024)S(1)}, bf16[2048,2048]{1,0:T(8,128)(2,1)}, f32[2048]{0:T(1024)S(1)}, f32[2048]{0:T(1024)S(1)}, /*inde...) fusion(f32[2048,2048]{1,0:T(8,128)} %fusion.107, f32[2048]{0:T(1024)S(1)} %bitcast.375, f32[2048]{0:T(1024)S(1)} %bitcast.374, ...), kind=kOutput, calls=%fused_computation.264 | convolution fusion | flops 6525280256 | bytes 56705024 | tf_op jit(solution)/shard_map/dot_general | solution.py:312
  619.8 12.3 %copy.247 = bf16[2048,2048]{1,0:T(8,128)(2,1)} copy(bf16[2048,2048]{0,1:T(8,128)(2,1)} %bitcast.320) | data formatting | bytes 16777216 | tf_op jit(solution)/shard_map/dot_general | solution.py:56
  632.2 12.6 %fusion.21 = bf16[2,2,2,256,1024]{4,3,2,1,0:T(8,128)(2,1)S(1)} fusion(bf16[2,2,2,256,2048]{4,3,2,1,0:T(8,128)(2,1)} %bitcast.323, bf16[2048,1024]{0,1:T(8,128)(2,1)} %get-tuple-element.93), kind=kOutput, calls=%fused_computation.55 | convolution fusion | flops 8589934592 | bytes 16777216 | tf_op jit(solution)/shard_map/dot_general | solution.py:56
  648.8 12.3 %copy.245 = bf16[2048,2048]{1,0:T(8,128)(2,1)} copy(bf16[2048,2048]{0,1:T(8,128)(2,1)} %bitcast.319) | data formatting | bytes 16777216 | tf_op jit(solution)/shard_map/dot_general | solution.py:56
  661.1 10.1 fusion.25
  678.7 51.2 %collective-permute-done.42 = bf16[2,2,3,256,256]{3,4,2,1,0:T(8,128)(2,1)} collective-permute-done((bf16[2,2,3,256,256]{3,4,2,1,0:T(8,128)(2,1)}, bf16[2,2,3,256,256]{3,4,2,1,0:T(8,128)(2,1)}, u32[]{:S(2)}, u32[]{:S(2)}) %collective-permute-start.42) | collective-permute-done | bytes 1572896 | tf_op jit(solution)/shard_map/ppermute | solution.py:71
  759.7 31.8 %collective-permute-done.43 = bf16[1,2,3,256,256]{3,4,2,1,0:T(8,128)(2,1)} collective-permute-done((bf16[1,2,3,256,256]{3,4,2,1,0:T(8,128)(2,1)}, bf16[1,2,3,256,256]{3,4,2,1,0:T(8,128)(2,1)}, u32[]{:S(2)}, u32[]{:S(2)}) %collective-permute-start.43) | collective-permute-done | bytes 786464 | tf_op jit(solution)/shard_map/ppermute | solution.py:71
  796.1 17.9 %collective-permute-done.49 = bf16[1,2,256,1024]{3,2,1,0:T(8,128)(2,1)} collective-permute-done((bf16[1,2,256,1024]{3,2,1,0:T(8,128)(2,1)}, bf16[1,2,256,1024]{3,2,1,0:T(8,128)(2,1)}, u32[]{:S(2)}, u32[]{:S(2)}) %collective-permute-start.49) | collective-permute-done | bytes 1048608 | tf_op jit(solution)/shard_map/ppermute | solution.py:71
  822.1 14.3 %collective-permute-done.30 = bf16[2,256,2048]{2,1,0:T(8,128)(2,1)} collective-permute-done((bf16[2,256,2048]{2,1,0:T(8,128)(2,1)}, bf16[2,256,2048]{2,1,0:T(8,128)(2,1)}, u32[]{:S(2)}, u32[]{:S(2)}) %collective-permute-start.30) | collective-permute-done | bytes 2097184 | tf_op jit(solution)/shard_map/ppermute | solution.py:74
  861.9 16.6 %collective-permute-done.31 = bf16[256,2048]{1,0:T(8,128)(2,1)} collective-permute-done((bf16[256,2048]{1,0:T(8,128)(2,1)}, bf16[256,2048]{1,0:T(8,128)(2,1)}, u32[]{:S(2)}, u32[]{:S(2)}) %collective-permute-start.31) | collective-permute-done | bytes 1048608 | tf_op jit(solution)/shard_map/ppermute | solution.py:71
  885.2 7.6 multiply_subtract_fusion.1
  892.7 114.0 %all-reduce.2.cloned.1.call-done = f32[1,26624]{1,0:T(1,128)} async-done(((f32[1,26624]{1,0:T(1,128)}), f32[1,26624]{1,0:T(1,128)}) %all-reduce.2.cloned.1.call-update) | async-done | bytes 106512 | tf_op jit(solution)/shard_map/psum | solution.py:353
  (406 shorter events, 317.5 us)
Async XLA Ops:
  7.2 999.5 %all-reduce.2.cloned.1.call-start = ((), (), s32[]{:S(2)}) async-start(), calls=%async_computation | async-start | bytes 212992 | tf_op jit(solution)/shard_map/psum | solution.py:353
  10.8 40.4 %collective-permute-start.9 = (bf16[3,256,256]{2,1,0:T(8,128)(2,1)}, bf16[3,256,256]{2,1,0:T(8,128)(2,1)}, u32[]{:S(2)}, u32[]{:S(2)}) collective-permute-start(bf16[3,256,256]{2,1,0:T(8,128)(2,1)} %bitcast.14), channel_id=1, source_target_pairs={{0,4},{4,0},{8,12},{12,8},{16,20},{20,16},{24,28},{28,24},{1,5},{5... | collective-permute-start | bytes 1179656 | tf_op jit(solution)/shard_map/ppermute | solution.py:71
  11.4 38.0 %collective-permute-start.8 = (bf16[3,256,256]{2,1,0:T(8,128)(2,1)}, bf16[3,256,256]{2,1,0:T(8,128)(2,1)}, u32[]{:S(2)}, u32[]{:S(2)}) collective-permute-start(bf16[3,256,256]{2,1,0:T(8,128)(2,1)} %bitcast.14), channel_id=1, source_target_pairs={{0,16},{4,20},{8,24},{12,28},{16,0},{20,4},{24,8},{28,12},{1,17},{... | collective-permute-start | bytes 1179656 | tf_op jit(solution)/shard_map/ppermute | solution.py:71
  14.2 70.6 %collective-permute-start.20 = (bf16[256,2,512]{2,0,1:T(8,128)(2,1)}, bf16[256,2,512]{2,0,1:T(8,128)(2,1)}, u32[]{:S(2)}, u32[]{:S(2)}) collective-permute-start(bf16[256,2,512]{2,0,1:T(8,128)(2,1)} %bitcast.47), channel_id=1, source_target_pairs={{0,4},{4,0},{8,12},{12,8},{16,20},{20,16},{24,28},{28,24},{1,5},{5... | collective-permute-start | bytes 1572872 | tf_op jit(solution)/shard_map/ppermute | solution.py:71
  15.7 38.4 %collective-permute-start.19 = (bf16[256,2,512]{2,0,1:T(8,128)(2,1)}, bf16[256,2,512]{2,0,1:T(8,128)(2,1)}, u32[]{:S(2)}, u32[]{:S(2)}) collective-permute-start(bf16[256,2,512]{2,0,1:T(8,128)(2,1)} %bitcast.47), channel_id=1, source_target_pairs={{0,16},{4,20},{8,24},{12,28},{16,0},{20,4},{24,8},{28,12},{1,17},{... | collective-permute-start | bytes 1572872 | tf_op jit(solution)/shard_map/ppermute | solution.py:71
  46.3 75.8 %collective-permute-start.32 = (bf16[256,2048]{1,0:T(8,128)(2,1)S(1)}, bf16[256,2048]{1,0:T(8,128)(2,1)S(1)}, u32[]{:S(2)}, u32[]{:S(2)}) collective-permute-start(bf16[256,2048]{1,0:T(8,128)(2,1)S(1)} %copy-done.23), channel_id=1, source_target_pairs={{0,8},{4,12},{8,0},{12,4},{16,24},{20,28},{24,16},{28,20},{1,9},{5... | collective-permute-start | bytes 3145736 | tf_op jit(solution)/shard_map/ppermute | solution.py:71
  49.4 165.2 %collective-permute-start.35 = (bf16[256,2048]{1,0:T(8,128)(2,1)S(1)}, bf16[256,2048]{1,0:T(8,128)(2,1)S(1)}, u32[]{:S(2)}, u32[]{:S(2)}) collective-permute-start(bf16[256,2048]{1,0:T(8,128)(2,1)S(1)} %copy-done.23), channel_id=1, source_target_pairs={{0,1},{1,0},{2,3},{3,2},{4,5},{5,4},{6,7},{7,6},{8,9},{9,8},{10,11... | collective-permute-start | bytes 3145736 | tf_op jit(solution)/shard_map/ppermute | solution.py:74
  84.7 34.9 %collective-permute-start.1 = (bf16[256,2048]{1,0:T(8,128)(2,1)S(1)}, bf16[256,2048]{1,0:T(8,128)(2,1)S(1)}, u32[]{:S(2)}, u32[]{:S(2)}) collective-permute-start(bf16[256,2048]{1,0:T(8,128)(2,1)S(1)} %copy-done.3), channel_id=1, source_target_pairs={{0,8},{4,12},{8,0},{12,4},{16,24},{20,28},{24,16},{28,20},{1,9},{5... | collective-permute-start | bytes 3145736 | tf_op jit(solution)/shard_map/ppermute | solution.py:71
  116.1 49.6 %collective-permute-start.33 = (bf16[256,2048]{1,0:T(8,128)(2,1)S(1)}, bf16[256,2048]{1,0:T(8,128)(2,1)S(1)}, u32[]{:S(2)}, u32[]{:S(2)}) collective-permute-start(bf16[256,2048]{1,0:T(8,128)(2,1)S(1)} %copy-done.23), channel_id=1, source_target_pairs={{0,2},{1,3},{2,0},{3,1},{4,6},{5,7},{6,4},{7,5},{8,10},{9,11},{10,... | collective-permute-start | bytes 3145736 | tf_op jit(solution)/shard_map/ppermute | solution.py:74
  117.4 45.7 %collective-permute-start.2 = (bf16[256,2048]{1,0:T(8,128)(2,1)S(1)}, bf16[256,2048]{1,0:T(8,128)(2,1)S(1)}, u32[]{:S(2)}, u32[]{:S(2)}) collective-permute-start(bf16[256,2048]{1,0:T(8,128)(2,1)S(1)} %copy-done.3), channel_id=1, source_target_pairs={{0,2},{1,3},{2,0},{3,1},{4,6},{5,7},{6,4},{7,5},{8,10},{9,11},{10,... | collective-permute-start | bytes 3145736 | tf_op jit(solution)/shard_map/ppermute | solution.py:74
  122.1 68.5 %collective-permute-start.4 = (bf16[256,2048]{1,0:T(8,128)(2,1)S(1)}, bf16[256,2048]{1,0:T(8,128)(2,1)S(1)}, u32[]{:S(2)}, u32[]{:S(2)}) collective-permute-start(bf16[256,2048]{1,0:T(8,128)(2,1)S(1)} %copy-done.3), channel_id=1, source_target_pairs={{0,1},{1,0},{2,3},{3,2},{4,5},{5,4},{6,7},{7,6},{8,9},{9,8},{10,11... | collective-permute-start | bytes 3145736 | tf_op jit(solution)/shard_map/ppermute | solution.py:74
  132.5 34.7 %collective-permute-start.21 = (bf16[256,2,512]{2,0,1:T(8,128)(2,1)}, bf16[256,2,512]{2,0,1:T(8,128)(2,1)S(1)}, u32[]{:S(2)}, u32[]{:S(2)}) collective-permute-start(bf16[256,2,512]{2,0,1:T(8,128)(2,1)} %collective-permute-done.19), channel_id=1, source_target_pairs={{0,4},{4,0},{8,12},{12,8},{16,20},{20,16},{24,28},{28,24},{1,5},{5... | collective-permute-start | bytes 1572872 | tf_op jit(solution)/shard_map/ppermute | solution.py:71
  163.1 121.2 %collective-permute-start.24 = (bf16[256,2,512]{2,0,1:T(8,128)(2,1)}, bf16[256,2,512]{2,0,1:T(8,128)(2,1)}, u32[]{:S(2)}, u32[]{:S(2)}) collective-permute-start(bf16[256,2,512]{2,0,1:T(8,128)(2,1)} %collective-permute-done.22), channel_id=1, source_target_pairs={{0,4},{4,0},{8,12},{12,8},{16,20},{20,16},{24,28},{28,24},{1,5},{5... | collective-permute-start | bytes 1572872 | tf_op jit(solution)/shard_map/ppermute | solution.py:71
  214.6 72.1 %collective-permute-start.25 = (bf16[256,2,512]{2,0,1:T(8,128)(2,1)}, bf16[256,2,512]{2,0,1:T(8,128)(2,1)}, u32[]{:S(2)}, u32[]{:S(2)}) collective-permute-start(bf16[256,2,512]{2,0,1:T(8,128)(2,1)} %collective-permute-done.23), channel_id=1, source_target_pairs={{0,4},{4,0},{8,12},{12,8},{16,20},{20,16},{24,28},{28,24},{1,5},{5... | collective-permute-start | bytes 1572872 | tf_op jit(solution)/shard_map/ppermute | solution.py:71
  217.7 54.3 %collective-permute-start.38 = (bf16[256,2048]{1,0:T(8,128)(2,1)}, bf16[256,2048]{1,0:T(8,128)(2,1)}, u32[]{:S(2)}, u32[]{:S(2)}) collective-permute-start(bf16[256,2048]{1,0:T(8,128)(2,1)} %collective-permute-done.34), channel_id=1, source_target_pairs={{0,1},{1,0},{2,3},{3,2},{4,5},{5,4},{6,7},{7,6},{8,9},{9,8},{10,11... | collective-permute-start | bytes 3145736 | tf_op jit(solution)/shard_map/ppermute | solution.py:74
  328.7 67.9 %collective-permute-start.51 = (bf16[2,256,2048]{2,1,0:T(8,128)(2,1)S(1)}, bf16[2,256,2048]{2,1,0:T(8,128)(2,1)S(1)}, u32[]{:S(2)}, u32[]{:S(2)}) collective-permute-start(bf16[2,256,2048]{2,1,0:T(8,128)(2,1)S(1)} %dynamic-slice_bitcast_fusion), channel_id=1, source_target_pairs={{0,4},{4,0},{8,12},{12,8},{16,20},{20,16},{24,28},{28,24},{1,5},{5... | collective-permute-start | bytes 6291464 | tf_op jit(solution)/shard_map/ppermute | solution.py:71
  330.1 52.8 %collective-permute-start.17 = (bf16[64,2048]{1,0:T(8,128)(2,1)S(1)}, bf16[64,2048]{1,0:T(8,128)(2,1)S(1)}, u32[]{:S(2)}, u32[]{:S(2)}) collective-permute-start(bf16[64,2048]{1,0:T(8,128)(2,1)S(1)} %collective-permute-done.15), channel_id=1, source_target_pairs={{0,4},{4,0},{8,12},{12,8},{16,20},{20,16},{24,28},{28,24},{1,5},{5... | collective-permute-start | bytes 786440 | tf_op jit(solution)/shard_map/ppermute | solution.py:71
  350.2 36.8 %collective-permute-start.18 = (bf16[64,2048]{1,0:T(8,128)(2,1)S(1)}, bf16[64,2048]{1,0:T(8,128)(2,1)S(1)}, u32[]{:S(2)}, u32[]{:S(2)}) collective-permute-start(bf16[64,2048]{1,0:T(8,128)(2,1)S(1)} %collective-permute-done.16), channel_id=1, source_target_pairs={{0,4},{4,0},{8,12},{12,8},{16,20},{20,16},{24,28},{28,24},{1,5},{5... | collective-permute-start | bytes 786440 | tf_op jit(solution)/shard_map/ppermute | solution.py:71
  398.6 48.6 %collective-permute-start.52 = (bf16[1,256,2048]{2,1,0:T(8,128)(2,1)}, bf16[1,256,2048]{2,1,0:T(8,128)(2,1)S(1)}, u32[]{:S(2)}, u32[]{:S(2)}) collective-permute-start(bf16[1,256,2048]{2,1,0:T(8,128)(2,1)} %constant_dynamic-slice_fusion), channel_id=1, source_target_pairs={{0,16},{4,20},{8,24},{12,28},{16,0},{20,4},{24,8},{28,12},{1,17},{... | collective-permute-start | bytes 3145736 | tf_op jit(solution)/shard_map/ppermute | solution.py:71
  453.2 45.5 %collective-permute-start.26 = (bf16[256,2048]{1,0:T(8,128)(2,1)}, bf16[256,2048]{1,0:T(8,128)(2,1)}, u32[]{:S(2)}, u32[]{:S(2)}) collective-permute-start(bf16[256,2048]{1,0:T(8,128)(2,1)} %get-tuple-element.59), channel_id=1, source_target_pairs={{0,16},{4,20},{8,24},{12,28},{16,0},{20,4},{24,8},{28,12},{1,17},{... | collective-permute-start | bytes 3145736 | tf_op jit(solution)/shard_map/ppermute | solution.py:71
  454.5 52.3 %collective-permute-start.27 = (bf16[256,2048]{1,0:T(8,128)(2,1)}, bf16[256,2048]{1,0:T(8,128)(2,1)}, u32[]{:S(2)}, u32[]{:S(2)}) collective-permute-start(bf16[256,2048]{1,0:T(8,128)(2,1)} %get-tuple-element.59), channel_id=1, source_target_pairs={{0,4},{4,0},{8,12},{12,8},{16,20},{20,16},{24,28},{28,24},{1,5},{5... | collective-permute-start | bytes 3145736 | tf_op jit(solution)/shard_map/ppermute | solution.py:71
  575.0 171.1 %collective-permute-start.29 = (bf16[2,2,256,2048]{3,2,0,1:T(8,128)(2,1)}, bf16[2,2,256,2048]{3,2,0,1:T(8,128)(2,1)}, u32[]{:S(2)}, u32[]{:S(2)}) collective-permute-start(bf16[2,2,256,2048]{3,2,0,1:T(8,128)(2,1)} %bitcast.305), channel_id=1, source_target_pairs={{0,1},{1,0},{2,3},{3,2},{4,5},{5,4},{6,7},{7,6},{8,9},{9,8},{10,11... | collective-permute-start | bytes 12582920 | tf_op jit(solution)/shard_map/ppermute | solution.py:74
  619.4 120.0 %collective-permute-start.39 = (bf16[2,2,256,2048]{3,2,0,1:T(8,128)(2,1)}, bf16[2,2,256,2048]{3,2,0,1:T(8,128)(2,1)}, u32[]{:S(2)}, u32[]{:S(2)}) collective-permute-start(bf16[2,2,256,2048]{3,2,0,1:T(8,128)(2,1)} %bitcast.304), channel_id=1, source_target_pairs={{0,1},{1,0},{2,3},{3,2},{4,5},{5,4},{6,7},{7,6},{8,9},{9,8},{10,11... | collective-permute-start | bytes 12582920 | tf_op jit(solution)/shard_map/ppermute | solution.py:74
  648.3 84.9 %collective-permute-start.48 = (bf16[2,2,256,1024]{3,2,1,0:T(8,128)(2,1)}, bf16[2,2,256,1024]{3,2,1,0:T(8,128)(2,1)}, u32[]{:S(2)}, u32[]{:S(2)}) collective-permute-start(bf16[2,2,256,1024]{3,2,1,0:T(8,128)(2,1)} %dynamic-slice_bitcast_fusion.1), channel_id=1, source_target_pairs={{0,4},{4,0},{8,12},{12,8},{16,20},{20,16},{24,28},{28,24},{1,5},{5... | collective-permute-start | bytes 6291464 | tf_op jit(solution)/shard_map/ppermute | solution.py:71
  674.2 55.7 %collective-permute-start.42 = (bf16[2,2,3,256,256]{3,4,2,1,0:T(8,128)(2,1)}, bf16[2,2,3,256,256]{3,4,2,1,0:T(8,128)(2,1)}, u32[]{:S(2)}, u32[]{:S(2)}) collective-permute-start(bf16[2,2,3,256,256]{3,4,2,1,0:T(8,128)(2,1)} %dynamic-slice_bitcast_fusion.4), channel_id=1, source_target_pairs={{0,4},{4,0},{8,12},{12,8},{16,20},{20,16},{24,28},{28,24},{1,5},{5... | collective-permute-start | bytes 4718600 | tf_op jit(solution)/shard_map/ppermute | solution.py:71
  732.8 58.7 %collective-permute-start.43 = (bf16[1,2,3,256,256]{3,4,2,1,0:T(8,128)(2,1)}, bf16[1,2,3,256,256]{3,4,2,1,0:T(8,128)(2,1)}, u32[]{:S(2)}, u32[]{:S(2)}) collective-permute-start(bf16[1,2,3,256,256]{3,4,2,1,0:T(8,128)(2,1)} %constant_dynamic-slice_fusion.6), channel_id=1, source_target_pairs={{0,16},{4,20},{8,24},{12,28},{16,0},{20,4},{24,8},{28,12},{1,17},{... | collective-permute-start | bytes 2359304 | tf_op jit(solution)/shard_map/ppermute | solution.py:71
  737.0 77.0 %collective-permute-start.49 = (bf16[1,2,256,1024]{3,2,1,0:T(8,128)(2,1)}, bf16[1,2,256,1024]{3,2,1,0:T(8,128)(2,1)}, u32[]{:S(2)}, u32[]{:S(2)}) collective-permute-start(bf16[1,2,256,1024]{3,2,1,0:T(8,128)(2,1)} %constant_dynamic-slice_fusion.2), channel_id=1, source_target_pairs={{0,16},{4,20},{8,24},{12,28},{16,0},{20,4},{24,8},{28,12},{1,17},{... | collective-permute-start | bytes 3145736 | tf_op jit(solution)/shard_map/ppermute | solution.py:71
  745.0 71.7 %collective-permute-start.40 = (bf16[2,256,2048]{2,1,0:T(8,128)(2,1)}, bf16[2,256,2048]{2,1,0:T(8,128)(2,1)}, u32[]{:S(2)}, u32[]{:S(2)}) collective-permute-start(bf16[2,256,2048]{2,1,0:T(8,128)(2,1)} %dynamic-slice_bitcast_fusion.2), channel_id=1, source_target_pairs={{0,2},{1,3},{2,0},{3,1},{4,6},{5,7},{6,4},{7,5},{8,10},{9,11},{10,... | collective-permute-start | bytes 6291464 | tf_op jit(solution)/shard_map/ppermute | solution.py:74
  754.7 81.7 %collective-permute-start.30 = (bf16[2,256,2048]{2,1,0:T(8,128)(2,1)}, bf16[2,256,2048]{2,1,0:T(8,128)(2,1)}, u32[]{:S(2)}, u32[]{:S(2)}) collective-permute-start(bf16[2,256,2048]{2,1,0:T(8,128)(2,1)} %dynamic-slice_bitcast_fusion.3), channel_id=1, source_target_pairs={{0,2},{1,3},{2,0},{3,1},{4,6},{5,7},{6,4},{7,5},{8,10},{9,11},{10,... | collective-permute-start | bytes 6291464 | tf_op jit(solution)/shard_map/ppermute | solution.py:74
  796.0 45.6 %collective-permute-start.44 = (bf16[3,256,256]{2,1,0:T(8,128)(2,1)}, bf16[3,256,256]{2,1,0:T(8,128)(2,1)S(1)}, u32[]{:S(2)}, u32[]{:S(2)}) collective-permute-start(bf16[3,256,256]{2,1,0:T(8,128)(2,1)} %bitcast.360), channel_id=1, source_target_pairs={{0,8},{4,12},{8,0},{12,4},{16,24},{20,28},{24,16},{28,20},{1,9},{5... | collective-permute-start | bytes 1179656 | tf_op jit(solution)/shard_map/ppermute | solution.py:71
  820.3 39.7 %collective-permute-start.41 = (bf16[256,2048]{1,0:T(8,128)(2,1)}, bf16[256,2048]{1,0:T(8,128)(2,1)}, u32[]{:S(2)}, u32[]{:S(2)}) collective-permute-start(bf16[256,2048]{1,0:T(8,128)(2,1)} %dynamic-slice_bitcast_fusion.5), channel_id=1, source_target_pairs={{0,8},{4,12},{8,0},{12,4},{16,24},{20,28},{24,16},{28,20},{1,9},{5... | collective-permute-start | bytes 3145736 | tf_op jit(solution)/shard_map/ppermute | solution.py:71
  841.1 37.4 %collective-permute-start.31 = (bf16[256,2048]{1,0:T(8,128)(2,1)}, bf16[256,2048]{1,0:T(8,128)(2,1)}, u32[]{:S(2)}, u32[]{:S(2)}) collective-permute-start(bf16[256,2048]{1,0:T(8,128)(2,1)} %dynamic-slice_bitcast_fusion.6), channel_id=1, source_target_pairs={{0,8},{4,12},{8,0},{12,4},{16,24},{20,28},{24,16},{28,20},{1,9},{5... | collective-permute-start | bytes 3145736 | tf_op jit(solution)/shard_map/ppermute | solution.py:71
  (95 other events, 1755.8 us)
Sparse Core Ops, SparseCore 0:
  885.2 121.4 all-reduce.1

commit v2 on v1

--- a/solution.py
+++ b/solution.py
@@ -1,6 +1,10 @@
+import functools
+
 import jax
 import jax.numpy as jnp
 from jax import lax
+from jax.experimental import pallas as pl
+from jax.experimental.pallas import tpu as pltpu
 from jax.sharding import PartitionSpec as P
 
 HD = 256
@@ -54,6 +58,251 @@
 
 def dot(a, b, dims, out=f32):
     return lax.dot_general(a, b, (dims, ((), ())), preferred_element_type=out)
+
+
+MESH = pl.DeviceIdType.MESH
+
+
+def bit_of(i, mask):
+    return (i // mask) % 2
+
+
+def flip(i, mask):
+    return i + mask - 2 * mask * bit_of(i, mask)
+
+
+class Links:
+    def __init__(self, send_sem, recv_sem):
+        self.send_sem, self.recv_sem, self.count, self.started = send_sem, recv_sem, 0, []
+
+    def copy(self, src, dst, device):
+        k = self.count
+        self.count += 1
+        c = pltpu.make_async_remote_copy(
+            src_ref=src,
+            dst_ref=dst,
+            send_sem=self.send_sem.at[k],
+            recv_sem=self.recv_sem.at[k],
+            device_id=device,
+            device_id_type=MESH,
+        )
+        self.started.append(c)
+        return c
+
+
+class Group:
+    def __init__(self, links, buf, slot, f, t, masks, root):
+        self.links, self.buf, self.slot, self.f, self.t, self.masks = links, buf, slot, f, t, masks
+        self.root, self.copies = root, {}
+
+    def _source(self, key):
+        g = self.root
+        for mask in self.masks:
+            if key & mask:
+                g = flip(g, mask)
+        return g
+
+    def have(self, key):
+        after = max([i + 1 for i, m in enumerate(self.masks) if key & m], default=0)
+        for mask in self.masks[after:]:
+            ref = self.buf.at[self.slot(self._source(key))]
+            c = self.links.copy(ref, ref, (flip(self.f, mask), self.t))
+            c.start()
+            self.copies[key | mask] = c
+
+    def arrive(self, key):
+        self.copies[key].wait_recv()
+        self.have(key)
+
+
+def gather_kernel(fsdp, masks, top, x, e, up, qkv, down, out, xa, ea, upa, qkva, downa, outa, send_sem, recv_sem, local_sem):
+    f = lax.axis_index("fsdp")
+    t = lax.axis_index("tp")
+    mid = bit_of(f, 2)
+    swapped = f + (top - 2) * (mid - bit_of(f, top))
+    barrier = pltpu.get_barrier_semaphore()
+    peers = [(flip(f, m), t) for m in masks + [2]] + [(f, flip(t, 1)), (f, flip(t, 2))]
+    for peer in peers:
+        pl.semaphore_signal(barrier, inc=1, device_id=peer, device_id_type=MESH)
+
+    @pl.when(swapped != f)
+    def _():
+        pl.semaphore_signal(barrier, inc=1, device_id=(swapped, t), device_id_type=MESH)
+
+    pl.semaphore_wait(barrier, len(peers) + (mid + bit_of(f, top)) % 2)
+    links = Links(send_sem, recv_sem)
+    locals_ = []
+
+    def local_copy(src, dst):
+        c = pltpu.make_async_copy(src, dst, local_sem.at[len(locals_)])
+        locals_.append(c)
+        c.start()
+        return c
+
+    mid_peer, y_peer, core_peer = (flip(f, 2), t), (f, flip(t, 2)), (f, flip(t, 1))
+    n_top = top // 4
+
+    def out_slot(g):
+        return (((g // 4) % n_top) * 2 + g // top) * 2 + g % 2
+
+    def down_slot(g):
+        return (g // 4) * 2 + g % 2
+
+    def same(g):
+        return g
+
+    qkv_own = Group(links, qkva, same, f, t, masks, f)
+    qkv_mid = Group(links, qkva, same, f, t, masks, flip(f, 2))
+    up_own = Group(links, upa, same, f, t, masks, f)
+    up_mid = Group(links, upa, same, f, t, masks, flip(f, 2))
+    down_own = Group(links, downa, down_slot, f, t, masks, f)
+    out_own = Group(links, outa, out_slot, f, t, masks, f)
+
+    def spread(group, source):
+        for mask in group.masks:
+            c = links.copy(source, group.buf.at[group.slot(f)], (flip(f, mask), t))
+            c.start()
+            group.copies[mask] = c
+
+    first_qkv = links.copy(qkv.at[1 - mid], qkva.at[f], mid_peer)
+    first_qkv.start()
+    spread(qkv_own, qkv.at[mid])
+
+    def tokens(source, buf):
+        parts = {}
+        for name, peer in (("m", mid_peer), ("y", y_peer), ("c", core_peer)):
+            c = links.copy(source, buf.at[mid, t], peer)
+            c.start()
+            parts[name] = c
+        return parts
+
+    def tokens_mid(buf, parts):
+        parts["m"].wait_recv()
+        ref = buf.at[1 - mid, t]
+        for name, peer in (("my", y_peer), ("mc", core_peer)):
+            parts[name] = links.copy(ref, ref, peer)
+            parts[name].start()
+
+    def tokens_y(buf, parts):
+        parts["y"].wait_recv()
+        ref = buf.at[mid, flip(t, 2)]
+        parts["yc"] = links.copy(ref, ref, core_peer)
+        parts["yc"].start()
+
+    def tokens_last(buf, parts):
+        parts["my"].wait_recv()
+        ref = buf.at[1 - mid, flip(t, 2)]
+        parts["myc"] = links.copy(ref, ref, core_peer)
+        parts["myc"].start()
+
+    def tokens_done(parts):
+        for name in ("c", "mc", "yc", "myc"):
+            parts[name].wait_recv()
+
+    x_parts = tokens(x, xa)
+    swap_copy = links.copy(out, outa.at[out_slot(swapped)], (swapped, t))
+    own_out = pltpu.make_async_copy(out, outa.at[out_slot(f)], local_sem.at[5])
+
+    @pl.when(swapped != f)
+    def _():
+        swap_copy.start()
+
+    @pl.when(swapped == f)
+    def _():
+        own_out.start()
+
+    first_up = links.copy(up.at[1 - mid], upa.at[f], mid_peer)
+    first_up.start()
+    own = [
+        local_copy(qkv.at[mid], qkva.at[f]),
+        local_copy(x, xa.at[mid, t]),
+        local_copy(up.at[mid], upa.at[f]),
+        local_copy(e, ea.at[mid, t]),
+        local_copy(down, downa.at[down_slot(f)]),
+    ]
+    first_qkv.wait_recv()
+    qkv_mid.have(0)
+    spread(up_own, up.at[mid])
+    e_parts = tokens(e, ea)
+    tokens_mid(xa, x_parts)
+    tokens_y(xa, x_parts)
+
+    @pl.when(swapped != f)
+    def _():
+        swap_copy.wait_recv()
+
+    @pl.when(swapped == f)
+    def _():
+        own_out.wait()
+
+    out_own.have(0)
+    for group in (qkv_own,):
+        for key in all_keys(masks)[1:]:
+            group.arrive(key)
+    first_up.wait_recv()
+    up_mid.have(0)
+    for key in all_keys(masks)[1:]:
+        qkv_mid.arrive(key)
+    tokens_last(xa, x_parts)
+    for key in all_keys(masks)[1:]:
+        out_own.arrive(key)
+    spread(down_own, down)
+    tokens_mid(ea, e_parts)
+    tokens_y(ea, e_parts)
+    tokens_done(x_parts)
+    for key in all_keys(masks)[1:]:
+        up_own.arrive(key)
+    for key in all_keys(masks)[1:]:
+        up_mid.arrive(key)
+    tokens_last(ea, e_parts)
+    tokens_done(e_parts)
+    for key in all_keys(masks)[1:]:
+        down_own.arrive(key)
+    for c in own:
+        c.wait()
+    for c in links.started:
+        if c is swap_copy:
+
+            @pl.when(swapped != f)
+            def _():
+                swap_copy.wait_send()
+
+        else:
+            c.wait_send()
+
+
+def all_keys(masks):
+    keys = [0]
+    for mask in masks:
+        keys = keys + [k | mask for k in keys]
+    return keys
+
+
+def gather_all(fsdp, masks, top, x, e, up, qkv, down, out, tp):
+    rows, d = x.shape
+    n_keys = 1 << len(masks)
+    copies = 2 * 7 + 2 * (1 + 2 * (n_keys - 1)) + n_keys - 1 + n_keys
+    shape = jax.ShapeDtypeStruct
+    return pl.pallas_call(
+        functools.partial(gather_kernel, fsdp, masks, top),
+        out_shape=(
+            shape((2, tp, rows, d), bf16),
+            shape((2, tp, rows, d), bf16),
+            shape((fsdp,) + up.shape[1:], bf16),
+            shape((fsdp,) + qkv.shape[1:], bf16),
+            shape((fsdp // 2,) + down.shape, bf16),
+            shape((fsdp // 2,) + out.shape, bf16),
+        ),
+        in_specs=[pl.BlockSpec(memory_space=pl.ANY)] * 6,
+        out_specs=(pl.BlockSpec(memory_space=pl.ANY),) * 6,
+        scratch_shapes=[
+            pltpu.SemaphoreType.DMA((copies,)),
+            pltpu.SemaphoreType.DMA((copies,)),
+            pltpu.SemaphoreType.DMA((6,)),
+        ],
+        compiler_params=pltpu.CompilerParams(collective_id=0, has_side_effects=True),
+        name="gather_all",
+    )(x, e, up, qkv, down, out)
 
 
 def make_local(fsdp, tp):
@@ -112,26 +361,14 @@
         vector = small_params[0]
 
         up16 = up_weight[0].astype(bf16).reshape(feat, hi_n, 2, lo_n * sub)
+        up16 = up16.transpose(2, 0, 1, 3).reshape(2, feat, mine)
+        qkv16 = qkv_weight[0].astype(bf16).reshape(3, feat, 2, HD)
+        qkv16 = qkv16.transpose(2, 1, 0, 3).reshape(2, feat, 3 * HD)
         down16 = down_weight[0].astype(bf16)
-        qkv16 = qkv_weight[0].astype(bf16).reshape(3, feat, 2, HD)
         out16 = out_weight[0].astype(bf16)
 
         def pick(v, index, axis):
             return lax.dynamic_index_in_dim(v, index, axis, keepdims=False)
-
-        def gather_tokens(own):
-            mid_block = px(own, 2)
-            y_own = pt(own, 2)
-            y_mid = pt(mid_block, 2)
-            blocks = {(0, 0): own, (2, 0): mid_block, (0, 2): y_own, (2, 2): y_mid}
-            for key in list(blocks):
-                blocks[(key[0], 1 ^ key[1])] = pt(blocks[key], 1)
-            whole = jnp.zeros((2, tp, rows, d), own.dtype)
-            for (a, b), block in blocks.items():
-                whole = lax.dynamic_update_slice(
-                    whole, block[None, None], ((mid ^ (a // 2)), t ^ b, 0, 0)
-                )
-            return whole.reshape(2 * tp * rows, d)
 
         def scatter_tokens(part):
             part = part.reshape(2, tp // 2, 2, rows, d)
@@ -144,13 +381,6 @@
             keep = pick(part, mid, 0)
             give = pick(part, 1 - mid, 0)
             return keep.astype(f32) + px(give, 2).astype(f32)
-
-        def gather_group(block):
-            blocks = {0: block}
-            for mask in hi_bits + [1]:
-                for key in list(blocks):
-                    blocks[key | mask] = px(blocks[key], mask)
-            return blocks
 
         def scatter_group(part):
             keep = pick(part, lo, 1)
@@ -172,48 +402,16 @@
         def halves(v, axis):
             return pick(v, mid, axis), pick(v, 1 - mid, axis)
 
-        own, other = halves(up16, 2)
-        from_mid = px(other, 2)
-        up_whole = jnp.zeros((hi_n, 2, lo_n, feat, hi_n, lo_n * sub), bf16)
-        for a, block in ((0, own), (2, from_mid)):
-            for mask, piece in gather_group(block).items():
-                g = f ^ a ^ mask
-                up_whole = lax.dynamic_update_slice(
-                    up_whole, piece[None, None, None], (g // 4, (g // 2) % 2, g % 2, 0, 0, 0)
-                )
-        up_full = up_whole.reshape(d, mine)
-        x_all = gather_tokens(layer_input)
-        own, other = halves(qkv16, 2)
-        from_mid = px(other, 2)
-        qkv_whole = jnp.zeros((3, hi_n, 2, lo_n, feat, HD), bf16)
-        for a, block in ((0, own), (2, from_mid)):
-            for mask, piece in gather_group(block).items():
-                g = f ^ a ^ mask
-                qkv_whole = lax.dynamic_update_slice(
-                    qkv_whole,
-                    piece[:, None, None, None],
-                    (0, g // 4, (g // 2) % 2, g % 2, 0, 0),
-                )
-        qkv_full = qkv_whole.reshape(3, d, HD)
-        e_all = gather_tokens(out_cotangent)
-        down_whole = jnp.zeros((hi_n, lo_n, sub, d), bf16)
-        for mask, piece in gather_group(down16).items():
-            g = f ^ mask
-            down_whole = lax.dynamic_update_slice(down_whole, piece[None, None], (g // 4, g % 2, 0, 0))
-        down_full = down_whole.reshape(mine, d)
-
+        x_all, e_all, up_full, qkv_full, down_full, out_full = gather_all(
+            fsdp, hi_bits + [1], top, layer_input, out_cotangent, up16, qkv16, down16, out16, tp
+        )
+        x_all = x_all.reshape(2 * tp * rows, d)
+        e_all = e_all.reshape(2 * tp * rows, d)
+        up_full = up_full.reshape(d, mine)
+        qkv_full = qkv_full.reshape(d, 3 * HD)
+        down_full = down_full.reshape(mine, d)
+        out_full = out_full.reshape(HD, d)
         swap_perm = [(i, swap_top(i)) for i in range(fsdp)]
-        out_block = lax.ppermute(out16, "fsdp", swap_perm)
-        out_whole = jnp.zeros((hi_n, lo_n, orow, d), bf16)
-        n_top = top // 4
-        hi_rest = hi % n_top if n_top > 1 else 0
-        for mask, piece in gather_group(out_block).items():
-            g = f ^ mask
-            g_top = g // top
-            g_rest = (g // 4) % n_top if n_top > 1 else 0
-            place = g_rest * 2 + g_top
-            out_whole = lax.dynamic_update_slice(out_whole, piece[None, None], (place, g % 2, 0, 0))
-        out_full = out_whole.reshape(HD, d)
 
         seg_other = px(segments.astype(f32), 2).astype(jnp.int32)
         seg = jnp.where(mid == 0, jnp.concatenate([segments, seg_other]), jnp.concatenate([seg_other, segments]))
@@ -250,9 +448,6 @@
         up_grad = dot(rows_two, pre_grad, ((0,), (0,)), bf16)
         up_bias_grad = jnp.sum(pre_grad, axis=0, dtype=f32)
 
-        def scatter_cols(grad, tail):
-            pass
-
         up_sum = scatter_group(
             up_grad.reshape(hi_n, 2, lo_n, feat, mine).transpose(0, 2, 1, 3, 4)
         ).astype(bf16)
@@ -264,7 +459,7 @@
             jnp.stack([got.reshape(feat, hi_n, lo_n * sub), keep.reshape(feat, hi_n, lo_n * sub)], 2),
         ).reshape(1, feat, hidden)
 
-        proj = dot(rows_one, qkv_full, ((1,), (1,))) + qkv_bias[None]
+        proj = dot(rows_one, qkv_full, ((1,), (0,))) + qkv_bias.reshape(3 * HD)
         proj = proj.reshape(2, length, 3, HD)
         query = rotate(proj[:, :, 0], cosine, sine).astype(bf16)
         key = rotate(proj[:, :, 1], cosine, sine).astype(bf16)
@@ -292,26 +487,24 @@
         query_grad = jnp.einsum("bqk,bkd->bqd", score_grad, key, preferred_element_type=f32) * scale
         key_grad = jnp.einsum("bqk,bqd->bkd", score_grad, query, preferred_element_type=f32) * scale
         value_grad = jnp.einsum("bqk,bqd->bkd", weights, mixed_grad, preferred_element_type=f32)
-        proj_grad = jnp.stack(
-            [rotate(query_grad, cosine, -sine), rotate(key_grad, cosine, -sine), value_grad], 0
-        ).astype(bf16).reshape(3, 2 * length, HD)
-        qkv_grad = dot(rows_one, proj_grad, ((0,), (1,)), bf16)
-        qkv_bias_grad = jnp.sum(proj_grad, axis=1, dtype=f32)
+        proj_grad = jnp.concatenate(
+            [rotate(query_grad, cosine, -sine), rotate(key_grad, cosine, -sine), value_grad], -1
+        ).astype(bf16).reshape(2 * length, 3 * HD)
+        qkv_grad = dot(rows_one, proj_grad, ((0,), (0,)), bf16)
+        qkv_bias_grad = jnp.sum(proj_grad, axis=0, dtype=f32).reshape(3, HD)
         qkv_sum = scatter_group(
-            qkv_grad.reshape(hi_n, 2, lo_n, feat, 3, HD).transpose(0, 2, 1, 4, 3, 5)
+            qkv_grad.reshape(hi_n, 2, lo_n, feat, 3 * HD).transpose(0, 2, 1, 3, 4)
         ).astype(bf16)
         keep, give = halves(qkv_sum, 0)
         got = px(give, 2)
         qkv_total = jnp.where(
-            mid == 0, jnp.concatenate([keep, got], -1), jnp.concatenate([got, keep], -1)
-        )[None].astype(f32)
+            mid == 0, jnp.stack([keep, got]), jnp.stack([got, keep])
+        ).reshape(2, feat, 3, HD).transpose(2, 1, 0, 3).reshape(1, 3, feat, width).astype(f32)
 
         branch = dot(mixed, out_full, ((1,), (0,))) + dot(active, down_full, ((1,), (0,)))
         layer_output = stream + scatter_tokens(branch.astype(bf16)) + bias_out + bias_down
 
-        first_norm = lax.dot_general(
-            proj_grad, qkv_full, (((0, 2), (0, 2)), ((), ())), preferred_element_type=f32
-        )
+        first_norm = dot(proj_grad, qkv_full, ((1,), (1,)))
         second_norm = dot(pre_grad, up_full, ((1,), (1,)))
         gain_one_grad = jnp.sum(first_norm * normal, axis=0)
         shift_one_grad = jnp.sum(first_norm, axis=0)
@@ -350,7 +543,11 @@
                 up_spread.reshape(-1),
             ]
         )
-        small_total = lax.psum(small_grad[None], ("fsdp", "tp"))
+        small_total = small_grad[None]
+        for mask in (1, 2):
+            small_total = small_total + pt(small_total, mask)
+        for mask in [1, 2] + hi_bits:
+            small_total = small_total + px(small_total, mask)
         rate_matrix = d ** (-0.5)
         rate_output = 4.0 * d ** (-0.5)
         down_total = down_sum[None]

time: 1030 us -> 762 us (0.74)
  waiting for transfers between devices: 510 us -> 140 us
  Pallas kernels: 0 us -> 189 us
  starting transfers between devices: 57.4 us -> 21.6 us
  local copies, waits for them, and re-layouts: 186 us -> 152 us
  between operations: 16 us -> 2 us
    ppermute x35 -> x16, waiting for transfers between devices: 333 us -> 121 us  [px(): return lax.ppermute(v, 'fsdp', [(i, i ^ mask) for i in range(fsdp)])]
    pallas_call x0 -> x1, Pallas kernels: none -> 189 us  [gather_all(): pl.pallas_call(functools.partial(gather_kernel, fsdp, masks, top), out_sh...]
    psum x1 -> x0, waiting for transfers between devices: 114 us -> none  [local(): small_total = lax.psum(small_grad[None], ('fsdp', 'tp'))]
    dynamic_update_slice x39 -> x0, local copies, waits for them, and re-layouts: 49.9 us -> none  [the longest x16 17.6 us: gather_tokens(): lax.dynamic_update_slice(whole, block[None, None], (mid ^ a // 2, t ^ b,...]
    ppermute x16 -> x6, waiting for transfers between devices: 63 us -> 18.7 us  [pt(): return lax.ppermute(v, 'tp', [(i, i ^ mask) for i in range(tp)])]
    ppermute x35 -> x16, starting transfers between devices: 49.7 us -> 17.3 us  [px(): return lax.ppermute(v, 'fsdp', [(i, i ^ mask) for i in range(fsdp)])]
    dot_general x11 -> x12, matrix products: 125 us -> 151 us  [dot(): return lax.dot_general(a, b, (dims, ((), ())), preferred_element_type=out)]
    dot_general x1 -> x0, matrix products: 21.1 us -> none  [local(): lax.dot_general(proj_grad, qkv_full, (((0, 2), (0, 2)), ((), ())), prefer...]
  transfers between devices with their start and end apart: 54 -> 23, of which waited for: 22 -> 9; matrix products, arithmetic and copies ran while one was open for 34% -> 51% of each run, Pallas kernels for 0% -> 25%
where the time goes in v2:
time: 762 us; the launch traced here: 750 us
  Pallas kernels  189 us (25%)
  matrix products  164 us (22%)
  local copies, waits for them, and re-layouts  152 us (20%)
  waiting for transfers between devices  140 us (18%)
  other arithmetic  81.7 us (11%)
  starting transfers between devices  21.6 us (3%)
    pallas_call x1, Pallas kernels, gather_all(): pl.pallas_call(functools.partial(gather_kernel, fsdp, masks, top), out_sh...  189 us
    dot_general x12, matrix products, dot(): return lax.dot_general(a, b, (dims, ((), ())), preferred_element_type=out)  151 us
    ppermute x16, waiting for transfers between devices, px(): return lax.ppermute(v, 'fsdp', [(i, i ^ mask) for i in range(fsdp)])  121 us
    unnamed x139, local copies, waits for them, and re-layouts  34.3 us
    dot_general x3, local copies, waits for them, and re-layouts, dot(): return lax.dot_general(a, b, (dims, ((), ())), preferred_element_type=out)  26.1 us
    dynamic_slice x9, local copies, waits for them, and re-layouts, pick(): return lax.dynamic_index_in_dim(v, index, axis, keepdims=False)  19.2 us
    ppermute x6, waiting for transfers between devices, pt(): return lax.ppermute(v, 'tp', [(i, i ^ mask) for i in range(tp)])  18.7 us
    sub x5, other arithmetic, adam_step(): weight - rate * (first_hat / (jnp.sqrt(second_hat) + adam_eps) + decay *...  18 us
  transfers between devices with their start and end apart: 23, of which 9 were waited for; matrix products, arithmetic and copies ran while one was open for 51% of the time, Pallas kernels for 25%

profile of v2, /device:TPU:30, one launch (start us, length us, event | category | flops | bytes accessed | tf_op | source)
XLA Modules:
  0.0 750.1 jit_solution(15089342190896247956)
XLA Ops:
  17.2 189.1 %gather_all.1 = (bf16[2,4,256,2048]{3,2,1,0:T(8,128)(2,1)}, bf16[2,4,256,2048]{3,2,1,0:T(8,128)(2,1)}, bf16[8,256,1024]{2,1,0:T(8,128)(2,1)}, bf16[8,256,768]{2,...) custom-call(bf16[256,2048]{1,0:T(8,128)(2,1)} %x.1, bf16[256,2048]{1,0:T(8,128)(2,1)} %e.1, ...), custom_call_target="tpu_custom_call" | custom-call | tf_op jit(solution)/shard_map/gather_all/pallas_call | solution.py:286
  206.3 4.7 convert_reduce_fusion
  214.5 9.8 %add_convert_fusion.5 = (bf16[2,4,256,2048]{3,2,1,0:T(8,128)(2,1)}, bf16[2,4,256,2048]{3,2,1,0:T(8,128)(2,1)S(1)}) fusion(bf16[2,4,256,2048]{3,2,1,0:T(8,128)(2,1)} %get-tuple-element.23, f32[2048]{0:T(1024)S(1)} %bitcast.253, f32[2048]{0:T(1024)S(1)} %bitcast.255, f32[2,4,256]{2,1,0:T(4,128)S(1)} %get-tuple-element.142, ...), kind=kLoop, calls=%fused_computation.9 | loop fusion | flops 37748736 | bytes 25214976 | tf_op jit(solution)/shard_map/convert_element_type | solution.py:437
  224.2 14.7 %fusion.11 = (bf16[1024,2048]{1,0:T(8,128)(2,1)}, f32[2048,1024]{0,1:T(8,128)}) fusion(f32[1024]{0:T(1024)S(1)} %bitcast.262, bf16[2048,2048]{1,0:T(8,128)(2,1)S(1)} %bitcast.223, bf16[2048,1024]{1,0:T(8,128)(2,1)} %bitcast.271), kind=kOutput, calls=%fused_computation.37 | convolution fusion | flops 8602517504 | bytes 25169920 | tf_op jit(solution)/shard_map/dot_general | solution.py:60
  238.9 12.5 %fusion.107 = bf16[2,2,256,2048]{3,2,1,0:T(8,128)(2,1)S(1)} fusion(bf16[2,2,256,2048]{3,2,1,0:T(8,128)(2,1)} %bitcast.277, bf16[2048,2048,1,1]{1,0,3,2:T(8,128)(2,1)} %bitcast.265), kind=kOutput, calls=%fused_computation.226 | convolution fusion | flops 8589934592 | bytes 16777216 | tf_op jit(solution)/shard_map/dot_general | solution.py:60
  260.3 11.9 %broadcast_add_fusion = f32[2048,768]{1,0:T(8,128)} fusion(f32[768]{0:T(1024)S(1)} %add.381, bf16[2048,2048]{1,0:T(8,128)(2,1)} %bitcast.219, bf16[2048,768]{1,0:T(8,128)(2,1)} %bitcast.275), kind=kOutput, calls=%fused_computation.63 | convolution fusion | flops 6444023808 | bytes 17828864 | tf_op jit(solution)/shard_map/dot_general | solution.py:60
  272.2 6.6 copy.157
  278.8 9.1 %reshape.497 = f32[2,1024,3,256]{1,0,3,2:T(2,128)} reshape(f32[2048,768]{0,1:T(8,128)} %copy.157) | data formatting | bytes 12582912 | tf_op jit(solution)/shard_map/reshape | solution.py:463
  291.8 15.3 %fusion.13 = f32[2048,2048]{1,0:T(8,128)} fusion(bf16[1024,2048]{1,0:T(8,128)(2,1)S(1)} %bitcast.273, f32[2048,1024]{0,1:T(8,128)} %get-tuple-element.148, f32[1024]{0:T(1024)S(1)} %bitcast.263), kind=kOutput, calls=%fused_computation.40 | convolution fusion | flops 8602517504 | bytes 29364224 | tf_op jit(solution)/shard_map/dot_general | solution.py:60
  307.1 15.4 %convert_reduce_fusion.1 = (f32[1024]{0:T(1024)S(1)}, bf16[2048,1024]{0,1:T(8,128)(2,1)}) fusion(f32[2048,1024]{0,1:T(8,128)} %get-tuple-element.148, f32[1024]{0:T(1024)S(1)} %bitcast.264, bf16[2048,2048]{1,0:T(8,128)(2,1)S(1)} %bitcast.269, bf16[1024,2048]{1,0:T(8,128)(2,1)S(1)} %bitcast.274), kind=kOutput, calls=%fused_computation.27 | convolution fusion | flops 8621390848 | bytes 25174016 | tf_op jit(solution)/shard_map/dot_general | solution.py:60
  368.2 6.0 fusion.106
  375.4 8.5 %add_convert_fusion.3 = bf16[2048,2048]{1,0:T(8,128)(2,1)S(1)} fusion(f32[2048,2048]{1,0:T(8,128)} %fusion.13, bf16[2048,256]{1,0:T(8,128)(2,1)S(1)} %bitcast.230, bf16[256,2048]{1,0:T(8,128)(2,1)} %bitcast.243), kind=kOutput, calls=%fused_computation.7 | convolution fusion | flops 2155872256 | bytes 27262976 | tf_op jit(solution)/shard_map/dot_general | solution.py:60
  388.0 4.8 copy.244
  400.8 5.8 concatenate.65
  406.7 11.6 %fusion.105 = f32[2048,2048]{1,0:T(8,128)} fusion(bf16[2048,768]{1,0:T(8,128)(2,1)S(1)} %concatenate.65, bf16[2048,768]{1,0:T(8,128)(2,1)} %bitcast.276), kind=kOutput, calls=%fused_computation.224 | convolution fusion | flops 6442450944 | bytes 23068672 | tf_op jit(solution)/shard_map/dot_general | solution.py:60
  418.4 27.2 %fusion.92 = (f32[2048]{0:T(1024)}, f32[2048]{0:T(1024)}, bf16[2048,2048]{1,0:T(8,128)(2,1)}, f32[2048]{0:T(1024)S(1)}, f32[2048]{0:T(1024)}, /*index=5*/bf16[2048,2048]{1,0:T(8,128)(2,1)}, bf16[2048,2048]{1,0:T(8,128)(2,1)}) fusion(f32[2048]{0:T(1024)S(1)} %bitcast.260, f32[2048]{0:T(1024)S(1)} %bitcast.259, ...), kind=kOutput, calls=%fused_computation.218 | convolution fusion | flops 8669618176 | bytes 58802176 | tf_op jit(solution)/shard_map/dot_general | solution.py:60
  445.6 6.8 constant_dynamic-slice_fusion.7
  454.7 12.3 %copy.216 = bf16[2048,2048]{1,0:T(8,128)(2,1)} copy(bf16[2048,2048]{0,1:T(8,128)(2,1)} %bitcast.221) | data formatting | bytes 16777216 | tf_op jit(solution)/shard_map/dot_general | solution.py:60
  467.0 13.9 %fusion.18 = bf16[2,2,2,256,1024]{4,3,2,1,0:T(8,128)(2,1)} fusion(bf16[2,2,2,256,2048]{4,3,2,1,0:T(8,128)(2,1)} %bitcast.224, bf16[2048,1024]{0,1:T(8,128)(2,1)} %get-tuple-element.150), kind=kOutput, calls=%fused_computation.51 | convolution fusion | flops 8589934592 | bytes 16777216 | tf_op jit(solution)/shard_map/dot_general | solution.py:60
  480.9 12.3 %copy.215 = bf16[2048,2048]{1,0:T(8,128)(2,1)} copy(bf16[2048,2048]{0,1:T(8,128)(2,1)} %bitcast.220) | data formatting | bytes 16777216 | tf_op jit(solution)/shard_map/dot_general | solution.py:60
  493.2 10.2 %fusion.22 = bf16[2,2,2,256,768]{4,3,2,1,0:T(8,128)(2,1)} fusion(bf16[2,2,2,256,2048]{4,3,2,1,0:T(8,128)(2,1)} %bitcast.225, bf16[2048,768]{1,0:T(8,128)(2,1)S(1)} %concatenate.65), kind=kOutput, calls=%fused_computation.59 | convolution fusion | flops 6442450944 | bytes 14680064 | tf_op jit(solution)/shard_map/dot_general | solution.py:60
  511.5 10.0 %collective-permute-done.11 = bf16[1,64,2048]{2,1,0:T(8,128)(2,1)} collective-permute-done((bf16[1,64,2048]{2,1,0:T(8,128)(2,1)S(1)}, bf16[1,64,2048]{2,1,0:T(8,128)(2,1)}, u32[]{:S(2)}, u32[]{:S(2)}) %collective-permute-start.11) | collective-permute-done | bytes 262176 | tf_op jit(solution)/shard_map/ppermute | solution.py:320
  528.2 15.7 %collective-permute-done.7 = bf16[2,2,256,768]{3,2,1,0:T(8,128)(2,1)S(1)} collective-permute-done((bf16[2,2,256,768]{3,2,1,0:T(8,128)(2,1)}, bf16[2,2,256,768]{3,2,1,0:T(8,128)(2,1)S(1)}, u32[]{:S(2)}, u32[]{:S(2)}) %collective-permute-start.7) | collective-permute-done | bytes 1572896 | tf_op jit(solution)/shard_map/ppermute | solution.py:320
  568.0 33.7 %collective-permute-done.8 = bf16[1,2,256,768]{3,2,1,0:T(8,128)(2,1)S(1)} collective-permute-done((bf16[1,2,256,768]{3,2,1,0:T(8,128)(2,1)}, bf16[1,2,256,768]{3,2,1,0:T(8,128)(2,1)S(1)}, u32[]{:S(2)}, u32[]{:S(2)}) %collective-permute-start.8) | collective-permute-done | bytes 786464 | tf_op jit(solution)/shard_map/ppermute | solution.py:320
  610.3 11.4 %collective-permute-done.9 = bf16[256,768]{1,0:T(8,128)(2,1)S(1)} collective-permute-done((bf16[256,768]{1,0:T(8,128)(2,1)}, bf16[256,768]{1,0:T(8,128)(2,1)S(1)}, u32[]{:S(2)}, u32[]{:S(2)}) %collective-permute-start.9) | collective-permute-done | bytes 393248 | tf_op jit(solution)/shard_map/ppermute | solution.py:320
  627.8 13.9 %collective-permute-done.2 = bf16[2,256,2048]{2,1,0:T(8,128)(2,1)} collective-permute-done((bf16[2,256,2048]{2,1,0:T(8,128)(2,1)}, bf16[2,256,2048]{2,1,0:T(8,128)(2,1)}, u32[]{:S(2)}, u32[]{:S(2)}) %collective-permute-start.2) | collective-permute-done | bytes 2097184 | tf_op jit(solution)/shard_map/ppermute | solution.py:323
  658.8 28.6 %collective-permute-done.6 = bf16[256,2048]{1,0:T(8,128)(2,1)} collective-permute-done((bf16[256,2048]{1,0:T(8,128)(2,1)}, bf16[256,2048]{1,0:T(8,128)(2,1)}, u32[]{:S(2)}, u32[]{:S(2)}) %collective-permute-start.6) | collective-permute-done | bytes 1048608 | tf_op jit(solution)/shard_map/ppermute | solution.py:320
  689.3 19.7 %collective-permute-done.3 = bf16[256,2048]{1,0:T(8,128)(2,1)} collective-permute-done((bf16[256,2048]{1,0:T(8,128)(2,1)}, bf16[256,2048]{1,0:T(8,128)(2,1)}, u32[]{:S(2)}, u32[]{:S(2)}) %collective-permute-start.3) | collective-permute-done | bytes 1048608 | tf_op jit(solution)/shard_map/ppermute | solution.py:320
  709.1 5.4 convert_reduce_fusion.5
  717.0 4.8 collective-permute-done.19
  723.4 5.3 multiply_subtract_fusion
  741.5 6.9 multiply_subtract_fusion.1
  (289 shorter events, 184.3 us)
Async XLA Ops:
  1.3 343.1 %collective-permute-start = (f32[1,1024]{1,0:T(1,128)S(1)}, f32[1,1024]{1,0:T(1,128)S(1)}, u32[]{:S(2)}, u32[]{:S(2)}) collective-permute-start(f32[1,1024]{1,0:T(1,128)S(1)} %convert_element_type.329), channel_id=1, source_target_pairs={{0,8},{4,12},{8,0},{12,4},{16,24},{20,28},{24,16},{28,20},{1,9},{5... | collective-permute-start | bytes 12296 | tf_op jit(solution)/shard_map/ppermute | solution.py:320
  4.0 210.4 %copy-start.43 = (f32[1,2048]{1,0:T(1,128)}, f32[1,2048]{1,0:T(1,128)S(1)}, u32[]{:S(2)}) copy-start(f32[1,2048]{1,0:T(1,128)S(1)} %get-tuple-element.130) | copy-start | bytes 24580
  4.0 210.4 %copy-start.45 = (f32[1,2048]{1,0:T(1,128)}, f32[1,2048]{1,0:T(1,128)S(1)}, u32[]{:S(2)}) copy-start(f32[1,2048]{1,0:T(1,128)S(1)} %get-tuple-element.131) | copy-start | bytes 24580
  4.0 210.4 %copy-start.47 = (f32[1,2048]{1,0:T(1,128)}, f32[1,2048]{1,0:T(1,128)S(1)}, u32[]{:S(2)}) copy-start(f32[1,2048]{1,0:T(1,128)S(1)} %get-tuple-element.132) | copy-start | bytes 24580
  4.0 210.4 %copy-start.49 = (f32[1,2048]{1,0:T(1,128)}, f32[1,2048]{1,0:T(1,128)S(1)}, u32[]{:S(2)}) copy-start(f32[1,2048]{1,0:T(1,128)S(1)} %get-tuple-element.133) | copy-start | bytes 24580
  15.8 190.5 %copy-start.9 = (f32[1,3,256,512]{2,3,1,0:T(8,128)}, f32[1,3,256,512]{2,3,1,0:T(8,128)S(1)}, u32[]{:S(2)}) copy-start(f32[1,3,256,512]{2,3,1,0:T(8,128)S(1)} %copy.154) | copy-start | bytes 4718596
  254.9 304.6 %collective-permute-start.16 = (bf16[2,256,2048]{2,1,0:T(8,128)(2,1)}, bf16[2,256,2048]{2,1,0:T(8,128)(2,1)}, u32[]{:S(2)}, u32[]{:S(2)}) collective-permute-start(bf16[2,256,2048]{2,1,0:T(8,128)(2,1)} %dynamic-slice_bitcast_fusion), channel_id=1, source_target_pairs={{0,4},{4,0},{8,12},{12,8},{16,20},{20,16},{24,28},{28,24},{1,5},{5... | collective-permute-start | bytes 6291464 | tf_op jit(solution)/shard_map/ppermute | solution.py:320
  375.2 132.7 %collective-permute-start.10 = (bf16[2,64,2048]{2,1,0:T(8,128)(2,1)}, bf16[2,64,2048]{2,1,0:T(8,128)(2,1)}, u32[]{:S(2)}, u32[]{:S(2)}) collective-permute-start(bf16[2,64,2048]{2,1,0:T(8,128)(2,1)} %dynamic-slice_bitcast_fusion.8), channel_id=1, source_target_pairs={{0,4},{4,0},{8,12},{12,8},{16,20},{20,16},{24,28},{28,24},{1,5},{5... | collective-permute-start | bytes 1572872 | tf_op jit(solution)/shard_map/ppermute | solution.py:320
  392.8 157.7 %collective-permute-start.1 = (bf16[2,2,256,2048]{3,2,0,1:T(8,128)(2,1)}, bf16[2,2,256,2048]{3,2,0,1:T(8,128)(2,1)}, u32[]{:S(2)}, u32[]{:S(2)}) collective-permute-start(bf16[2,2,256,2048]{3,2,0,1:T(8,128)(2,1)} %bitcast.216), channel_id=1, source_target_pairs={{0,1},{1,0},{2,3},{3,2},{4,5},{5,4},{6,7},{7,6},{8,9},{9,8},{10,11... | collective-permute-start | bytes 12582920 | tf_op jit(solution)/shard_map/ppermute | solution.py:323
  454.6 90.7 %collective-permute-start.4 = (bf16[2,2,256,2048]{3,2,0,1:T(8,128)(2,1)}, bf16[2,2,256,2048]{3,2,0,1:T(8,128)(2,1)}, u32[]{:S(2)}, u32[]{:S(2)}) collective-permute-start(bf16[2,2,256,2048]{3,2,0,1:T(8,128)(2,1)} %bitcast.215), channel_id=1, source_target_pairs={{0,1},{1,0},{2,3},{3,2},{4,5},{5,4},{6,7},{7,6},{8,9},{9,8},{10,11... | collective-permute-start | bytes 12582920 | tf_op jit(solution)/shard_map/ppermute | solution.py:323
  506.5 37.4 %collective-permute-start.7 = (bf16[2,2,256,768]{3,2,1,0:T(8,128)(2,1)}, bf16[2,2,256,768]{3,2,1,0:T(8,128)(2,1)S(1)}, u32[]{:S(2)}, u32[]{:S(2)}) collective-permute-start(bf16[2,2,256,768]{3,2,1,0:T(8,128)(2,1)} %dynamic-slice_bitcast_fusion.4), channel_id=1, source_target_pairs={{0,4},{4,0},{8,12},{12,8},{16,20},{20,16},{24,28},{28,24},{1,5},{5... | collective-permute-start | bytes 4718600 | tf_op jit(solution)/shard_map/ppermute | solution.py:320
  509.3 12.2 %collective-permute-start.11 = (bf16[1,64,2048]{2,1,0:T(8,128)(2,1)S(1)}, bf16[1,64,2048]{2,1,0:T(8,128)(2,1)}, u32[]{:S(2)}, u32[]{:S(2)}) collective-permute-start(bf16[1,64,2048]{2,1,0:T(8,128)(2,1)S(1)} %constant_dynamic-slice_fusion.3), channel_id=1, source_target_pairs={{0,16},{4,20},{8,24},{12,28},{16,0},{20,4},{24,8},{28,12},{1,17},{... | collective-permute-start | bytes 786440 | tf_op jit(solution)/shard_map/ppermute | solution.py:320
  522.5 3.5 collective-permute-start.12
  526.0 78.1 %collective-permute-start.13 = (bf16[2,2,256,1024]{3,2,1,0:T(8,128)(2,1)S(1)}, bf16[2,2,256,1024]{3,2,1,0:T(8,128)(2,1)S(1)}, u32[]{:S(2)}, u32[]{:S(2)}) collective-permute-start(bf16[2,2,256,1024]{3,2,1,0:T(8,128)(2,1)S(1)} %dynamic-slice_bitcast_fusion.1), channel_id=1, source_target_pairs={{0,4},{4,0},{8,12},{12,8},{16,20},{20,16},{24,28},{28,24},{1,5},{5... | collective-permute-start | bytes 6291464 | tf_op jit(solution)/shard_map/ppermute | solution.py:320
  545.3 56.4 %collective-permute-start.8 = (bf16[1,2,256,768]{3,2,1,0:T(8,128)(2,1)}, bf16[1,2,256,768]{3,2,1,0:T(8,128)(2,1)S(1)}, u32[]{:S(2)}, u32[]{:S(2)}) collective-permute-start(bf16[1,2,256,768]{3,2,1,0:T(8,128)(2,1)} %constant_dynamic-slice_fusion.5), channel_id=1, source_target_pairs={{0,16},{4,20},{8,24},{12,28},{16,0},{20,4},{24,8},{28,12},{1,17},{... | collective-permute-start | bytes 2359304 | tf_op jit(solution)/shard_map/ppermute | solution.py:320
  549.7 72.6 %collective-permute-start.5 = (bf16[2,256,2048]{2,1,0:T(8,128)(2,1)S(1)}, bf16[2,256,2048]{2,1,0:T(8,128)(2,1)}, u32[]{:S(2)}, u32[]{:S(2)}) collective-permute-start(bf16[2,256,2048]{2,1,0:T(8,128)(2,1)S(1)} %dynamic-slice_bitcast_fusion.2), channel_id=1, source_target_pairs={{0,2},{1,3},{2,0},{3,1},{4,6},{5,7},{6,4},{7,5},{8,10},{9,11},{10,... | collective-permute-start | bytes 6291464 | tf_op jit(solution)/shard_map/ppermute | solution.py:323
  558.7 83.0 %collective-permute-start.2 = (bf16[2,256,2048]{2,1,0:T(8,128)(2,1)}, bf16[2,256,2048]{2,1,0:T(8,128)(2,1)}, u32[]{:S(2)}, u32[]{:S(2)}) collective-permute-start(bf16[2,256,2048]{2,1,0:T(8,128)(2,1)} %dynamic-slice_bitcast_fusion.3), channel_id=1, source_target_pairs={{0,2},{1,3},{2,0},{3,1},{4,6},{5,7},{6,4},{7,5},{8,10},{9,11},{10,... | collective-permute-start | bytes 6291464 | tf_op jit(solution)/shard_map/ppermute | solution.py:323
  565.1 158.2 %collective-permute-start.17 = (bf16[1,256,2048]{2,1,0:T(8,128)(2,1)}, bf16[1,256,2048]{2,1,0:T(8,128)(2,1)}, u32[]{:S(2)}, u32[]{:S(2)}) collective-permute-start(bf16[1,256,2048]{2,1,0:T(8,128)(2,1)} %constant_dynamic-slice_fusion), channel_id=1, source_target_pairs={{0,16},{4,20},{8,24},{12,28},{16,0},{20,4},{24,8},{28,12},{1,17},{... | collective-permute-start | bytes 3145736 | tf_op jit(solution)/shard_map/ppermute | solution.py:320
  602.7 19.0 %collective-permute-start.9 = (bf16[256,768]{1,0:T(8,128)(2,1)}, bf16[256,768]{1,0:T(8,128)(2,1)S(1)}, u32[]{:S(2)}, u32[]{:S(2)}) collective-permute-start(bf16[256,768]{1,0:T(8,128)(2,1)} %get-tuple-element.128), channel_id=1, source_target_pairs={{0,8},{4,12},{8,0},{12,4},{16,24},{20,28},{24,16},{28,20},{1,9},{5... | collective-permute-start | bytes 1179656 | tf_op jit(solution)/shard_map/ppermute | solution.py:320
  606.9 107.8 %collective-permute-start.14 = (bf16[1,2,256,1024]{3,2,1,0:T(8,128)(2,1)}, bf16[1,2,256,1024]{3,2,1,0:T(8,128)(2,1)}, u32[]{:S(2)}, u32[]{:S(2)}) collective-permute-start(bf16[1,2,256,1024]{3,2,1,0:T(8,128)(2,1)} %constant_dynamic-slice_fusion.2), channel_id=1, source_target_pairs={{0,16},{4,20},{8,24},{12,28},{16,0},{20,4},{24,8},{28,12},{1,17},{... | collective-permute-start | bytes 3145736 | tf_op jit(solution)/shard_map/ppermute | solution.py:320
  627.8 59.6 %collective-permute-start.6 = (bf16[256,2048]{1,0:T(8,128)(2,1)}, bf16[256,2048]{1,0:T(8,128)(2,1)}, u32[]{:S(2)}, u32[]{:S(2)}) collective-permute-start(bf16[256,2048]{1,0:T(8,128)(2,1)} %dynamic-slice_bitcast_fusion.5), channel_id=1, source_target_pairs={{0,8},{4,12},{8,0},{12,4},{16,24},{20,28},{24,16},{28,20},{1,9},{5... | collective-permute-start | bytes 3145736 | tf_op jit(solution)/shard_map/ppermute | solution.py:320
  646.4 62.6 %collective-permute-start.3 = (bf16[256,2048]{1,0:T(8,128)(2,1)}, bf16[256,2048]{1,0:T(8,128)(2,1)}, u32[]{:S(2)}, u32[]{:S(2)}) collective-permute-start(bf16[256,2048]{1,0:T(8,128)(2,1)} %dynamic-slice_bitcast_fusion.6), channel_id=1, source_target_pairs={{0,8},{4,12},{8,0},{12,4},{16,24},{20,28},{24,16},{28,20},{1,9},{5... | collective-permute-start | bytes 3145736 | tf_op jit(solution)/shard_map/ppermute | solution.py:320
  655.8 53.3 %copy-start.51 = (f32[1,2048]{1,0:T(1,128)S(1)}, f32[1,2048]{1,0:T(1,128)}, u32[]{:S(2)}) copy-start(f32[1,2048]{1,0:T(1,128)} %get-tuple-element.129) | copy-start | bytes 24580
  655.8 53.3 %copy-start.52 = (f32[1,2048]{1,0:T(1,128)S(1)}, f32[1,2048]{1,0:T(1,128)}, u32[]{:S(2)}) copy-start(f32[1,2048]{1,0:T(1,128)} %get-tuple-element.134) | copy-start | bytes 24580
  658.8 50.2 %copy-start.17 = (bf16[2,256,2048]{2,1,0:T(8,128)(2,1)S(1)}, bf16[2,256,2048]{2,1,0:T(8,128)(2,1)}, u32[]{:S(2)}) copy-start(bf16[2,256,2048]{2,1,0:T(8,128)(2,1)} %copy-done.16) | copy-start | bytes 6291460
  658.8 50.2 %copy-start.25 = (bf16[256,2048]{1,0:T(8,128)(2,1)S(1)}, bf16[256,2048]{1,0:T(8,128)(2,1)}, u32[]{:S(2)}) copy-start(bf16[256,2048]{1,0:T(8,128)(2,1)} %e.1) | copy-start | bytes 3145732
  714.5 1.9 collective-permute-start.18
  716.6 5.3 collective-permute-start.19
  716.9 14.0 %collective-permute-start.15 = (bf16[256,1024]{1,0:T(8,128)(2,1)S(1)}, bf16[256,1024]{1,0:T(8,128)(2,1)S(1)}, u32[]{:S(2)}, u32[]{:S(2)}) collective-permute-start(bf16[256,1024]{1,0:T(8,128)(2,1)S(1)} %get-tuple-element.126), channel_id=1, source_target_pairs={{0,8},{4,12},{8,0},{12,4},{16,24},{20,28},{24,16},{28,20},{1,9},{5... | collective-permute-start | bytes 1572872 | tf_op jit(solution)/shard_map/ppermute | solution.py:320
  721.9 9.2 %collective-permute-start.20 = (f32[1,26624]{1,0:T(1,128)S(1)}, f32[1,26624]{1,0:T(1,128)S(1)}, u32[]{:S(2)}, u32[]{:S(2)}) collective-permute-start(f32[1,26624]{1,0:T(1,128)S(1)} %add.463), channel_id=1, source_target_pairs={{0,4},{4,0},{8,12},{12,8},{16,20},{20,16},{24,28},{28,24},{1,5},{5... | collective-permute-start | bytes 319496 | tf_op jit(solution)/shard_map/ppermute | solution.py:320
  731.3 7.0 collective-permute-start.21
  738.5 9.9 %collective-permute-start.22 = (f32[1,26624]{1,0:T(1,128)S(1)}, f32[1,26624]{1,0:T(1,128)S(1)}, u32[]{:S(2)}, u32[]{:S(2)}) collective-permute-start(f32[1,26624]{1,0:T(1,128)S(1)} %add.465), channel_id=1, source_target_pairs={{0,16},{4,20},{8,24},{12,28},{16,0},{20,4},{24,8},{28,12},{1,17},{... | collective-permute-start | bytes 319496 | tf_op jit(solution)/shard_map/ppermute | solution.py:320
  (52 other events, 636.6 us)

commit v3 on v2

v3 whole, which is shorter than its diff:
```python
import functools

import jax
import jax.numpy as jnp
from jax import lax
from jax.experimental import pallas as pl
from jax.experimental.pallas import tpu as pltpu
from jax.sharding import PartitionSpec as P

HD = 256
ROT = 64
STEP = 10

norm_eps = 1e-05
beta_one = 0.9
beta_two = 0.95
adam_eps = 1e-08
decay_rate = 0.01
rate_vector = 0.2
masked_score = -1e30
f32 = jnp.float32
bf16 = jnp.bfloat16


def adam_step(weight, first, second, grad, rate, decay):
    first_new = beta_one * first + (1.0 - beta_one) * grad
    second_new = beta_two * second + (1.0 - beta_two) * grad * grad
    first_hat = first_new / (1.0 - beta_one**STEP)
    second_hat = second_new / (1.0 - beta_two**STEP)
    weight_new = weight - rate * (first_hat / (jnp.sqrt(second_hat) + adam_eps) + decay * weight)
    return (first_new, second_new, weight_new)


MESH = pl.DeviceIdType.MESH


def bit_of(i, mask):
    return (i // mask) % 2


def flip(i, mask):
    return i + mask - 2 * mask * bit_of(i, mask)


class Links:
    def __init__(self, send_sem, recv_sem):
        self.send_sem, self.recv_sem, self.count, self.started = send_sem, recv_sem, 0, []

    def copy(self, src, dst, device):
        k = self.count
        self.count += 1
        c = pltpu.make_async_remote_copy(
            src_ref=src,
            dst_ref=dst,
            send_sem=self.send_sem.at[k],
            recv_sem=self.recv_sem.at[k],
            device_id=device,
            device_id_type=MESH,
        )
        self.started.append(c)
        return c


class Group:
    def __init__(self, links, at, f, t, masks, root):
        self.links, self.at, self.f, self.t, self.masks = links, at, f, t, masks
        self.root, self.copies = root, {}

    def _source(self, key):
        g = self.root
        for mask in self.masks:
            if key & mask:
                g = flip(g, mask)
        return g

    def have(self, key):
        after = max([i + 1 for i, m in enumerate(self.masks) if key & m], default=0)
        for mask in self.masks[after:]:
            ref = self.at(self._source(key))
            c = self.links.copy(ref, ref, (flip(self.f, mask), self.t))
            c.start()
            self.copies[key | mask] = c

    def arrive(self, key):
        self.copies[key].wait_recv()
        self.have(key)


def all_keys(masks):
    keys = [0]
    for mask in masks:
        keys = keys + [k | mask for k in keys]
    return keys


def normalise(x):
    mean = jnp.mean(x, axis=-1, keepdims=True)
    centred = x - mean
    inverse = lax.rsqrt(jnp.mean(centred * centred, axis=-1, keepdims=True) + norm_eps)
    return centred * inverse


def rope(u, c, s):
    lane = lax.broadcasted_iota(jnp.int32, u.shape, 1)
    partner = jnp.where(lane < ROT // 2, pltpu.roll(u, 128 - ROT // 2, 1), pltpu.roll(u, ROT // 2, 1))
    return u * c + partner * s


def dot(a, b, dims):
    return lax.dot_general(a, b, (dims, ((), ())), preferred_element_type=f32)


NN = ((1,), (0,))
NT = ((1,), (1,))
TN = ((0,), (0,))
TILE = 256


def tiles(width):
    return pl.BlockSpec((TILE, width), lambda i: (i, 0))


def columns(height, width):
    return pl.BlockSpec((height, width), lambda i: (0, i))


def held(height, width):
    return pl.BlockSpec((height, width), lambda i: (0, 0))


def run_project(vec, qkv_bias, x, w, c, s, n1, n2, p):
    tokens, d = x.shape
    wide = w.shape[1]

    def body(x_ref, w_ref, c_ref, s_ref, n1_ref, n2_ref, p_ref):
        normal = normalise(x_ref[...].astype(f32))
        one = (normal * vec[0:1, :] + vec[1:2, :]).astype(bf16)
        n1_ref[...] = one
        n2_ref[...] = (normal * vec[2:3, :] + vec[3:4, :]).astype(bf16)
        proj = dot(one, w_ref[...], NN) + qkv_bias[...]
        for j in range(2):
            p_ref[:, j * HD : j * HD + 128] = rope(
                proj[:, j * HD : j * HD + 128], c_ref[...], s_ref[...]
            ).astype(bf16)
            p_ref[:, j * HD + 128 : (j + 1) * HD] = proj[:, j * HD + 128 : (j + 1) * HD].astype(bf16)
        p_ref[:, 2 * HD :] = proj[:, 2 * HD :].astype(bf16)

    pltpu.emit_pipeline(
        body,
        grid=(tokens // TILE,),
        in_specs=[tiles(d), held(d, wide), tiles(128), tiles(128)],
        out_specs=[tiles(d), tiles(d), tiles(wide)],
    )(x, w, c, s, n1, n2, p)


def run_times(a, b, out, dims):
    def body(a_ref, b_ref, out_ref):
        out_ref[...] = dot(a_ref[...], b_ref[...], dims).astype(bf16)

    pltpu.emit_pipeline(
        body,
        grid=(a.shape[0] // TILE,),
        in_specs=[tiles(a.shape[1]), held(*b.shape)],
        out_specs=[tiles(out.shape[1])],
    )(a, b, out)


def run_outer(a, b, out):
    def body(a_ref, b_ref, out_ref):
        out_ref[...] = dot(a_ref[...], b_ref[...], TN).astype(bf16)

    pltpu.emit_pipeline(
        body,
        grid=(a.shape[1] // TILE,),
        in_specs=[columns(a.shape[0], TILE), held(*b.shape)],
        out_specs=[tiles(b.shape[1])],
    )(a, b, out)


def run_outer_wide(a, b, out):
    block = 2 * TILE

    def body(a_ref, b_ref, out_ref):
        out_ref[...] = dot(a_ref[...], b_ref[...], TN).astype(bf16)

    pltpu.emit_pipeline(
        body,
        grid=(b.shape[1] // block,),
        in_specs=[held(*a.shape), columns(b.shape[0], block)],
        out_specs=[columns(a.shape[1], block)],
    )(a, b, out)


def run_attention(length, bounds, p, da, c, s, a, dproj, dk, dv):
    scale = HD ** (-0.5)
    rows = pl.BlockSpec((length, HD), lambda i: (i, 0))
    wide = pl.BlockSpec((length, 3 * HD), lambda i: (i, 0))
    narrow = pl.BlockSpec((length, 128), lambda i: (i, 0))

    def body(p_ref, da_ref, c_ref, s_ref, a_ref, out_ref):
        seq = pl.program_id(0)
        first, second = bounds[seq, 0], bounds[seq, 1]

        def put(at, value, column):
            out_ref[at, column : column + 128] = rope(value[:, :128], c_ref[at, :], -s_ref[at, :]).astype(bf16)
            out_ref[at, column + 128 : column + HD] = value[:, 128:].astype(bf16)

        dk[...] = jnp.zeros_like(dk)
        dv[...] = jnp.zeros_like(dv)
        for i in range(length // TILE):
            at = slice(i * TILE, (i + 1) * TILE)
            n = (i + 1) * TILE
            q = p_ref[at, 0:HD]
            k = p_ref[0:n, HD : 2 * HD]
            v = p_ref[0:n, 2 * HD :]
            rows_da = da_ref[at, :]
            scores = dot(q, k, NT) * scale
            qi = i * TILE + lax.broadcasted_iota(jnp.int32, (TILE, n), 0)
            ki = lax.broadcasted_iota(jnp.int32, (TILE, n), 1)
            start = jnp.where(qi >= second, second, jnp.where(qi >= first, first, 0))
            scores = jnp.where((ki <= qi) & (ki >= start), scores, masked_score)
            peak = jnp.max(scores, axis=-1, keepdims=True)
            raised = jnp.exp(scores - peak)
            probs = raised * (1.0 / jnp.sum(raised, axis=-1, keepdims=True))
            weights = probs.astype(bf16)
            a_ref[at, :] = dot(weights, v, NN).astype(bf16)
            prob_grad = dot(rows_da, v, NT)
            delta = jnp.sum(probs * prob_grad, axis=-1, keepdims=True)
            score_grad = (probs * (prob_grad - delta)).astype(bf16)
            put(at, dot(score_grad, k, NN) * scale, 0)
            dk[0:n, :] += dot(score_grad, q, TN)
            dv[0:n, :] += dot(weights, rows_da, TN)
        for i in range(length // TILE):
            at = slice(i * TILE, (i + 1) * TILE)
            put(at, dk[at, :] * scale, HD)
            out_ref[at, 2 * HD :] = dv[at, :].astype(bf16)

    pltpu.emit_pipeline(
        body,
        grid=(p.shape[0] // length,),
        in_specs=[wide, rows, narrow, narrow],
        out_specs=[rows, wide],
    )(p, da, c, s, a, dproj)


def run_up(up_bias, n2, w, g, slope):
    def body(n_ref, w_ref, g_ref, s_ref):
        h = dot(n_ref[...], w_ref[...], NN) + up_bias[...]
        cdf = 0.5 + 0.5 * lax.erf(h * 0.7071067811865476)
        g_ref[...] = (h * cdf).astype(bf16)
        s_ref[...] = (cdf + h * (jnp.exp(-0.5 * h * h) * 0.3989422804014327)).astype(bf16)

    width = w.shape[1]
    pltpu.emit_pipeline(
        body,
        grid=(n2.shape[0] // TILE,),
        in_specs=[tiles(n2.shape[1]), held(*w.shape)],
        out_specs=[tiles(width), tiles(width)],
    )(n2, w, g, slope)


def run_hidden_grad(e, w, slope, dh, bias_sum):
    def body(e_ref, w_ref, s_ref, dh_ref):
        @pl.when(pl.program_id(0) == 0)
        def _():
            bias_sum[...] = jnp.zeros_like(bias_sum)

        value = (dot(e_ref[...], w_ref[...], NT) * s_ref[...].astype(f32)).astype(bf16)
        dh_ref[...] = value
        bias_sum[0:1, :] += jnp.sum(value.astype(f32), axis=0, keepdims=True)

    width = w.shape[0]
    pltpu.emit_pipeline(
        body,
        grid=(e.shape[0] // TILE,),
        in_specs=[tiles(e.shape[1]), held(*w.shape), tiles(width)],
        out_specs=[tiles(width)],
    )(e, w, slope, dh)


def run_branch(a, w_out, g, w_down, out):
    def body(a_ref, wo_ref, g_ref, wd_ref, out_ref):
        out_ref[...] = (dot(a_ref[...], wo_ref[...], NN) + dot(g_ref[...], wd_ref[...], NN)).astype(bf16)

    pltpu.emit_pipeline(
        body,
        grid=(a.shape[0] // TILE,),
        in_specs=[tiles(a.shape[1]), held(*w_out.shape), tiles(g.shape[1]), held(*w_down.shape)],
        out_specs=[tiles(out.shape[1])],
    )(a, w_out, g, w_down, out)


def run_norm_grad(vec, dh, w_up, dproj, w_qkv, x, out, sums, qkv_sum):
    def body(dh_ref, wu_ref, dp_ref, wq_ref, x_ref, out_ref):
        @pl.when(pl.program_id(0) == 0)
        def _():
            sums[...] = jnp.zeros_like(sums)
            qkv_sum[...] = jnp.zeros_like(qkv_sum)

        normal = normalise(x_ref[...].astype(f32))
        one = dot(dp_ref[...], wq_ref[...], NT)
        two = dot(dh_ref[...], wu_ref[...], NT)
        for j, value in ((0, one * normal), (1, one), (2, two * normal), (3, two)):
            sums[j : j + 1, :] += jnp.sum(value, axis=0, keepdims=True)
        out_ref[...] = (one * vec[0:1, :] + two * vec[2:3, :]).astype(bf16)
        qkv_sum[0:1, :] += jnp.sum(dp_ref[...].astype(f32), axis=0, keepdims=True)

    pltpu.emit_pipeline(
        body,
        grid=(x.shape[0] // TILE,),
        in_specs=[tiles(dh.shape[1]), held(*w_up.shape), tiles(dproj.shape[1]), held(*w_qkv.shape), tiles(x.shape[1])],
        out_specs=[tiles(out.shape[1])],
    )(dh, w_up, dproj, w_qkv, x, out)


def run_add(a, b, out):
    rows, cols = out.shape
    step = min(rows, TILE)

    def body(a_ref, b_ref, out_ref):
        out_ref[...] = (a_ref[...].astype(f32) + b_ref[...].astype(f32)).astype(bf16)

    spec = pl.BlockSpec((step, cols), lambda i: (i, 0))
    pltpu.emit_pipeline(body, grid=(rows // step,), in_specs=[spec, spec], out_specs=[spec])(a, b, out)


def block(ref, index, rows):
    return ref.at[pl.ds(pl.multiple_of(index * rows, rows), rows)]


def out_place(g, top):
    return (((g // 4) % (top // 4)) * 2 + g // top) * 2 + g % 2


def greet(f, t, masks, top):
    mid = bit_of(f, 2)
    swapped = f + (top - 2) * (mid - bit_of(f, top))
    barrier = pltpu.get_barrier_semaphore()
    peers = [(flip(f, m), t) for m in masks + [2]] + [(f, flip(t, 1)), (f, flip(t, 2))]
    for peer in peers:
        pl.semaphore_signal(barrier, inc=1, device_id=peer, device_id_type=MESH)

    @pl.when(swapped != f)
    def _():
        pl.semaphore_signal(barrier, inc=1, device_id=(swapped, t), device_id_type=MESH)

    pl.semaphore_wait(barrier, len(peers) + (mid + bit_of(f, top)) % 2)
    return swapped


def gather_kernel(
    masks, top, length,
    x, e, up, qkv, down, out, cos, sin, vec, qkv_bias, up_bias, bounds,
    xa, ea, upa, qkva, downa, outa, n1, n2, p, da, a, dproj, g_qkv, g_out, g, slope, g_down,
    send_sem, recv_sem, local_sem, dk, dv,
):
    f = lax.axis_index("fsdp")
    t = lax.axis_index("tp")
    mid = bit_of(f, 2)
    rows, feat, sub, orow = x.shape[0], up.shape[1], down.shape[0], out.shape[0]
    swapped = greet(f, t, masks, top)
    links = Links(send_sem, recv_sem)
    own = []

    def local_copy(src, dst):
        c = pltpu.make_async_copy(src, dst, local_sem.at[len(own)])
        own.append(c)
        c.start()
        return c

    mid_peer, y_peer, core_peer = (flip(f, 2), t), (f, flip(t, 2)), (f, flip(t, 1))
    qkv_block = lambda i: block(qkva, i, feat)
    up_block = lambda i: block(upa, i, feat)
    down_block = lambda i: block(downa, (i // 4) * 2 + i % 2, sub)
    out_block = lambda i: block(outa, out_place(i, top), orow)
    tok = lambda buf, m, j: block(buf, m * 4 + j, rows)
    qkv_own = Group(links, qkv_block, f, t, masks, f)
    qkv_mid = Group(links, qkv_block, f, t, masks, flip(f, 2))
    up_own = Group(links, up_block, f, t, masks, f)
    up_mid = Group(links, up_block, f, t, masks, flip(f, 2))
    down_own = Group(links, down_block, f, t, masks, f)
    out_own = Group(links, out_block, f, t, masks, f)

    def spread(group, source):
        for mask in group.masks:
            c = links.copy(source, group.at(f), (flip(f, mask), t))
            c.start()
            group.copies[mask] = c

    def tokens(source, buf):
        parts = {}
        for name, peer in (("m", mid_peer), ("y", y_peer), ("c", core_peer)):
            parts[name] = links.copy(source, tok(buf, mid, t), peer)
            parts[name].start()
        return parts

    def forward(buf, parts, name, m, j, sends):
        parts[name].wait_recv()
        ref = tok(buf, m, j)
        for new, peer in sends:
            parts[new] = links.copy(ref, ref, peer)
            parts[new].start()

    def tokens_mid(buf, parts):
        forward(buf, parts, "m", 1 - mid, t, (("my", y_peer), ("mc", core_peer)))

    def tokens_y(buf, parts):
        forward(buf, parts, "y", mid, flip(t, 2), (("yc", core_peer),))

    def tokens_last(buf, parts):
        forward(buf, parts, "my", 1 - mid, flip(t, 2), (("myc", core_peer),))

    def tokens_done(parts):
        for name in ("c", "mc", "yc", "myc"):
            parts[name].wait_recv()

    keys = all_keys(masks)[1:]
    first_qkv = links.copy(qkv.at[1 - mid], qkv_block(f), mid_peer)
    first_qkv.start()
    spread(qkv_own, qkv.at[mid])
    x_parts = tokens(x, xa)
    swap_copy = links.copy(out, out_block(swapped), (swapped, t))
    own_out = pltpu.make_async_copy(out, out_block(f), local_sem.at[5])

    @pl.when(swapped != f)
    def _():
        swap_copy.start()

    @pl.when(swapped == f)
    def _():
        own_out.start()

    first_up = links.copy(up.at[1 - mid], up_block(f), mid_peer)
    first_up.start()
    local_copy(qkv.at[mid], qkv_block(f))
    local_copy(x, tok(xa, mid, t))
    local_copy(up.at[mid], up_block(f))
    local_copy(e, tok(ea, mid, t))
    local_copy(down, down_block(f))
    first_qkv.wait_recv()
    qkv_mid.have(0)
    spread(up_own, up.at[mid])
    e_parts = tokens(e, ea)
    tokens_mid(xa, x_parts)
    tokens_y(xa, x_parts)

    @pl.when(swapped != f)
    def _():
        swap_copy.wait_recv()

    @pl.when(swapped == f)
    def _():
        own_out.wait()

    out_own.have(0)
    for key in keys:
        qkv_own.arrive(key)
    first_up.wait_recv()
    up_mid.have(0)
    for key in keys:
        qkv_mid.arrive(key)
    tokens_last(xa, x_parts)
    for key in keys:
        out_own.arrive(key)
    spread(down_own, down)
    tokens_mid(ea, e_parts)
    tokens_y(ea, e_parts)
    tokens_done(x_parts)
    own[0].wait()
    own[1].wait()
    run_project(vec, qkv_bias, xa, qkva, cos, sin, n1, n2, p)
    for key in keys:
        up_own.arrive(key)
    for key in keys:
        up_mid.arrive(key)
    tokens_last(ea, e_parts)
    tokens_done(e_parts)
    own[3].wait()
    run_times(ea, outa, da, NT)
    run_attention(length, bounds, p, da, cos, sin, a, dproj, dk, dv)
    run_outer(n1, dproj, g_qkv)
    run_outer_wide(a, ea, g_out)
    own[2].wait()
    run_up(up_bias, n2, upa, g, slope)
    run_outer(g, ea, g_down)
    for key in keys:
        down_own.arrive(key)
    own[4].wait()
    for c in links.started:
        if c is swap_copy:

            @pl.when(swapped != f)
            def _():
                swap_copy.wait_send()

        else:
            c.wait_send()


ANY = pl.BlockSpec(memory_space=pl.ANY)
VMEM = pl.BlockSpec(memory_space=pltpu.VMEM)
SMEM = pl.BlockSpec(memory_space=pltpu.SMEM)


def gather_all(masks, top, length, tp, x, e, up, qkv, down, out, cos, sin, vec, qkv_bias, up_bias, bounds):
    rows, d = x.shape
    tokens = 2 * tp * rows
    mine, wide = up.shape[2], qkv.shape[2]
    n_keys = 1 << len(masks)
    copies = 2 * 7 + 2 * (1 + 2 * (n_keys - 1)) + n_keys - 1 + n_keys
    shapes = [
        (tokens, d), (tokens, d), (d, mine), (d, wide), (mine, d), (HD, d),
        (tokens, d), (tokens, d), (tokens, wide), (tokens, HD), (tokens, HD), (tokens, wide),
        (d, wide), (HD, d), (tokens, mine), (tokens, mine), (mine, d),
    ]
    return pl.pallas_call(
        functools.partial(gather_kernel, masks, top, length),
        out_shape=[jax.ShapeDtypeStruct(shape, bf16) for shape in shapes],
        in_specs=[ANY] * 8 + [VMEM] * 3 + [SMEM],
        out_specs=[ANY] * len(shapes),
        scratch_shapes=[
            pltpu.SemaphoreType.DMA((copies,)),
            pltpu.SemaphoreType.DMA((copies,)),
            pltpu.SemaphoreType.DMA((6,)),
            pltpu.VMEM((length, HD), f32),
            pltpu.VMEM((length, HD), f32),
        ],
        compiler_params=pltpu.CompilerParams(
            collective_id=0, has_side_effects=True, vmem_limit_bytes=56 * 2**20
        ),
        name="gather_and_attend",
    )(x, e, up, qkv, down, out, cos, sin, vec, qkv_bias, up_bias, bounds)


class Scatter:
    def __init__(self, links, part, place, rows, mids, recv, sums, f, t, masks):
        self.links, self.part, self.place, self.rows, self.mids = links, part, place, rows, mids
        self.recv, self.sums, self.f, self.t = recv, sums, f, t
        self.stages = [1] + [m for m in reversed(masks) if m != 1]
        self.n_hi = 1 << (len(masks) - 1)
        self.hi, self.lo = f // 4, f % 2
        self.copies = {}

    def high(self, k):
        hi = self.hi
        b = 1
        while b < self.n_hi:
            if k & b:
                hi = flip(hi, b)
            b *= 2
        return hi

    def slot(self, level, k, m):
        n = self.n_hi >> level
        i = (self.high(k) % n) if n > 1 else 0
        return i * len(self.mids) + m

    def source(self, k, m, lo):
        mid = bit_of(self.f, 2) if m is None else m
        return block(self.part, self.place((self.high(k) * 2 + mid) * 2 + lo), self.rows)

    def start(self):
        for k in reversed(range(self.n_hi)):
            for j, m in enumerate(self.mids):
                c = self.links.copy(
                    self.source(k, m, 1 - self.lo),
                    block(self.recv[0], self.slot(0, k, j), self.rows),
                    (flip(self.f, 1), self.t),
                )
                c.start()
                self.copies[0, k, j] = c

    def add(self, level, k, out=None):
        for j, m in enumerate(self.mids):
            self.copies[level, k, j].wait_recv()
            place = self.slot(level, k, j)
            mine = (
                self.source(k, m, self.lo)
                if level == 0
                else block(self.sums[level - 1], self.slot(level - 1, k, j), self.rows)
            )
            total = block(self.sums[level], place, self.rows)
            run_add(mine, block(self.recv[level], place, self.rows), total)
            n = self.n_hi >> (level + 1)
            if n >= 1 and k & n:
                c = self.links.copy(
                    total,
                    block(self.recv[level + 1], self.slot(level + 1, k, j), self.rows),
                    (flip(self.f, self.stages[level + 1]), self.t),
                )
                c.start()
                self.copies[level + 1, k - n, j] = c

    def level(self, level):
        for k in reversed(range(self.n_hi >> level)):
            self.add(level, k)

    @property
    def last(self):
        return len(self.stages) - 1


def scatter_kernel(
    masks, top,
    e, vec, x, ea, xa, upa, qkva, downa, outa, n2, a, dproj, g_qkv, g_out, g, slope, g_down,
    *rest,
):
    n_stage = len(masks)
    (dh, g_up, norm_grad, branch), rest = rest[:4], rest[4:]
    stage_refs = []
    for _ in range(4):
        stage_refs.append((rest[:n_stage], rest[n_stage : 2 * n_stage]))
        rest = rest[2 * n_stage :]
    token_refs = [rest[:4], rest[4:8]]
    (up_new, qkv_new, out_new, small), rest = rest[8:12], rest[12:]
    (send_sem, recv_sem, local_sem, sums, qkv_sum, bias_sum, small_in) = rest
    f = lax.axis_index("fsdp")
    t = lax.axis_index("tp")
    mid = bit_of(f, 2)
    rows, d = x.shape
    fsdp = 2 << len(masks)
    feat = d // fsdp
    sub = g.shape[1] * 2 // fsdp
    orow = 2 * HD // fsdp
    mine = g.shape[1]
    swapped = greet(f, t, masks, top)
    links = Links(send_sem, recv_sem)
    mid_peer, y_peer, core_peer = (flip(f, 2), t), (f, flip(t, 2)), (f, flip(t, 1))
    down_place = lambda i: (i // 4) * 2 + i % 2
    same = lambda i: i
    qkv_s = Scatter(links, g_qkv, same, feat, (0, 1), *stage_refs[0], f, t, masks)
    out_s = Scatter(links, g_out, lambda i: out_place(i, top), orow, (None,), *stage_refs[1], f, t, masks)
    down_s = Scatter(links, g_down, down_place, sub, (None,), *stage_refs[2], f, t, masks)
    up_s = Scatter(links, g_up, same, feat, (0, 1), *stage_refs[3], f, t, masks)

    def exchange_columns(job, dst):
        total = job.sums[-1]
        c = links.copy(block(total, 1 - mid, feat), dst.at[mid], mid_peer)
        c.start()
        k = pltpu.make_async_copy(block(total, mid, feat), dst.at[mid], local_sem.at[0 if job is qkv_s else 1])
        k.start()
        return c, k

    class Tokens:
        def __init__(self, part, refs):
            self.part, (self.got, self.sum, self.got_y, self.final) = part, refs
            self.copies = {}

        def start(self):
            for y in (1, 0):
                for m in (1, 0):
                    yy, mm = (1 - t // 2 if y else t // 2), (1 - mid if m else mid)
                    c = links.copy(
                        block(self.part, mm * 4 + yy * 2 + 1 - t % 2, rows),
                        block(self.got, mm * 2 + yy, rows),
                        core_peer,
                    )
                    c.start()
                    self.copies["c", y, m] = c

        def core(self):
            for y in (1, 0):
                for m in (1, 0):
                    yy, mm = (1 - t // 2 if y else t // 2), (1 - mid if m else mid)
                    self.copies["c", y, m].wait_recv()
                    total = block(self.sum, mm * 2 + yy, rows)
                    run_add(block(self.part, mm * 4 + yy * 2 + t % 2, rows), block(self.got, mm * 2 + yy, rows), total)
                    if y:
                        c = links.copy(total, block(self.got_y, mm, rows), y_peer)
                        c.start()
                        self.copies["y", m] = c

        def across(self):
            self.copies["y", 1].wait_recv()
            self.copies["y", 1].wait_send()
            total = block(self.sum, (1 - mid) * 2 + 1 - t // 2, rows)
            run_add(block(self.sum, (1 - mid) * 2 + t // 2, rows), block(self.got_y, 1 - mid, rows), total)
            self.copies["m"] = links.copy(total, self.final.at[1], mid_peer)
            self.copies["m"].start()
            self.copies["y", 0].wait_recv()
            run_add(block(self.sum, mid * 2 + t // 2, rows), block(self.got_y, mid, rows), self.final.at[0])

        def finish(self):
            self.copies["m"].wait_recv()

        def drain(self):
            for key, c in self.copies.items():
                if key != ("y", 1):
                    c.wait_send()

    norm_t = Tokens(norm_grad, token_refs[0])
    branch_t = Tokens(branch, token_refs[1])

    qkv_s.start()
    out_s.start()
    down_s.start()
    run_hidden_grad(ea, downa, slope, dh, bias_sum)
    qkv_s.level(0)
    out_s.level(0)
    run_outer(n2, dh, g_up)
    up_s.start()
    run_norm_grad(vec, dh, upa, dproj, qkva, xa, norm_grad, sums, qkv_sum)
    norm_t.start()
    down_s.level(0)
    run_branch(a, outa, g, downa, branch)
    norm_t.core()
    branch_t.start()
    small[...] = jnp.zeros_like(small)
    small[0:4, :] = sums[0:4, :]
    small[4:5, :] = jnp.sum(e[...].astype(f32), axis=0, keepdims=True)
    n_heads = d // HD
    for c in range(3):
        for h in range(n_heads):
            small[5 + c : 6 + c, h * HD : (h + 1) * HD] = jnp.where(
                t * 2 + mid == h, qkv_sum[0:1, c * HD : (c + 1) * HD], 0.0
            )
    hi_n = fsdp // 4
    chunk = 2 * sub
    for tt in range(4):
        for hh in range(hi_n):
            for mm in range(2):
                at = (hh * 2 + mm) * chunk
                small[8 + tt : 9 + tt, at : at + chunk] = jnp.where(
                    (t == tt) & (mid == mm), bias_sum[0:1, hh * chunk : (hh + 1) * chunk], 0.0
                )
    small_peers = [core_peer, y_peer, mid_peer] + [(flip(f, m), t) for m in masks]
    small_copies = []

    def small_round(r):
        c = links.copy(small, small_in.at[r], small_peers[r])
        c.start()
        small_copies.append(c)

    def small_add(r):
        small_copies[r].wait()
        small[...] += small_in[r]

    small_round(0)
    branch_t.core()
    small_add(0)
    small_round(1)
    qkv_s.level(1)
    qkv_x = exchange_columns(qkv_s, qkv_new) if n_stage == 2 else None
    small_add(1)
    small_round(2)
    norm_t.across()
    small_add(2)
    small_round(3)
    out_s.level(1)
    down_s.level(1)
    for r in range(3, len(small_peers)):
        small_add(r)
        if r + 1 < len(small_peers):
            small_round(r + 1)
    branch_t.across()
    for level in range(2, n_stage):
        qkv_s.level(level)
        out_s.level(level)
        down_s.level(level)
    if qkv_x is None:
        qkv_x = exchange_columns(qkv_s, qkv_new)
    total = out_s.sums[-1]
    swap_copy = links.copy(total, out_new, (swapped, t))
    own_out = pltpu.make_async_copy(total, out_new, local_sem.at[2])

    @pl.when(swapped != f)
    def _():
        swap_copy.start()

    @pl.when(swapped == f)
    def _():
        own_out.start()

    for level in range(n_stage):
        up_s.level(level)
    up_x = exchange_columns(up_s, up_new)
    norm_t.finish()
    branch_t.finish()
    for c, k in (qkv_x, up_x):
        c.wait_recv()
        c.wait_send()
        k.wait()

    @pl.when(swapped != f)
    def _():
        swap_copy.wait_recv()
        swap_copy.wait_send()

    @pl.when(swapped == f)
    def _():
        own_out.wait()

    for job in (qkv_s, out_s, down_s, up_s):
        for c in job.copies.values():
            c.wait_send()
    norm_t.drain()
    branch_t.drain()


def scatter_all(masks, top, tp, e, vec, x, ea, xa, upa, qkva, downa, outa, n2, a, dproj, g_qkv, g_out, g, slope, g_down):
    rows, d = x.shape
    tokens = 2 * tp * rows
    mine, wide = upa.shape[1], qkva.shape[1]
    fsdp = 2 << len(masks)
    feat, sub, orow = d // fsdp, 2 * mine // fsdp, 2 * HD // fsdp
    hi_n = fsdp // 4
    shapes = [(tokens, mine), (d, mine), (tokens, d), (tokens, d)]
    copies = 0
    for height, width, mids in ((feat, wide, 2), (orow, d, 1), (sub, d, 1), (feat, mine, 2)):
        for _ in range(2):
            for level in range(len(masks)):
                n = max(hi_n >> level, 1)
                shapes.append((n * mids * height, width))
        copies += (2 * hi_n - 1) * mids + 1
    for _ in range(2):
        shapes += [(4 * rows, d), (4 * rows, d), (2 * rows, d), (2, rows, d)]
        copies += 7
    shapes += [(2, feat, mine), (2, feat, wide), (orow, d)]
    n_small = len(masks) + 3
    out_shape = [jax.ShapeDtypeStruct(shape, bf16) for shape in shapes]
    out_shape.append(jax.ShapeDtypeStruct((16, d), f32))
    result = pl.pallas_call(
        functools.partial(scatter_kernel, masks, top),
        out_shape=out_shape,
        in_specs=[VMEM, VMEM] + [ANY] * 15,
        out_specs=[ANY] * len(shapes) + [VMEM],
        scratch_shapes=[
            pltpu.SemaphoreType.DMA((copies + n_small,)),
            pltpu.SemaphoreType.DMA((copies + n_small,)),
            pltpu.SemaphoreType.DMA((3,)),
            pltpu.VMEM((8, d), f32),
            pltpu.VMEM((8, wide), f32),
            pltpu.VMEM((8, mine), f32),
            pltpu.VMEM((n_small, 16, d), f32),
        ],
        compiler_params=pltpu.CompilerParams(
            collective_id=1, has_side_effects=True, vmem_limit_bytes=56 * 2**20
        ),
        name="scatter_all",
    )(e, vec, x, ea, xa, upa, qkva, downa, outa, n2, a, dproj, g_qkv, g_out, g, slope, g_down)
    stage = len(masks)
    down_new = result[4 + 2 * stage * 3 - 1]
    at = 4 + 2 * stage * 4
    norm_final, branch_final = result[at + 3], result[at + 7]
    up_new, qkv_new, out_new, small = result[at + 8 : at + 12]
    return norm_final, branch_final, up_new, qkv_new, out_new, down_new, small


def make_local(fsdp, tp):
    lo_n = 2
    hi_n = fsdp // 4
    masks = [1 << b for b in range(2, fsdp.bit_length() - 1)] + [1]
    top = fsdp // 2

    def local(
        layer_input,
        out_cotangent,
        segments,
        qkv_weight,
        qkv_first,
        qkv_second,
        out_weight,
        out_first,
        out_second,
        up_weight,
        up_first,
        up_second,
        down_weight,
        down_first,
        down_second,
        small_params,
        small_first,
        small_second,
    ):
        f = lax.axis_index("fsdp")
        t = lax.axis_index("tp")
        mid = (f // 2) % 2
        rows, d = layer_input.shape
        length = segments.shape[1]
        width = qkv_weight.shape[3]
        hidden = up_weight.shape[2]
        sub = hidden // fsdp
        feat = d // fsdp
        mine = hidden // 2
        vector = small_params[0]

        up16 = up_weight[0].astype(bf16).reshape(feat, hi_n, 2, lo_n * sub)
        up16 = up16.transpose(2, 0, 1, 3).reshape(2, feat, mine)
        qkv16 = qkv_weight[0].astype(bf16).reshape(3, feat, 2, HD)
        qkv16 = qkv16.transpose(2, 1, 0, 3).reshape(2, feat, 3 * HD)
        down16 = down_weight[0].astype(bf16)
        out16 = out_weight[0].astype(bf16)

        own_bounds = jnp.stack([jnp.sum(segments[0] < 1), jnp.sum(segments[0] < 2)]).astype(f32)
        other_bounds = lax.ppermute(own_bounds, "fsdp", [(i, i ^ 2) for i in range(fsdp)])
        bounds = jnp.where(
            mid == 0, jnp.stack([own_bounds, other_bounds]), jnp.stack([other_bounds, own_bounds])
        ).astype(jnp.int32)
        index = jnp.arange(length, dtype=jnp.int32)[None]
        first, second = bounds[:, 0:1], bounds[:, 1:2]
        start = jnp.where(index >= second, second, jnp.where(index >= first, first, 0))
        position = (index - start).astype(f32).reshape(2 * length, 1)
        half = ROT // 2
        lane = jnp.arange(128)
        frequency = 10000.0 ** (-(2 * (lane % half)).astype(f32) / ROT)
        angle = position * frequency[None]
        cosine = jnp.where(lane < ROT, jnp.cos(angle), 1.0)
        sine = jnp.where(lane < ROT, jnp.where(lane < half, -1.0, 1.0) * jnp.sin(angle), 0.0)

        norms = vector[0 : 4 * d].reshape(4, d)
        vec = jnp.concatenate([norms, jnp.zeros((4, d), f32)])
        qkv_bias = lax.dynamic_slice_in_dim(
            vector[6 * d : 9 * d].reshape(3, d), t * width + mid * HD, HD, 1
        ).reshape(1, 3 * HD)
        up_bias = lax.dynamic_slice(
            vector[9 * d :].reshape(tp, hi_n, 2, lo_n * sub), (t, 0, mid, 0), (1, hi_n, 1, lo_n * sub)
        ).reshape(1, mine)

        (
            x_all, e_all, up_full, qkv_full, down_full, out_full,
            n1, n2, p, da, a, dproj, g_qkv, g_out, g, slope, g_down,
        ) = gather_all(
            masks, top, length, tp, layer_input, out_cotangent, up16, qkv16, down16, out16,
            cosine, sine, vec, qkv_bias, up_bias, bounds,
        )
        norm_final, branch_final, up_new, qkv_new, out_new, down_new, small = scatter_all(
            masks, top, tp, out_cotangent, vec, layer_input, e_all, x_all, up_full, qkv_full, down_full,
            out_full, n2, a, dproj, g_qkv, g_out, g, slope, g_down,
        )

        stream = layer_input.astype(f32)
        bias = vector[4 * d : 5 * d] + vector[5 * d : 6 * d]
        layer_output = stream + (branch_final[0].astype(f32) + branch_final[1].astype(f32)) + bias
        scaled = norm_final[0].astype(f32) + norm_final[1].astype(f32)
        centred = stream - jnp.mean(stream, axis=-1, keepdims=True)
        inverse = lax.rsqrt(jnp.mean(centred * centred, axis=-1, keepdims=True) + norm_eps)
        normal = centred * inverse
        input_grad = out_cotangent.astype(f32) + inverse * (
            scaled
            - jnp.mean(scaled, axis=-1, keepdims=True)
            - normal * jnp.mean(scaled * normal, axis=-1, keepdims=True)
        )
        qkv_total = qkv_new.reshape(2, feat, 3, HD).transpose(2, 1, 0, 3).reshape(1, 3, feat, width)
        up_total = up_new.reshape(2, feat, hi_n, lo_n * sub).transpose(1, 2, 0, 3).reshape(1, feat, hidden)
        small_total = jnp.concatenate(
            [small[0:5].reshape(-1), small[4:5].reshape(-1), small[5:12].reshape(-1)]
        )[None]
        rate_matrix = d ** (-0.5)
        rate_output = 4.0 * d ** (-0.5)
        results = [layer_output, input_grad]
        for weight, first, second, grad, rate, decay in (
            (qkv_weight, qkv_first, qkv_second, qkv_total, rate_matrix, decay_rate),
            (out_weight, out_first, out_second, out_new[None], rate_output, decay_rate),
            (up_weight, up_first, up_second, up_total, rate_matrix, decay_rate),
            (down_weight, down_first, down_second, down_new[None], rate_matrix, decay_rate),
            (small_params, small_first, small_second, small_total, rate_vector, 0.0),
        ):
            results.extend(adam_step(weight, first, second, grad.astype(f32), rate, decay))
        return tuple(results)

    return local


def solution(mesh):
    tokens = P(("fsdp", "tp"), None)
    inner = P(None, ("tp", "fsdp"), None)
    qkv = P(None, None, "fsdp", "tp")
    up = P(None, "fsdp", "tp")
    weights = (qkv,) * 3 + (inner,) * 3 + (up,) * 3 + (inner,) * 3 + (P(),) * 3
    return jax.shard_map(
        make_local(mesh.shape["fsdp"], mesh.shape["tp"]),
        mesh=mesh,
        in_specs=(tokens, tokens, P("fsdp", None)) + weights,
        out_specs=(tokens, tokens) + weights,
        check_vma=False,
    )
```

time: 762 us -> 694 us (0.911)
  Pallas kernels: 189 us -> 601 us
  matrix products: 164 us -> 0 us
  waiting for transfers between devices: 140 us -> 0.01 us
  local copies, waits for them, and re-layouts: 152 us -> 42.6 us
  other arithmetic: 81.7 us -> 36.9 us
  starting transfers between devices: 21.6 us -> 0.45 us
    pallas_call x1 -> x2, Pallas kernels: 189 us -> 601 us  [the longest x1 337 us: scatter_all(): pl.pallas_call(functools.partial(scatter_kernel, masks, top), out_shape=o...]
    dot_general x18 -> x0, matrix products: 164 us -> none  [the longest x12 151 us: dot(): return lax.dot_general(a, b, (dims, ((), ())), preferred_element_type=out)]
    ppermute x23 -> x1, waiting for transfers between devices: 140 us -> 0.01 us  [local(): lax.ppermute(own_bounds, 'fsdp', [(i, i ^ 2) for i in range(fsdp)])]
    convert_element_type x18 -> x4, other arithmetic: 34.7 us -> 2.76 us  [the longest x2 2.74 us: local(): jnp.stack([jnp.sum(segments[0] < 1), jnp.sum(segments[0] < 2)]).astype(f32)]
    dot_general x3 -> x0, local copies, waits for them, and re-layouts: 26.1 us -> none  [dot(): return lax.dot_general(a, b, (dims, ((), ())), preferred_element_type=out)]
    ppermute x23 -> x1, starting transfers between devices: 21.6 us -> 0.45 us  [local(): lax.ppermute(own_bounds, 'fsdp', [(i, i ^ 2) for i in range(fsdp)])]
    dynamic_slice x10 -> x1, local copies, waits for them, and re-layouts: 19.2 us -> 0.6 us  [local(): lax.dynamic_slice(vector[9 * d:].reshape(tp, hi_n, 2, lo_n * sub), (t, 0,...]
    squeeze x13 -> x0, local copies, waits for them, and re-layouts: 16.5 us -> none  [the longest x12 14 us: pick(): return lax.dynamic_index_in_dim(v, index, axis, keepdims=False)]
  transfers between devices with their start and end apart: 23 -> 1, of which waited for: 9 -> 0; matrix products, arithmetic and copies ran while one was open for 51% -> 4% of each run, Pallas kernels for 25% -> 0%
where the time goes in v3:
time: 694 us; the launch traced here: 683 us
  Pallas kernels  601 us (87%)
  local copies, waits for them, and re-layouts  42.6 us (6%)
  other arithmetic  36.9 us (5%)
    pallas_call x1, Pallas kernels, scatter_all(): pl.pallas_call(functools.partial(scatter_kernel, masks, top), out_shape=o...  337 us
    pallas_call x1, Pallas kernels, gather_all(): pl.pallas_call(functools.partial(gather_kernel, masks, top, length), out_...  265 us
    unnamed x62, local copies, waits for them, and re-layouts  20.3 us
    sub x5, other arithmetic, adam_step(): weight - rate * (first_hat / (jnp.sqrt(second_hat) + adam_eps) + decay *...  16.1 us
  transfers between devices with their start and end apart: 1, of which 0 were waited for; matrix products, arithmetic and copies ran while one was open for 4% of the time, Pallas kernels for 0%

profile of v3, /device:TPU:30, one launch (start us, length us, event | category | flops | bytes accessed | tf_op | source)
XLA Modules:
  0.0 682.5 jit_solution(17161393256601964750)
XLA Ops:
  0.7 1.3 fusion.28
  2.0 1.4 add_convert_fusion.1
  3.9 0.9 slice_reduce_fusion
  7.0 1.9 copy.46
  9.0 1.2 copy.49.qkv
  10.2 1.7 convert_element_type.140
  11.9 1.6 convert_element_type.141
  13.5 2.0 copy.71
  15.6 1.5 reshape.405.up
  17.1 2.9 convert_bitcast_fusion.down
  20.7 1.6 copy.50
  22.3 3.1 copy.53
  26.1 1.4 add_convert_fusion
  29.0 5.6 fusion.20
  34.6 264.8 %gather_and_attend.1 = (bf16[2048,2048]{1,0:T(8,128)(2,1)}, bf16[2048,2048]{1,0:T(8,128)(2,1)}, bf16[2048,1024]{1,0:T(8,128)(2,1)}, bf16[2048,768]{1,0:T(8,128)(...) custom-call(bf16[256,2048]{1,0:T(8,128)(2,1)} %x.5, ...), custom_call_target="tpu_custom_call" | custom-call | tf_op jit(solution)/shard_map/gather_and_attend/pallas_call | solution.py:516
  299.4 336.6 %scatter_all.1 = (bf16[2048,1024]{1,0:T(8,128)(2,1)}, bf16[2048,1024]{1,0:T(8,128)(2,1)}, bf16[2048,2048]{1,0:T(8,128)(2,1)}, bf16[2048,2048]{1,0:T(8,128)(2,1)}...) custom-call(bf16[256,2048]{1,0:T(8,128)(2,1)} %e.3, ...), custom_call_target="tpu_custom_call" | custom-call | tf_op jit(solution)/shard_map/scatter_all/pallas_call | solution.py:822
  638.7 1.4 copy.51
  640.3 1.3 copy-done.7
  642.0 2.8 multiply_subtract_fusion.2
  644.9 3.1 copy.57
  648.0 1.6 copy.58
  649.6 1.6 copy.59
  651.2 3.1 reshape.414
  654.4 2.9 copy.56
  657.3 4.3 reshape.412
  663.5 1.1 copy-done.4
  664.6 6.4 multiply_subtract_fusion.1
  671.1 3.9 multiply_subtract_fusion
  675.0 1.4 multiply_subtract_fusion.3
  676.4 1.0 copy-done.14
  677.5 3.4 fusion.7
  680.8 1.5 multiply_subtract_fusion.4
  (80 shorter events, 11.0 us)
Async XLA Ops:
  3.4 25.3 %collective-permute-start = (f32[2]{0:T(128)S(1)}, f32[2]{0:T(128)S(1)}, u32[]{:S(2)}, u32[]{:S(2)}) collective-permute-start(f32[2]{0:T(128)S(1)} %add_convert_fusion.1), channel_id=1, source_target_pairs={{0,8},{4,12},{8,0},{12,4},{16,24},{20,28},{24,16},{28,20},{1,9},{5... | collective-permute-start | bytes 32 | tf_op jit(solution)/shard_map/ppermute | solution.py:895
  17.1 2.9 copy-start.10
  17.1 3.6 copy-start.15
  22.3 3.1 copy-start
  28.7 5.9 copy-start.23
  640.2 1.4 copy-start.7
  640.2 1.9 copy-start.8
  644.9 3.1 copy-start.9
  657.3 4.3 copy-start.2
  661.6 1.2 copy-start.1
  661.6 1.9 copy-start.5
  662.8 1.7 copy-start.4
  664.6 6.4 copy-start.6
  664.6 6.4 copy-start.12
  664.6 6.4 copy-start.13
  664.6 6.4 copy-start.16
  671.0 4.0 copy-start.11
  671.0 4.0 copy-start.17
  671.0 3.9 copy-start.18
  671.0 3.9 copy-start.20
  675.0 1.5 copy-start.3
  675.0 2.5 copy-start.14
  677.5 3.4 copy-start.19
  677.5 3.4 copy-start.21
  677.5 3.4 copy-start.22

commit v4 on v1

v4 whole, which is shorter than its diff:
```python
import functools

import jax
import jax.numpy as jnp
from jax import lax
from jax.experimental import pallas as pl
from jax.experimental.pallas import tpu as pltpu
from jax.sharding import PartitionSpec as P

HD = 256
ROT = 64
STEP = 10

norm_eps = 1e-05
beta_one = 0.9
beta_two = 0.95
adam_eps = 1e-08
decay_rate = 0.01
rate_vector = 0.2
masked_score = -1e30
f32 = jnp.float32
bf16 = jnp.bfloat16


def adam_step(weight, first, second, grad, rate, decay):
    first_new = beta_one * first + (1.0 - beta_one) * grad
    second_new = beta_two * second + (1.0 - beta_two) * grad * grad
    first_hat = first_new / (1.0 - beta_one**STEP)
    second_hat = second_new / (1.0 - beta_two**STEP)
    weight_new = weight - rate * (first_hat / (jnp.sqrt(second_hat) + adam_eps) + decay * weight)
    return (first_new, second_new, weight_new)


MESH = pl.DeviceIdType.MESH


def bit_of(i, mask):
    return (i // mask) % 2


def flip(i, mask):
    return i + mask - 2 * mask * bit_of(i, mask)


class Links:
    def __init__(self, send_sem, recv_sem):
        self.send_sem, self.recv_sem, self.count, self.started = send_sem, recv_sem, 0, []

    def copy(self, src, dst, device):
        k = self.count
        self.count += 1
        c = pltpu.make_async_remote_copy(
            src_ref=src,
            dst_ref=dst,
            send_sem=self.send_sem.at[k],
            recv_sem=self.recv_sem.at[k],
            device_id=device,
            device_id_type=MESH,
        )
        self.started.append(c)
        return c


class Group:
    def __init__(self, links, at, f, t, masks, root, own=None):
        self.copies, self.masks = {}, masks
        for key in all_keys(masks):
            g = root
            for mask in masks:
                if key & mask:
                    g = flip(g, mask)
            ref = at(g)
            for mask in self.later(key):
                src = own if key == 0 and own is not None else ref
                self.copies[key | mask] = links.copy(src, ref, (flip(f, mask), t))

    def later(self, key):
        after = max([i + 1 for i, m in enumerate(self.masks) if key & m], default=0)
        return self.masks[after:]

    def send(self, key, mask):
        self.copies[key | mask].start()

    def send_all(self, key):
        for mask in self.later(key):
            self.send(key, mask)

    def wait(self, key):
        self.copies[key].wait_recv()

    def arrive(self, key):
        self.wait(key)
        self.send_all(key)


def all_keys(masks):
    keys = [0]
    for mask in masks:
        keys = keys + [k | mask for k in keys]
    return keys


def normalise(x):
    mean = jnp.mean(x, axis=-1, keepdims=True)
    centred = x - mean
    inverse = lax.rsqrt(jnp.mean(centred * centred, axis=-1, keepdims=True) + norm_eps)
    return centred * inverse


def rope(u, c, s):
    lane = lax.broadcasted_iota(jnp.int32, u.shape, 1)
    partner = jnp.where(lane < ROT // 2, pltpu.roll(u, 128 - ROT // 2, 1), pltpu.roll(u, ROT // 2, 1))
    return u * c + partner * s


def dot(a, b, dims):
    return lax.dot_general(a, b, (dims, ((), ())), preferred_element_type=f32)


NN = ((1,), (0,))
NT = ((1,), (1,))
TN = ((0,), (0,))
TILE = 256


def pipe(body, steps, ins, outs, hooks=()):
    hooks = list(hooks)

    def whole(*refs):
        for i, hook in enumerate(hooks):
            pl.when(pl.program_id(0) == i * steps // len(hooks))(hook)
        body(*refs)

    pltpu.emit_pipeline(
        whole,
        grid=(steps,),
        in_specs=[spec for _, spec in ins],
        out_specs=[spec for _, spec in outs],
    )(*[ref for ref, _ in ins], *[ref for ref, _ in outs])


def by_rows(ref, index=lambda i: i, rows=TILE):
    return ref, pl.BlockSpec((rows, ref.shape[1]), lambda i: (index(i), 0))


def by_columns(ref, index, width):
    return ref, pl.BlockSpec((ref.shape[0], width), lambda i: (0, index(i)))


def here(i, rows=TILE):
    return pl.ds(pl.multiple_of(i * rows, rows), rows)


def run_norms(vec, x, n1, n2, index, steps, hooks=()):
    def body(x_ref, one_ref, two_ref):
        normal = normalise(x_ref[...].astype(f32))
        one_ref[...] = (normal * vec[0:1, :] + vec[1:2, :]).astype(bf16)
        two_ref[...] = (normal * vec[2:3, :] + vec[3:4, :]).astype(bf16)

    pipe(body, steps, [by_rows(x, index)], [by_rows(n1, index), by_rows(n2, index)], hooks)


def run_project(qkv_bias, n1, w, c, s, p, hooks=()):
    def body(n_ref, c_ref, s_ref):
        at = here(pl.program_id(0))
        proj = dot(n_ref[...], w[...], NN) + qkv_bias[...]
        for j in range(2):
            p[at, j * HD : j * HD + 128] = rope(proj[:, j * HD : j * HD + 128], c_ref[...], s_ref[...]).astype(bf16)
            p[at, j * HD + 128 : (j + 1) * HD] = proj[:, j * HD + 128 : (j + 1) * HD].astype(bf16)
        p[at, 2 * HD :] = proj[:, 2 * HD :].astype(bf16)

    pipe(body, n1.shape[0] // TILE, [by_rows(n1), by_rows(c), by_rows(s)], [], hooks)


def run_up(up_bias, n2, w, g, slope, hooks=()):
    width = w.shape[1]
    part = min(width, 256)

    def body(n_ref, g_ref, s_ref):
        n = n_ref[...]
        for j in range(0, width, part):
            h = dot(n, w[:, j : j + part], NN) + up_bias[:, j : j + part]
            cdf = 0.5 + 0.5 * lax.erf(h * 0.7071067811865476)
            g_ref[:, j : j + part] = (h * cdf).astype(bf16)
            s_ref[:, j : j + part] = (cdf + h * (jnp.exp(-0.5 * h * h) * 0.3989422804014327)).astype(bf16)

    pipe(body, n2.shape[0] // TILE, [by_rows(n2)], [by_rows(g), by_rows(slope)], hooks)


def run_attention(length, seq, bounds, p, da, c, s, a, dproj, dk, dv):
    scale = HD ** (-0.5)
    base = seq * length
    first, second = bounds[seq, 0], bounds[seq, 1]

    def put(at, value, column):
        dproj[at, column : column + 128] = rope(value[:, :128], c[at, :], -s[at, :]).astype(bf16)
        dproj[at, column + 128 : column + HD] = value[:, 128:].astype(bf16)

    dk[...] = jnp.zeros_like(dk)
    dv[...] = jnp.zeros_like(dv)
    for i in range(length // TILE):
        at = slice(base + i * TILE, base + (i + 1) * TILE)
        n = (i + 1) * TILE
        q = p[at, 0:HD]
        k = p[base : base + n, HD : 2 * HD]
        v = p[base : base + n, 2 * HD :]
        rows_da = da[at, :]
        scores = dot(q, k, NT) * scale
        qi = i * TILE + lax.broadcasted_iota(jnp.int32, (TILE, n), 0)
        ki = lax.broadcasted_iota(jnp.int32, (TILE, n), 1)
        start = jnp.where(qi >= second, second, jnp.where(qi >= first, first, 0))
        scores = jnp.where((ki <= qi) & (ki >= start), scores, masked_score)
        peak = jnp.max(scores, axis=-1, keepdims=True)
        raised = jnp.exp(scores - peak)
        probs = raised * (1.0 / jnp.sum(raised, axis=-1, keepdims=True))
        weights = probs.astype(bf16)
        a[at, :] = dot(weights, v, NN).astype(bf16)
        prob_grad = dot(rows_da, v, NT)
        delta = jnp.sum(probs * prob_grad, axis=-1, keepdims=True)
        score_grad = (probs * (prob_grad - delta)).astype(bf16)
        put(at, dot(score_grad, k, NN) * scale, 0)
        dk[0:n, :] += dot(score_grad, q, TN)
        dv[0:n, :] += dot(weights, rows_da, TN)
    for i in range(length // TILE):
        at = slice(base + i * TILE, base + (i + 1) * TILE)
        local = slice(i * TILE, (i + 1) * TILE)
        put(at, dk[local, :] * scale, HD)
        dproj[at, 2 * HD :] = dv[local, :].astype(bf16)


def run_outer(a, b, out, index_in, index_out, steps, width, add=None, hooks=()):
    def body(*refs):
        value = dot(refs[0][...], b[...], TN)
        if add is not None:
            value = value + refs[1][...].astype(f32)
        refs[-1][...] = value.astype(bf16)

    ins = [by_columns(a, index_in, width)]
    if add is not None:
        ins.append(by_rows(add, index_out, width))
    pipe(body, steps, ins, [by_rows(out, index_out, width)], hooks)


def run_outer_wide(a, b, out):
    width = 2 * TILE

    def body(out_ref):
        at = pl.ds(pl.multiple_of(pl.program_id(0) * width, width), width)
        out_ref[...] = dot(a[...], b[:, at], TN).astype(bf16)

    pipe(body, b.shape[1] // width, [], [by_columns(out, lambda i: i, width)])


def run_hidden_grad(e, w, slope, dh, bias_sum, hooks=()):
    bias_sum[...] = jnp.zeros_like(bias_sum)

    def body(s_ref):
        at = here(pl.program_id(0))
        value = (dot(e[at, :], w[...], NT) * s_ref[...].astype(f32)).astype(bf16)
        dh[at, :] = value
        bias_sum[0:1, :] += jnp.sum(value.astype(f32), axis=0, keepdims=True)

    pipe(body, e.shape[0] // TILE, [by_rows(slope)], [], hooks)


def run_norm_grad(vec, dh, w_up, dproj, w_qkv, x, sums, qkv_sum):
    sums[...] = jnp.zeros_like(sums)
    qkv_sum[...] = jnp.zeros_like(qkv_sum)

    def tile(at, x_ref):
        normal = normalise(x_ref[...].astype(f32))
        rows = dproj[at, :]
        one = dot(rows, w_qkv[...], NT)
        two = dot(dh[at, :], w_up[...], NT)
        for j, value in ((0, one * normal), (1, one), (2, two * normal), (3, two)):
            sums[j : j + 1, :] += jnp.sum(value, axis=0, keepdims=True)
        qkv_sum[0:1, :] += jnp.sum(rows.astype(f32), axis=0, keepdims=True)
        return one * vec[0:1, :] + two * vec[2:3, :]

    return x, tile


def run_branch(a, w_out, g, w_down):
    def tile(at, g_ref):
        return dot(a[at, :], w_out[...], NN) + dot(g_ref[...], w_down[...], NN)

    return g, tile


def run_token_tiles(job, out, index, index_out, steps, add=None, hooks=()):
    source, tile = job

    def body(*refs):
        value = tile(here(index(pl.program_id(0))), refs[0])
        if add is not None:
            value = value + refs[1][...].astype(f32)
        refs[-1][...] = value.astype(bf16)

    ins = [by_rows(source, index)]
    if add is not None:
        ins.append(by_rows(add, index_out))
    pipe(body, steps, ins, [by_rows(out, index_out)], hooks)


def run_add(a, b, out):
    rows, cols = out.shape
    step = min(rows, TILE)

    def body(a_ref, b_ref, out_ref):
        out_ref[...] = (a_ref[...].astype(f32) + b_ref[...].astype(f32)).astype(bf16)

    pipe(body, rows // step, [by_rows(a, rows=step), by_rows(b, rows=step)], [by_rows(out, rows=step)])


def block(ref, index, rows):
    return ref.at[pl.ds(pl.multiple_of(index * rows, rows), rows)]


def out_place(g, top):
    return (((g // 4) % (top // 4)) * 2 + g // top) * 2 + g % 2


class Scatter:
    def __init__(self, links, part, place, rows, mids, recv, sums, f, t, masks):
        self.links, self.part, self.place, self.rows, self.mids = links, part, place, rows, mids
        self.recv, self.sums, self.f, self.t = recv, sums, f, t
        self.stages = [1] + [m for m in reversed(masks) if m != 1]
        self.n_hi = 1 << (len(masks) - 1)
        self.hi, self.lo, self.mid = f // 4, f % 2, bit_of(f, 2)
        self.copies = {}
        for k in range(self.n_hi):
            for j, m in enumerate(mids):
                self.copies[0, k, j] = links.copy(
                    block(part, self.at_place(self.high(k), m, 1 - self.lo), rows),
                    block(recv[0], self.slot(0, k, j), rows),
                    (flip(f, 1), t),
                )
        for level in range(len(self.stages) - 1):
            n = self.n_hi >> (level + 1)
            for k in range(n, 2 * n):
                for j in range(len(mids)):
                    self.copies[level + 1, k - n, j] = links.copy(
                        block(sums[level], self.slot(level, k, j), rows),
                        block(recv[level + 1], self.slot(level + 1, k, j), rows),
                        (flip(f, self.stages[level + 1]), t),
                    )

    def high(self, k):
        hi, b = self.hi, 1
        while b < self.n_hi:
            if k & b:
                hi = flip(hi, b)
            b *= 2
        return hi

    def slot(self, level, k, j):
        n = self.n_hi >> level
        i = (self.high(k) % n) if n > 1 else 0
        return i * len(self.mids) + j

    def at_place(self, hi, m, lo):
        return self.place((hi * 2 + (self.mid if m is None else m)) * 2 + lo)

    def ks(self, far):
        half = self.n_hi // 2
        return range(half, self.n_hi) if far else range(half)

    def each(self, far):
        return [(k, j) for k in self.ks(far) for j in range(len(self.mids))]

    def send(self, far):
        for k, j in self.each(far):
            self.copies[0, k, j].start()

    def got(self, far):
        for k, j in self.each(far):
            self.copies[0, k, j].wait_recv()

    def send_on(self):
        half = self.n_hi // 2
        for k, j in self.each(True):
            self.copies[1, k - half, j].start()

    def tile(self, i, far, lo):
        n = len(self.mids)
        half = self.n_hi // 2
        upper = self.hi // half
        hi = (1 - upper if far else upper) * half + i // n
        j = i % n
        m = None if self.mids[0] is None else j
        return self.at_place(hi, m, lo), hi * n + j

    def add(self, level, k, j):
        mine = (
            block(self.part, self.at_place(self.high(k), self.mids[j], self.lo), self.rows)
            if level == 0
            else block(self.sums[level - 1], self.slot(level - 1, k, j), self.rows)
        )
        at = self.slot(level, k, j)
        run_add(mine, block(self.recv[level], at, self.rows), block(self.sums[level], at, self.rows))

    def first_adds(self, far):
        for k, j in self.each(far):
            self.add(0, k, j)

    def finish(self):
        for level in range(1, len(self.stages)):
            n = self.n_hi >> level
            for k in reversed(range(n)):
                for j in range(len(self.mids)):
                    self.copies[level, k, j].wait_recv()
                    self.add(level, k, j)
                    if level + 1 < len(self.stages) and k & (n // 2):
                        self.copies[level + 1, k - n // 2, j].start()


class Outer:
    def __init__(self, scatter, a, b):
        self.s, self.a, self.b = scatter, a, b
        self.fused = scatter.rows % 128 == 0
        self.steps = scatter.n_hi // 2 * len(scatter.mids)

    def give(self, far, hooks=()):
        s = self.s
        if self.fused:
            at = lambda i: s.tile(i, far, 1 - s.lo)[0]
            run_outer(self.a, self.b, s.part, at, at, self.steps, s.rows, hooks=hooks)
        elif far:
            run_outer(self.a, self.b, s.part, lambda i: i, lambda i: i, self.a.shape[1] // 128, 128, hooks=hooks)

    def keep(self, far, hooks=()):
        s = self.s
        s.got(far)
        if self.fused:
            at = lambda i: s.tile(i, far, s.lo)[0]
            to = lambda i: s.tile(i, far, s.lo)[1]
            run_outer(self.a, self.b, s.sums[0], at, to, self.steps, s.rows, add=s.recv[0], hooks=hooks)
        else:
            for hook in hooks:
                hook()
            s.first_adds(far)


class Tokens:
    def __init__(self, links, refs, rows, f, t):
        self.give_buf, self.got, self.sum, self.got_y, self.sum_y, self.final = refs
        self.rows, self.mid, self.y, self.core = rows, bit_of(f, 2), t // 2, t % 2
        core_peer, y_peer, mid_peer = (f, flip(t, 1)), (f, flip(t, 2)), (flip(f, 2), t)
        self.copies = {}
        for i in range(4):
            self.copies["c", i] = links.copy(block(self.give_buf, i, rows), block(self.got, i, rows), core_peer)
        for m in range(2):
            self.copies["y", m] = links.copy(
                block(self.sum, m * 2 + 1 - self.y, rows), block(self.got_y, m, rows), y_peer
            )
        self.copies["m"] = links.copy(block(self.sum_y, 1 - self.mid, rows), self.final.at[1], mid_peer)

    def give(self, job, hooks=()):
        index = lambda i: (i // 2) * 4 + (i % 2) * 2 + 1 - self.core
        run_token_tiles(job, self.give_buf, index, lambda i: i, 4, hooks=hooks)
        for i in range(4):
            self.copies["c", i].start()

    def keep(self, job, far, hooks=()):
        yy = 1 - self.y if far else self.y
        index = lambda i: i * 4 + yy * 2 + self.core
        if far:
            for i in range(4):
                self.copies["c", i].wait_recv()
        run_token_tiles(job, self.sum, index, lambda i: i * 2 + yy, 2, add=self.got, hooks=hooks)
        if far:
            for m in range(2):
                self.copies["y", m].start()

    def across(self):
        for m in range(2):
            self.copies["y", m].wait_recv()
        for m, to, send in (
            (1 - self.mid, block(self.sum_y, 1 - self.mid, self.rows), True),
            (self.mid, self.final.at[0], False),
        ):
            run_add(block(self.sum, m * 2 + self.y, self.rows), block(self.got_y, m, self.rows), to)
            if send:
                self.copies["m"].start()

    def finish(self):
        self.copies["m"].wait_recv()


def greet(f, t, masks, top):
    mid = bit_of(f, 2)
    swapped = f + (top - 2) * (mid - bit_of(f, top))
    barrier = pltpu.get_barrier_semaphore()
    peers = [(flip(f, m), t) for m in masks + [2]] + [(f, flip(t, 1)), (f, flip(t, 2))]
    for peer in peers:
        pl.semaphore_signal(barrier, inc=1, device_id=peer, device_id_type=MESH)

    @pl.when(swapped != f)
    def _():
        pl.semaphore_signal(barrier, inc=1, device_id=(swapped, t), device_id_type=MESH)

    pl.semaphore_wait(barrier, len(peers) + (mid + bit_of(f, top)) % 2)
    return swapped


class Swap:
    def __init__(self, links, src, dst, stay, f, t, swapped, sem):
        self.move = links.copy(src, dst, (swapped, t))
        links.started = [c for c in links.started if c is not self.move]
        self.copy = pltpu.make_async_copy(src, stay, sem)
        self.moves, self.stays = swapped != f, swapped == f

    def start(self):
        pl.when(self.moves)(self.move.start)
        pl.when(self.stays)(self.copy.start)

    def wait(self):
        pl.when(self.moves)(self.move.wait_recv)
        pl.when(self.stays)(self.copy.wait)

    def drain(self):
        pl.when(self.moves)(self.move.wait_send)


N_HBM = 9


def layer_kernel(
    masks, top, length,
    x, e, up, qkv, down, out, cos, sin, e_own, vec, qkv_bias, up_bias, bounds,
    *rest,
):
    n_stage = len(masks)
    (xa, n1, n2, g, slope, g_qkv, g_out, g_down, g_up), rest = rest[:N_HBM], rest[N_HBM:]
    stage_refs = []
    for _ in range(4):
        stage_refs.append((rest[:n_stage], rest[n_stage : 2 * n_stage]))
        rest = rest[2 * n_stage :]
    token_refs, rest = [rest[:6], rest[6:12]], rest[12:]
    (up_new, qkv_new, out_new, small), rest = rest[:4], rest[4:]
    (
        ea, upa, qkva, downa, outa, p, da, a, dproj, dh, dk, dv, sums, qkv_sum, bias_sum, small_in,
        send_sem, recv_sem, local_sem,
    ) = rest
    f = lax.axis_index("fsdp")
    t = lax.axis_index("tp")
    mid = bit_of(f, 2)
    rows, d = x.shape
    feat, sub, orow = up.shape[1], down.shape[0], out.shape[0]
    mine = up.shape[2]
    swapped = greet(f, t, masks, top)
    links = Links(send_sem, recv_sem)
    own = []

    def local_copy(src, dst):
        c = pltpu.make_async_copy(src, dst, local_sem.at[len(own)])
        own.append(c)
        return c

    mid_peer, y_peer, core_peer = (flip(f, 2), t), (f, flip(t, 2)), (f, flip(t, 1))
    qkv_block = lambda i: block(qkva, i, feat)
    up_block = lambda i: block(upa, i, feat)
    half_sub = sub // 2
    down_blocks = [
        lambda i, h=h: block(downa, ((i // 4) * 2 + i % 2) * 2 + h, half_sub) for h in range(2)
    ]
    out_block = lambda i: block(outa, out_place(i, top), orow)
    tok = lambda buf, m, j: block(buf, m * 4 + j, rows)

    first_up = links.copy(up.at[1 - mid], up_block(f), mid_peer)
    first_qkv = links.copy(qkv.at[1 - mid], qkv_block(f), mid_peer)
    up_own = Group(links, up_block, f, t, masks, f, up.at[mid])
    up_mid = Group(links, up_block, f, t, masks, flip(f, 2))
    qkv_own = Group(links, qkv_block, f, t, masks, f, qkv.at[mid])
    qkv_mid = Group(links, qkv_block, f, t, masks, flip(f, 2))
    out_own = Group(links, out_block, f, t, masks, f)
    down_own = [
        Group(links, down_blocks[h], f, t, masks, f, down.at[pl.ds(h * half_sub, half_sub)]) for h in range(2)
    ]
    out_in = Swap(links, out, out_block(swapped), out_block(f), f, t, swapped, local_sem.at[6])

    def tokens(source, buf):
        c = {}
        for name, m, j, peer in (
            ("m", mid, t, mid_peer), ("y", mid, t, y_peer), ("c", mid, t, core_peer),
            ("my", 1 - mid, t, y_peer), ("mc", 1 - mid, t, core_peer),
            ("yc", mid, flip(t, 2), core_peer), ("myc", 1 - mid, flip(t, 2), core_peer),
        ):
            ref = tok(buf, m, j)
            c[name] = links.copy(source if len(name) == 1 else ref, ref, peer)
        return c

    xs = tokens(x, xa)
    es = tokens(e, ea)
    own_x = local_copy(x, tok(xa, mid, t))
    own_e = local_copy(e, tok(ea, mid, t))
    own_up = local_copy(up.at[mid], up_block(f))
    own_qkv = local_copy(qkv.at[mid], qkv_block(f))
    own_down = local_copy(down, block(downa, (f // 4) * 2 + f % 2, sub))

    def then(wait, *starts):
        def run():
            wait()
            for start in starts:
                start()

        return run

    def arrived(c, *starts):
        return then(c.wait_recv, *[s.start for s in starts])

    keys = all_keys(masks)[1:]
    inner = [k for k in keys if not k & 1]

    def passes(group):
        return [functools.partial(group.arrive, k) for k in inner]

    def ends(groups):
        for group in groups:
            for k in keys:
                if k & 1:
                    group.wait(k)

    first_up.start()
    up_own.send_all(0)
    xs["y"].start()
    xs["c"].start()
    out_in.start()
    for c in own:
        c.start()
    own_x.wait()
    then(first_up.wait_recv, functools.partial(up_mid.send_all, 0), xs["m"].start)()
    arrived(xs["y"], xs["yc"], es["y"], es["c"])()
    for hook in passes(up_own):
        hook()
    qkv_own.send_all(0)
    arrived(xs["m"], xs["my"], xs["mc"], first_qkv)()
    xs["c"].wait_recv()
    xs["yc"].wait_recv()
    run_norms(vec, xa, n1, n2, lambda i: mid * 4 + i, 4)
    out_in.wait()
    out_own.send(0, 1)
    for hook in passes(up_mid):
        hook()
    then(first_qkv.wait_recv, functools.partial(qkv_mid.send_all, 0), es["m"].start)()
    arrived(xs["my"], xs["myc"])()
    xs["mc"].wait_recv()
    xs["myc"].wait_recv()
    run_norms(vec, xa, n1, n2, lambda i: (1 - mid) * 4 + i, 4)
    ends([up_own, up_mid])
    own_up.wait()
    hooks = [arrived(es["y"], es["yc"])] + passes(qkv_own)

    def out_and_down():
        for mask in masks[:-1]:
            out_own.send(0, mask)
        down_own[0].send_all(0)

    hooks += [out_and_down, arrived(es["m"], es["my"], es["mc"])]
    hooks += passes(qkv_mid)
    hooks += [functools.partial(down_own[1].send_all, 0)]
    run_up(up_bias, n2, upa, g, slope, hooks)
    ends([qkv_own, qkv_mid])
    own_qkv.wait()
    run_project(qkv_bias, n1, qkva, cos, sin, p, passes(out_own) + [arrived(es["my"], es["myc"])])

    same = lambda i: i
    qkv_s = Scatter(links, g_qkv, same, feat, (0, 1), *stage_refs[0], f, t, masks)
    out_s = Scatter(links, g_out, lambda i: out_place(i, top), orow, (None,), *stage_refs[1], f, t, masks)
    down_s = Scatter(links, g_down, lambda i: (i // 4) * 2 + i % 2, sub, (None,), *stage_refs[2], f, t, masks)
    up_s = Scatter(links, g_up, same, feat, (0, 1), *stage_refs[3], f, t, masks)
    down_o, qkv_o, up_o = Outer(down_s, g, ea), Outer(qkv_s, n1, dproj), Outer(up_s, n2, dh)

    for name in ("c", "mc", "yc", "myc"):
        es[name].wait_recv()
    own_e.wait()
    ends([out_own])
    down_o.give(True)
    down_s.send(True)
    down_o.give(False, passes(down_own[0]))
    for i in range(ea.shape[0] // TILE):
        at = slice(i * TILE, (i + 1) * TILE)
        da[at, :] = dot(ea[at, :], outa[...], NT).astype(bf16)
    run_attention(length, 0, bounds, p, da, cos, sin, a, dproj, dk, dv)
    for hook in passes(down_own[1]):
        hook()
    run_attention(length, 1, bounds, p, da, cos, sin, a, dproj, dk, dv)
    qkv_o.give(True)
    qkv_s.send(True)
    qkv_o.give(False)
    down_o.keep(True)
    down_s.send_on()
    ends(down_own)
    own_down.wait()
    run_hidden_grad(ea, downa, slope, dh, bias_sum)
    down_s.send(False)
    up_o.give(True)
    up_s.send(True)
    up_o.give(False)
    qkv_o.keep(True)
    qkv_s.send_on()
    norm_t = Tokens(links, token_refs[0], rows, f, t)
    branch_t = Tokens(links, token_refs[1], rows, f, t)
    norm_job = run_norm_grad(vec, dh, upa, dproj, qkva, xa, sums, qkv_sum)
    branch_job = run_branch(a, outa, g, downa)
    norm_t.give(norm_job)
    qkv_s.send(False)
    norm_t.keep(norm_job, True)
    up_o.keep(True)
    up_s.send_on()
    up_s.send(False)
    norm_t.keep(norm_job, False)
    branch_t.give(branch_job)
    run_outer_wide(a, ea, g_out)
    out_s.send(True)
    out_s.send(False)
    branch_t.keep(branch_job, True)
    branch_t.keep(branch_job, False)

    small[...] = jnp.zeros_like(small)
    small[0:4, :] = sums[0:4, :]
    small[4:5, :] = jnp.sum(e_own[...].astype(f32), axis=0, keepdims=True)
    for c in range(3):
        for h in range(d // HD):
            small[5 + c : 6 + c, h * HD : (h + 1) * HD] = jnp.where(
                t * 2 + mid == h, qkv_sum[0:1, c * HD : (c + 1) * HD], 0.0
            )
    chunk = 2 * sub
    for tt in range(4):
        for hh in range(mine // chunk):
            for mm in range(2):
                at = (hh * 2 + mm) * chunk
                small[8 + tt : 9 + tt, at : at + chunk] = jnp.where(
                    (t == tt) & (mid == mm), bias_sum[0:1, hh * chunk : (hh + 1) * chunk], 0.0
                )
    small_peers = [core_peer, y_peer, mid_peer] + [(flip(f, m), t) for m in masks]
    small_copies = [links.copy(small, small_in.at[r], peer) for r, peer in enumerate(small_peers)]

    def small_add(r):
        small_copies[r].wait()
        small[...] += small_in[r]
        if r + 1 < len(small_peers):
            small_copies[r + 1].start()

    def exchange_columns(job, dst, k):
        total = job.sums[-1]
        c = links.copy(block(total, 1 - mid, feat), dst.at[mid], mid_peer)
        c.start()
        stay = pltpu.make_async_copy(block(total, mid, feat), dst.at[mid], local_sem.at[k])
        stay.start()
        return c, stay

    small_copies[0].start()
    out_s.got(True)
    out_s.first_adds(True)
    out_s.send_on()
    small_add(0)
    down_o.keep(False)
    small_add(1)
    qkv_o.keep(False)
    small_add(2)
    norm_t.across()
    small_add(3)
    up_o.keep(False)
    out_s.got(False)
    out_s.first_adds(False)
    for r in range(4, len(small_peers)):
        small_add(r)
    down_s.finish()
    qkv_s.finish()
    qkv_x = exchange_columns(qkv_s, qkv_new, 7)
    branch_t.across()
    out_s.finish()
    out_back = Swap(links, out_s.sums[-1], out_new, out_new, f, t, swapped, local_sem.at[8])
    out_back.start()
    up_s.finish()
    up_x = exchange_columns(up_s, up_new, 9)
    norm_t.finish()
    branch_t.finish()
    for c, stay in (qkv_x, up_x):
        c.wait_recv()
        stay.wait()
    out_back.wait()
    out_in.drain()
    out_back.drain()
    for c in links.started:
        if all(c is not other for other in small_copies):
            c.wait_send()


ANY = pl.BlockSpec(memory_space=pl.ANY)
VMEM = pl.BlockSpec(memory_space=pltpu.VMEM)
SMEM = pl.BlockSpec(memory_space=pltpu.SMEM)


def run_layer(masks, top, length, tp, x, e, up, qkv, down, out, cos, sin, vec, qkv_bias, up_bias, bounds):
    rows, d = x.shape
    tokens = 2 * tp * rows
    mine, wide = up.shape[2], qkv.shape[2]
    feat, sub, orow = up.shape[1], down.shape[0], out.shape[0]
    n_keys = 1 << len(masks)
    hi_n = n_keys // 2
    shapes = [
        (tokens, d), (tokens, d), (tokens, d), (tokens, mine), (tokens, mine),
        (d, wide), (HD, d), (mine, d), (d, mine),
    ]
    copies = 2 * 7 + 2 * (1 + 2 * (n_keys - 1)) + 2 * (n_keys - 1) + n_keys
    for height, width, mids in ((feat, wide, 2), (orow, d, 1), (sub, d, 1), (feat, mine, 2)):
        for _ in range(2):
            for level in range(len(masks)):
                shapes.append(((hi_n >> level) * mids * height, width))
        copies += (2 * hi_n - 1) * mids + 1
    for _ in range(2):
        shapes += [(4 * rows, d)] * 3 + [(2 * rows, d)] * 2 + [(2, rows, d)]
        copies += 7
    shapes += [(2, feat, mine), (2, feat, wide), (orow, d)]
    n_small = len(masks) + 3
    copies += n_small
    out_shape = [jax.ShapeDtypeStruct(shape, bf16) for shape in shapes]
    out_shape.append(jax.ShapeDtypeStruct((16, d), f32))
    result = pl.pallas_call(
        functools.partial(layer_kernel, masks, top, length),
        out_shape=out_shape,
        in_specs=[ANY] * 6 + [VMEM] * 6 + [SMEM],
        out_specs=[ANY] * len(shapes) + [VMEM],
        scratch_shapes=[
            pltpu.VMEM((tokens, d), bf16),
            pltpu.VMEM((d, mine), bf16),
            pltpu.VMEM((d, wide), bf16),
            pltpu.VMEM((mine, d), bf16),
            pltpu.VMEM((HD, d), bf16),
            pltpu.VMEM((tokens, wide), bf16),
            pltpu.VMEM((tokens, HD), bf16),
            pltpu.VMEM((tokens, HD), bf16),
            pltpu.VMEM((tokens, wide), bf16),
            pltpu.VMEM((tokens, mine), bf16),
            pltpu.VMEM((length, HD), f32),
            pltpu.VMEM((length, HD), f32),
            pltpu.VMEM((8, d), f32),
            pltpu.VMEM((8, wide), f32),
            pltpu.VMEM((8, mine), f32),
            pltpu.VMEM((n_small, 16, d), f32),
            pltpu.SemaphoreType.DMA((copies,)),
            pltpu.SemaphoreType.DMA((copies,)),
            pltpu.SemaphoreType.DMA((10,)),
        ],
        compiler_params=pltpu.CompilerParams(
            collective_id=0, has_side_effects=True, vmem_limit_bytes=60 * 2**20
        ),
        name="layer",
    )(x, e, up, qkv, down, out, cos, sin, e, vec, qkv_bias, up_bias, bounds)
    stage = len(masks)
    at = N_HBM + 2 * stage * 4
    down_new = result[N_HBM + 2 * stage * 3 - 1]
    norm_final, branch_final = result[at + 5], result[at + 11]
    up_new, qkv_new, out_new, small = result[at + 12 : at + 16]
    return norm_final, branch_final, up_new, qkv_new, out_new, down_new, small


def make_local(fsdp, tp):
    lo_n = 2
    hi_n = fsdp // 4
    masks = [1 << b for b in range(2, fsdp.bit_length() - 1)] + [1]
    top = fsdp // 2

    def local(
        layer_input,
        out_cotangent,
        segments,
        qkv_weight,
        qkv_first,
        qkv_second,
        out_weight,
        out_first,
        out_second,
        up_weight,
        up_first,
        up_second,
        down_weight,
        down_first,
        down_second,
        small_params,
        small_first,
        small_second,
    ):
        f = lax.axis_index("fsdp")
        t = lax.axis_index("tp")
        mid = (f // 2) % 2
        rows, d = layer_input.shape
        length = segments.shape[1]
        width = qkv_weight.shape[3]
        hidden = up_weight.shape[2]
        sub = hidden // fsdp
        feat = d // fsdp
        mine = hidden // 2
        vector = small_params[0]

        up16 = up_weight[0].astype(bf16).reshape(feat, hi_n, 2, lo_n * sub)
        up16 = up16.transpose(2, 0, 1, 3).reshape(2, feat, mine)
        qkv16 = qkv_weight[0].astype(bf16).reshape(3, feat, 2, HD)
        qkv16 = qkv16.transpose(2, 1, 0, 3).reshape(2, feat, 3 * HD)
        down16 = down_weight[0].astype(bf16)
        out16 = out_weight[0].astype(bf16)

        own_bounds = jnp.stack([jnp.sum(segments[0] < 1), jnp.sum(segments[0] < 2)]).astype(f32)
        other_bounds = lax.ppermute(own_bounds, "fsdp", [(i, i ^ 2) for i in range(fsdp)])
        bounds = jnp.where(
            mid == 0, jnp.stack([own_bounds, other_bounds]), jnp.stack([other_bounds, own_bounds])
        ).astype(jnp.int32)
        index = jnp.arange(length, dtype=jnp.int32)[None]
        first, second = bounds[:, 0:1], bounds[:, 1:2]
        start = jnp.where(index >= second, second, jnp.where(index >= first, first, 0))
        position = (index - start).astype(f32).reshape(2 * length, 1)
        half = ROT // 2
        lane = jnp.arange(128)
        frequency = 10000.0 ** (-(2 * (lane % half)).astype(f32) / ROT)
        angle = position * frequency[None]
        cosine = jnp.where(lane < ROT, jnp.cos(angle), 1.0)
        sine = jnp.where(lane < ROT, jnp.where(lane < half, -1.0, 1.0) * jnp.sin(angle), 0.0)

        norms = vector[0 : 4 * d].reshape(4, d)
        vec = jnp.concatenate([norms, jnp.zeros((4, d), f32)])
        qkv_bias = lax.dynamic_slice_in_dim(
            vector[6 * d : 9 * d].reshape(3, d), t * width + mid * HD, HD, 1
        ).reshape(1, 3 * HD)
        up_bias = lax.dynamic_slice(
            vector[9 * d :].reshape(tp, hi_n, 2, lo_n * sub), (t, 0, mid, 0), (1, hi_n, 1, lo_n * sub)
        ).reshape(1, mine)

        norm_final, branch_final, up_new, qkv_new, out_new, down_new, small = run_layer(
            masks, top, length, tp, layer_input, out_cotangent, up16, qkv16, down16, out16,
            cosine, sine, vec, qkv_bias, up_bias, bounds,
        )

        stream = layer_input.astype(f32)
        bias = vector[4 * d : 5 * d] + vector[5 * d : 6 * d]
        layer_output = stream + (branch_final[0].astype(f32) + branch_final[1].astype(f32)) + bias
        scaled = norm_final[0].astype(f32) + norm_final[1].astype(f32)
        centred = stream - jnp.mean(stream, axis=-1, keepdims=True)
        inverse = lax.rsqrt(jnp.mean(centred * centred, axis=-1, keepdims=True) + norm_eps)
        normal = centred * inverse
        input_grad = out_cotangent.astype(f32) + inverse * (
            scaled
            - jnp.mean(scaled, axis=-1, keepdims=True)
            - normal * jnp.mean(scaled * normal, axis=-1, keepdims=True)
        )
        qkv_total = qkv_new.reshape(2, feat, 3, HD).transpose(2, 1, 0, 3).reshape(1, 3, feat, width)
        up_total = up_new.reshape(2, feat, hi_n, lo_n * sub).transpose(1, 2, 0, 3).reshape(1, feat, hidden)
        small_total = jnp.concatenate(
            [small[0:5].reshape(-1), small[4:5].reshape(-1), small[5:12].reshape(-1)]
        )[None]
        rate_matrix = d ** (-0.5)
        rate_output = 4.0 * d ** (-0.5)
        results = [layer_output, input_grad]
        for weight, first, second, grad, rate, decay in (
            (qkv_weight, qkv_first, qkv_second, qkv_total, rate_matrix, decay_rate),
            (out_weight, out_first, out_second, out_new[None], rate_output, decay_rate),
            (up_weight, up_first, up_second, up_total, rate_matrix, decay_rate),
            (down_weight, down_first, down_second, down_new[None], rate_matrix, decay_rate),
            (small_params, small_first, small_second, small_total, rate_vector, 0.0),
        ):
            results.extend(adam_step(weight, first, second, grad.astype(f32), rate, decay))
        return tuple(results)

    return local


def solution(mesh):
    tokens = P(("fsdp", "tp"), None)
    inner = P(None, ("tp", "fsdp"), None)
    qkv = P(None, None, "fsdp", "tp")
    up = P(None, "fsdp", "tp")
    weights = (qkv,) * 3 + (inner,) * 3 + (up,) * 3 + (inner,) * 3 + (P(),) * 3
    return jax.shard_map(
        make_local(mesh.shape["fsdp"], mesh.shape["tp"]),
        mesh=mesh,
        in_specs=(tokens, tokens, P("fsdp", None)) + weights,
        out_specs=(tokens, tokens) + weights,
        check_vma=False,
    )
```

time: 1030 us -> 534 us (0.52)
  waiting for transfers between devices: 510 us -> 0.01 us
  Pallas kernels: 0 us -> 442 us
  matrix products: 161 us -> 0 us
  local copies, waits for them, and re-layouts: 186 us -> 42.7 us
  starting transfers between devices: 57.4 us -> 0.45 us
  other arithmetic: 85.5 us -> 36.9 us
  between operations: 16 us -> 1.38 us
    pallas_call x0 -> x1, Pallas kernels: none -> 442 us  [run_layer(): pl.pallas_call(functools.partial(layer_kernel, masks, top, length), out_s...]
    ppermute x53 -> x1, waiting for transfers between devices: 396 us -> 0.01 us  [local(): lax.ppermute(own_bounds, 'fsdp', [(i, i ^ 2) for i in range(fsdp)])]
    dot_general x18 -> x0, matrix products: 161 us -> none  [the longest x11 125 us: dot(): return lax.dot_general(a, b, (dims, ((), ())), preferred_element_type=out)]
    psum x1 -> x0, waiting for transfers between devices: 114 us -> none  [local(): small_total = lax.psum(small_grad[None], ('fsdp', 'tp'))]
    ppermute x53 -> x1, starting transfers between devices: 57.3 us -> 0.45 us  [local(): lax.ppermute(own_bounds, 'fsdp', [(i, i ^ 2) for i in range(fsdp)])]
    dynamic_update_slice x41 -> x0, local copies, waits for them, and re-layouts: 50.2 us -> none  [the longest x16 17.6 us: gather_tokens(): lax.dynamic_update_slice(whole, block[None, None], (mid ^ a // 2, t ^ b,...]
    dynamic_slice x17 -> x1, local copies, waits for them, and re-layouts: 29.2 us -> 0.6 us  [local(): lax.dynamic_slice(vector[9 * d:].reshape(tp, hi_n, 2, lo_n * sub), (t, 0,...]
    convert_element_type x17 -> x8, other arithmetic: 34.8 us -> 8.16 us  [the longest x1 2.86 us: local(): down16 = down_weight[0].astype(bf16)]
  transfers between devices with their start and end apart: 54 -> 1, of which waited for: 22 -> 0; matrix products, arithmetic and copies ran while one was open for 34% -> 5% of each run, Pallas kernels for 0% -> 0%
where the time goes in v4:
time: 534 us; the launch traced here: 524 us
  Pallas kernels  442 us (83%)
  local copies, waits for them, and re-layouts  42.7 us (8%)
  other arithmetic  36.9 us (7%)
    pallas_call x1, Pallas kernels, run_layer(): pl.pallas_call(functools.partial(layer_kernel, masks, top, length), out_s...  442 us
    unnamed x62, local copies, waits for them, and re-layouts  20.3 us
    sub x5, other arithmetic, adam_step(): weight - rate * (first_hat / (jnp.sqrt(second_hat) + adam_eps) + decay *...  16.1 us
    convert_element_type x5, local copies, waits for them, and re-layouts, local(): grad.astype(f32)  12 us
  transfers between devices with their start and end apart: 1, of which 0 were waited for; matrix products, arithmetic and copies ran while one was open for 5% of the time, Pallas kernels for 0%

profile of v4, /device:TPU:30, one launch (start us, length us, event | category | flops | bytes accessed | tf_op | source)
XLA Modules:
  0.0 523.6 jit_solution(17473859116355840522)
XLA Ops:
  0.7 1.3 fusion.28
  2.0 1.4 add_convert_fusion.1
  3.9 0.9 slice_reduce_fusion
  7.0 1.9 copy.46
  9.0 1.2 copy.49.qkv
  10.2 1.7 convert_element_type.140
  11.9 1.6 convert_element_type.141
  13.5 2.0 copy.71
  15.6 1.5 reshape.404.up
  17.1 2.9 convert_bitcast_fusion.down
  20.7 1.6 copy.50
  22.3 3.1 copy.53
  26.1 1.4 add_convert_fusion
  29.0 5.6 %fusion.20 = (f32[2048,128]{1,0:T(8,128)}, f32[2048,128]{1,0:T(8,128)}) fusion(f32[128]{0:T(128)S(1)} %get-tuple-element.75, f32[128]{0:T(128)S(1)} %get-tuple-element.76, f32[2048]{0:T(1024)S(1)} %fusion.27, pred[128]{0:T(512)(128)(4,1)S(1)} %iota_compare_fusion), kind=kLoop, calls=%fused_computation.36 | loop fusion | flops 1048576 | bytes 2106496 | tf_op jit(solution)/shard_map/jit(_where)/select_n | solution.py:919
  34.6 442.2 %layer.1 = (bf16[2048,2048]{1,0:T(8,128)(2,1)}, bf16[2048,2048]{1,0:T(8,128)(2,1)}, bf16[2048,2048]{1,0:T(8,128)(2,1)}, bf16[2048,1024]{1,0:T(8,128)(2,1)}, bf16...) custom-call(bf16[256,2048]{1,0:T(8,128)(2,1)} %x.3, ...), custom_call_target="tpu_custom_call" | custom-call | tf_op jit(solution)/shard_map/layer/pallas_call | solution.py:821
  476.8 0.9 slice_bitcast_fusion
  479.5 1.4 copy.51
  481.0 1.3 copy-done.7
  482.8 2.8 multiply_subtract_fusion.2
  485.6 3.1 copy.57
  488.8 1.6 copy.58
  490.4 1.6 copy.59
  492.0 3.4 reshape.414
  495.4 2.9 copy.56
  498.3 4.2 reshape.412
  504.4 1.1 copy-done.4
  505.5 6.4 %multiply_subtract_fusion.1 = (f32[1,256,2048]{2,1,0:T(8,128)}, f32[1,256,2048]{2,1,0:T(8,128)}, f32[1,256,2048]{2,1,0:T(8,128)}) fusion(f32[1,256,2048]{2,1,0:T(8,128)S(1)} %copy-done.4, f32[1,256,2048]{2,1,0:T(8,128)S(1)} %copy-done.5, f32[1,256,2048]{2,1,0:T(8,128)} %param.29, f32[1,256,2048]{2,1,0:T(8,128)} %param.28), kind=kLoop, calls=%fused_computation.24 | loop fusion | flops 7864320 | bytes 14680064 | tf_op jit(solution)/shard_map/sub | solution.py:30
  511.9 3.9 multiply_subtract_fusion
  515.9 1.4 multiply_subtract_fusion.3
  517.3 1.0 copy-done.14
  518.3 3.4 fusion.7
  521.7 1.5 multiply_subtract_fusion.4
  (79 shorter events, 10.0 us)
Async XLA Ops:
  3.4 25.3 %collective-permute-start = (f32[2]{0:T(128)S(1)}, f32[2]{0:T(128)S(1)}, u32[]{:S(2)}, u32[]{:S(2)}) collective-permute-start(f32[2]{0:T(128)S(1)} %add_convert_fusion.1), channel_id=1, source_target_pairs={{0,8},{4,12},{8,0},{12,4},{16,24},{20,28},{24,16},{28,20},{1,9},{5... | collective-permute-start | bytes 32 | tf_op jit(solution)/shard_map/ppermute | solution.py:906
  17.1 2.9 copy-start.10
  17.1 3.6 copy-start.15
  22.3 3.1 copy-start
  28.7 5.9 %copy-start.23 = (s32[2,2]{1,0:T(2,128)}, s32[2,2]{1,0:T(2,128)S(1)}, u32[]{:S(2)}) copy-start(s32[2,2]{1,0:T(2,128)S(1)} %fusion.30.bounds) | copy-start | bytes 52
  480.9 1.4 copy-start.7
  480.9 1.9 copy-start.8
  485.6 3.1 copy-start.9
  498.3 4.2 copy-start.2
  502.5 1.2 copy-start.1
  502.5 1.9 copy-start.5
  503.7 1.7 copy-start.4
  505.5 6.4 %copy-start.6 = (f32[1,256,2048]{2,1,0:T(8,128)S(1)}, f32[1,256,2048]{2,1,0:T(8,128)}, u32[]{:S(2)}) copy-start(f32[1,256,2048]{2,1,0:T(8,128)} %param.30) | copy-start | bytes 6291460
  505.5 6.4 %copy-start.12 = (f32[1,256,2048]{2,1,0:T(8,128)S(1)}, f32[1,256,2048]{2,1,0:T(8,128)}, u32[]{:S(2)}) copy-start(f32[1,256,2048]{2,1,0:T(8,128)} %param.32) | copy-start | bytes 6291460
  505.5 6.4 %copy-start.13 = (f32[1,256,2048]{2,1,0:T(8,128)S(1)}, f32[1,256,2048]{2,1,0:T(8,128)}, u32[]{:S(2)}) copy-start(f32[1,256,2048]{2,1,0:T(8,128)} %param.31) | copy-start | bytes 6291460
  505.5 6.4 %copy-start.16 = (bf16[256,2048]{1,0:T(8,128)(2,1)S(1)}, bf16[256,2048]{1,0:T(8,128)(2,1)}, u32[]{:S(2)}) copy-start(bf16[256,2048]{1,0:T(8,128)(2,1)} %get-tuple-element.29) | copy-start | bytes 3145732
  511.9 4.0 copy-start.11
  511.9 4.0 copy-start.17
  511.9 3.9 copy-start.18
  511.9 3.9 copy-start.20
  515.9 1.5 copy-start.3
  515.9 2.5 copy-start.14
  518.3 3.4 copy-start.19
  518.3 3.4 copy-start.21
  518.3 3.4 copy-start.22

commit v5 on v4

v5 whole, which is shorter than its diff:
```python
import functools

import jax
import jax.numpy as jnp
import numpy as np
from jax import lax
from jax.experimental import pallas as pl
from jax.experimental.pallas import tpu as pltpu
from jax.sharding import PartitionSpec as P

HD = 256
ROT = 64
STEP = 10

norm_eps = 1e-05
beta_one = 0.9
beta_two = 0.95
adam_eps = 1e-08
decay_rate = 0.01
rate_vector = 0.2
masked_score = -1e30
f32 = jnp.float32
bf16 = jnp.bfloat16


def adam_step(weight, first, second, grad, rate, decay):
    first_new = beta_one * first + (1.0 - beta_one) * grad
    second_new = beta_two * second + (1.0 - beta_two) * grad * grad
    first_hat = first_new / (1.0 - beta_one**STEP)
    second_hat = second_new / (1.0 - beta_two**STEP)
    weight_new = weight - rate * (first_hat / (jnp.sqrt(second_hat) + adam_eps) + decay * weight)
    return (first_new, second_new, weight_new)


MESH = pl.DeviceIdType.MESH


def bit_of(i, mask):
    return (i // mask) % 2


def flip(i, mask):
    return i + mask - 2 * mask * bit_of(i, mask)


class Copy:
    def __init__(self, copy):
        self.copy, self.started, self.received, self.sent = copy, False, False, False

    def start(self):
        self.started = True
        self.copy.start()

    def wait_recv(self):
        self.received = True
        self.copy.wait_recv()

    def wait_send(self):
        self.sent = True
        self.copy.wait_send()


class Local:
    def __init__(self, copy):
        self.copy, self.started, self.done = copy, False, False

    def start(self):
        self.started = True
        self.copy.start()

    def wait(self):
        self.done = True
        self.copy.wait()


class Links:
    def __init__(self, send_sem, recv_sem, local_sem):
        self.send_sem, self.recv_sem, self.local_sem = send_sem, recv_sem, local_sem
        self.copies, self.locals, self.swaps, self.n_local = [], [], [], 0

    def local(self, src, dst):
        c = Local(pltpu.make_async_copy(src, dst, self.local_sem.at[self.n_local]))
        self.n_local += 1
        self.locals.append(c)
        return c

    def copy(self, src, dst, device):
        k = len(self.copies)
        c = Copy(
            pltpu.make_async_remote_copy(
                src_ref=src,
                dst_ref=dst,
                send_sem=self.send_sem.at[k],
                recv_sem=self.recv_sem.at[k],
                device_id=device,
                device_id_type=MESH,
            )
        )
        self.copies.append(c)
        return c

    def drain(self):
        for c in self.copies:
            if c.started and not c.received:
                c.wait_recv()
            if c.started and not c.sent:
                c.wait_send()
        for c in self.locals:
            if c.started and not c.done:
                c.wait()
        for c in self.swaps:
            c.drain()


class Group:
    def __init__(self, links, at, f, t, masks, root):
        self.copies, self.masks = {}, masks
        for key in all_keys(masks):
            g = root
            for mask in masks:
                if key & mask:
                    g = flip(g, mask)
            ref = at(g)
            after = max([i + 1 for i, m in enumerate(masks) if key & m], default=0)
            for mask in masks[after:]:
                self.copies[key | mask] = links.copy(ref, ref, (flip(f, mask), t))

    def low(self):
        self.copies[1].start()

    def high(self):
        self.copies[self.masks[0]].start()

    def rest(self):
        keys = all_keys(self.masks[:-1])
        for s, mask in enumerate(self.masks[1:-1]):
            for key in all_keys(self.masks[: s + 1]):
                if key:
                    self.copies[key].wait_recv()
                self.copies[key | mask].start()
        last = self.masks[-2]
        for key in keys:
            if key & last:
                self.copies[key].wait_recv()
            if key:
                self.copies[key | 1].start()

    def ends(self):
        return [c for key, c in self.copies.items() if key & 1]


def all_keys(masks):
    keys = [0]
    for mask in masks:
        keys = keys + [k | mask for k in keys]
    return keys


def normalise(x):
    mean = jnp.mean(x, axis=-1, keepdims=True)
    centred = x - mean
    inverse = lax.rsqrt(jnp.mean(centred * centred, axis=-1, keepdims=True) + norm_eps)
    return centred * inverse


def rope(u, c, s):
    lane = lax.broadcasted_iota(jnp.int32, u.shape, 1)
    partner = jnp.where(lane < ROT // 2, pltpu.roll(u, 128 - ROT // 2, 1), pltpu.roll(u, ROT // 2, 1))
    return u * c + partner * s


def dot(a, b, dims):
    return lax.dot_general(a, b, (dims, ((), ())), preferred_element_type=f32)


NN = ((1,), (0,))
NT = ((1,), (1,))
TN = ((0,), (0,))
TILE = 256


def pipe(body, steps, ins, outs, hooks=()):
    def whole(*refs):
        for i, n, run in hooks:
            pl.when(pl.program_id(0) == i * steps // n)(run)
        body(*refs)

    pltpu.emit_pipeline(
        whole,
        grid=(steps,),
        in_specs=[spec for _, spec in ins],
        out_specs=[spec for _, spec in outs],
    )(*[ref for ref, _ in ins], *[ref for ref, _ in outs])


def by_rows(ref, index=lambda i: i, rows=TILE):
    return ref, pl.BlockSpec((rows, ref.shape[1]), lambda i: (index(i), 0))


def by_columns(ref, index, width):
    return ref, pl.BlockSpec((ref.shape[0], width), lambda i: (0, index(i)))


def here(i, rows=TILE):
    return pl.ds(pl.multiple_of(i * rows, rows), rows)


def run_cast(weight, index, steps, width, dst):
    def body(w_ref):
        at = pl.ds(pl.multiple_of(pl.program_id(0) * width, width), width)
        dst[:, at] = w_ref[...].astype(bf16)

    pipe(body, steps, [by_columns(weight, index, width)], [])


def run_cast_qkv(weight, half, dst):
    def body(w_ref):
        at = pl.ds(pl.multiple_of(pl.program_id(0) * HD, HD), HD)
        dst[:, at] = w_ref[...].reshape(w_ref.shape[-2:]).astype(bf16)

    spec = pl.BlockSpec((1, weight.shape[1], HD), lambda i: (i, 0, half))
    pipe(body, 3, [(weight, spec)], [])


def run_norms(vec, x, n1, n2, index, steps, hooks=()):
    def body(x_ref, one_ref, two_ref):
        normal = normalise(x_ref[...].astype(f32))
        one_ref[...] = (normal * vec[0:1, :] + vec[1:2, :]).astype(bf16)
        two_ref[...] = (normal * vec[2:3, :] + vec[3:4, :]).astype(bf16)

    pipe(body, steps, [by_rows(x, index)], [by_rows(n1, index), by_rows(n2, index)], hooks)


class Rotary:
    def __init__(self, table, starts, seq):
        self.table, self.starts, self.seq = table, starts, seq

    def bounds(self):
        at = pl.ds(self.seq * 8, 1)
        return self.starts[at, 0:1].astype(jnp.int32), self.starts[at, 1:2].astype(jnp.int32)

    def __call__(self, tile):
        shape = (TILE, 128)
        lane = lax.broadcasted_iota(jnp.int32, (1, 128), 1)
        first, second = self.bounds()
        turning = lane < ROT
        rate = self.table[0:1, 256:384]
        one, two = first.astype(f32) * rate, second.astype(f32) * rate
        index = tile * TILE + lax.broadcasted_iota(jnp.int32, shape, 0)
        pick = lambda a, b, c: jnp.where(index >= second, c, jnp.where(index >= first, b, a))
        cos_b = pick(jnp.ones_like(one), jnp.cos(one), jnp.cos(two))
        sin_b = pick(jnp.zeros_like(one), jnp.sin(one), jnp.sin(two))
        rows = here(tile)
        cos_t, sin_t = self.table[rows, 0:128], self.table[rows, 128:256]
        sign = jnp.where(lane < ROT // 2, -1.0, 1.0)
        c = jnp.where(turning, cos_t * cos_b + sin_t * sin_b, 1.0)
        s = jnp.where(turning, sign * (sin_t * cos_b - cos_t * sin_b), 0.0)
        return c, s


def run_project(qkv_bias, n1, w, rotary, seq, p, turns, steps, hooks=()):
    def body(n_ref):
        i = pl.program_id(0)
        at = here(seq * steps + i)
        c, s = rotary(i)
        turns[at, 0:128] = c
        turns[at, 128:256] = s
        proj = dot(n_ref[...], w[...], NN) + qkv_bias()
        for j in range(2):
            p[at, j * HD : j * HD + 128] = rope(proj[:, j * HD : j * HD + 128], c, s).astype(bf16)
            p[at, j * HD + 128 : (j + 1) * HD] = proj[:, j * HD + 128 : (j + 1) * HD].astype(bf16)
        p[at, 2 * HD :] = proj[:, 2 * HD :].astype(bf16)

    pipe(body, steps, [by_rows(n1, lambda i: seq * steps + i)], [], hooks)


def run_up(up_bias, n2, w, g, slope, index, steps, hooks=()):
    width = w.shape[1]
    part = min(width, 256)

    def body(n_ref, g_ref, s_ref):
        n = n_ref[...]
        for j in range(0, width, part):
            h = dot(n, w[:, j : j + part], NN) + up_bias[0:1, j : j + part]
            cdf = 0.5 + 0.5 * lax.erf(h * 0.7071067811865476)
            g_ref[:, j : j + part] = (h * cdf).astype(bf16)
            s_ref[:, j : j + part] = (cdf + h * (jnp.exp(-0.5 * h * h) * 0.3989422804014327)).astype(bf16)

    pipe(body, steps, [by_rows(n2, index)], [by_rows(g, index), by_rows(slope, index)], hooks)


def run_attention(length, seq, rotary, p, da, turns, a, dproj, dk, dv):
    scale = HD ** (-0.5)
    tiles_n = length // TILE
    first, second = rotary.bounds()
    rows = lambda i: here(seq * tiles_n + i)

    def put(i, value, column):
        at = rows(i)
        dproj[at, column : column + 128] = rope(value[:, :128], turns[at, 0:128], -turns[at, 128:256]).astype(bf16)
        dproj[at, column + 128 : column + HD] = value[:, 128:].astype(bf16)

    dk[...] = jnp.zeros_like(dk)
    dv[...] = jnp.zeros_like(dv)
    for i in range(tiles_n):
        n = (i + 1) * TILE
        until = pl.ds(pl.multiple_of(seq * length, length), n)
        q = p[rows(i), 0:HD]
        k = p[until, HD : 2 * HD]
        v = p[until, 2 * HD :]
        rows_da = da[rows(i), :]
        scores = dot(q, k, NT) * scale
        qi = i * TILE + lax.broadcasted_iota(jnp.int32, (TILE, n), 0)
        ki = lax.broadcasted_iota(jnp.int32, (TILE, n), 1)
        start = jnp.where(qi >= second, second, jnp.where(qi >= first, first, 0))
        scores = jnp.where((ki <= qi) & (ki >= start), scores, masked_score)
        peak = jnp.max(scores, axis=-1, keepdims=True)
        raised = jnp.exp(scores - peak)
        probs = raised * (1.0 / jnp.sum(raised, axis=-1, keepdims=True))
        weights = probs.astype(bf16)
        a[rows(i), :] = dot(weights, v, NN).astype(bf16)
        prob_grad = dot(rows_da, v, NT)
        delta = jnp.sum(probs * prob_grad, axis=-1, keepdims=True)
        score_grad = (probs * (prob_grad - delta)).astype(bf16)
        put(i, dot(score_grad, k, NN) * scale, 0)
        dk[0:n, :] += dot(score_grad, q, TN)
        dv[0:n, :] += dot(weights, rows_da, TN)
    for i in range(tiles_n):
        local = slice(i * TILE, (i + 1) * TILE)
        put(i, dk[local, :] * scale, HD)
        dproj[rows(i), 2 * HD :] = dv[local, :].astype(bf16)


def run_outer(a, b, out, index_in, index_out, steps, width, add=None, hooks=()):
    def body(*refs):
        value = dot(refs[0][...], b[...], TN)
        if add is not None:
            value = value + refs[1][...].astype(f32)
        refs[-1][...] = value.astype(bf16)

    ins = [by_columns(a, index_in, width)]
    if add is not None:
        ins.append(by_rows(add, index_out, width))
    pipe(body, steps, ins, [by_rows(out, index_out, width)], hooks)


def run_outer_wide(a, b, out):
    width = 2 * TILE

    def body(out_ref):
        at = pl.ds(pl.multiple_of(pl.program_id(0) * width, width), width)
        out_ref[...] = dot(a[...], b[:, at], TN).astype(bf16)

    pipe(body, b.shape[1] // width, [], [by_columns(out, lambda i: i, width)])


def run_hidden_grad(e, w, slope, dh, bias_sum, index, steps, hooks=()):
    def body(s_ref):
        at = here(index(pl.program_id(0)))
        value = (dot(e[at, :], w[...], NT) * s_ref[...].astype(f32)).astype(bf16)
        dh[at, :] = value
        bias_sum[0:1, :] += jnp.sum(value.astype(f32), axis=0, keepdims=True)

    pipe(body, steps, [by_rows(slope, index)], [], hooks)


def run_norm_grad(vec, dh, w_up, dproj, w_qkv, x, sums, qkv_sum):
    def tile(at, x_ref):
        normal = normalise(x_ref[...].astype(f32))
        rows = dproj[at, :]
        one = dot(rows, w_qkv[...], NT)
        two = dot(dh[at, :], w_up[...], NT)
        for j, value in ((0, one * normal), (1, one), (2, two * normal), (3, two)):
            sums[j : j + 1, :] += jnp.sum(value, axis=0, keepdims=True)
        qkv_sum[0:1, :] += jnp.sum(rows.astype(f32), axis=0, keepdims=True)
        return one * vec[0:1, :] + two * vec[2:3, :]

    return x, tile


def run_branch(a, w_out, g, w_down):
    def tile(at, g_ref):
        return dot(a[at, :], w_out[...], NN) + dot(g_ref[...], w_down[...], NN)

    return g, tile


def run_token_tiles(job, out, index, index_out, steps, add=None, hooks=()):
    source, tile = job

    def body(*refs):
        value = tile(here(index(pl.program_id(0))), refs[0])
        if add is not None:
            value = value + refs[1][...].astype(f32)
        refs[-1][...] = value.astype(bf16)

    ins = [by_rows(source, index)]
    if add is not None:
        ins.append(by_rows(add, index_out))
    pipe(body, steps, ins, [by_rows(out, index_out)], hooks)


def run_add(a, b, out):
    rows, cols = out.shape
    step = min(rows, TILE)

    def body(a_ref, b_ref, out_ref):
        out_ref[...] = (a_ref[...].astype(f32) + b_ref[...].astype(f32)).astype(bf16)

    pipe(body, rows // step, [by_rows(a, rows=step), by_rows(b, rows=step)], [by_rows(out, rows=step)])


def block(ref, index, rows):
    return ref.at[pl.ds(pl.multiple_of(index * rows, rows), rows)]


def out_place(g, top):
    return (((g // 4) % (top // 4)) * 2 + g // top) * 2 + g % 2


class Scatter:
    def __init__(self, links, part, place, rows, mids, recv, sums, f, t, masks):
        self.links, self.part, self.place, self.rows, self.mids = links, part, place, rows, mids
        self.recv, self.sums, self.f, self.t = recv, sums, f, t
        self.stages = [1] + [m for m in reversed(masks) if m != 1]
        self.n_hi = 1 << (len(masks) - 1)
        self.hi, self.lo, self.mid = f // 4, f % 2, bit_of(f, 2)
        self.copies = {}
        for k in range(self.n_hi):
            for j, m in enumerate(mids):
                self.copies[0, k, j] = links.copy(
                    block(part, self.at_place(self.high(k), m, 1 - self.lo), rows),
                    block(recv[0], self.slot(0, k, j), rows),
                    (flip(f, 1), t),
                )
        for level in range(len(self.stages) - 1):
            n = self.n_hi >> (level + 1)
            for k in range(n, 2 * n):
                for j in range(len(mids)):
                    self.copies[level + 1, k - n, j] = links.copy(
                        block(sums[level], self.slot(level, k, j), rows),
                        block(recv[level + 1], self.slot(level + 1, k, j), rows),
                        (flip(f, self.stages[level + 1]), t),
                    )

    def high(self, k):
        hi, b = self.hi, 1
        while b < self.n_hi:
            if k & b:
                hi = flip(hi, b)
            b *= 2
        return hi

    def slot(self, level, k, j):
        n = self.n_hi >> level
        i = (self.high(k) % n) if n > 1 else 0
        return i * len(self.mids) + j

    def at_place(self, hi, m, lo):
        return self.place((hi * 2 + (self.mid if m is None else m)) * 2 + lo)

    def ks(self, far):
        half = self.n_hi // 2
        return range(half, self.n_hi) if far else range(half)

    def each(self, far):
        return [(k, j) for k in self.ks(far) for j in range(len(self.mids))]

    def tile(self, i, far, lo):
        n = len(self.mids)
        half = self.n_hi // 2
        upper = self.hi // half
        hi = (1 - upper if far else upper) * half + i // n
        j = i % n
        m = None if self.mids[0] is None else j
        return self.at_place(hi, m, lo), hi * n + j

    def add(self, level, k, j):
        mine = (
            block(self.part, self.at_place(self.high(k), self.mids[j], self.lo), self.rows)
            if level == 0
            else block(self.sums[level - 1], self.slot(level - 1, k, j), self.rows)
        )
        at = self.slot(level, k, j)
        run_add(mine, block(self.recv[level], at, self.rows), block(self.sums[level], at, self.rows))

    def first_adds(self, far):
        for k, j in self.each(far):
            self.add(0, k, j)

    def finish(self, waited):
        for level in range(1, len(self.stages)):
            n = self.n_hi >> level
            for k in reversed(range(n)):
                for j in range(len(self.mids)):
                    if not waited:
                        self.copies[level, k, j].wait_recv()
                    self.add(level, k, j)
                    if level + 1 < len(self.stages) and k & (n // 2):
                        self.copies[level + 1, k - n // 2, j].start()


class Outer:
    def __init__(self, scatter, a, b):
        self.s, self.a, self.b = scatter, a, b
        self.fused = scatter.rows % 128 == 0
        self.steps = scatter.n_hi // 2 * len(scatter.mids)

    def give(self, far, hooks=()):
        s = self.s
        if self.fused:
            at = lambda i: s.tile(i, far, 1 - s.lo)[0]
            run_outer(self.a, self.b, s.part, at, at, self.steps, s.rows, hooks=hooks)
        elif far:
            run_outer(self.a, self.b, s.part, lambda i: i, lambda i: i, self.a.shape[1] // 128, 128, hooks=hooks)

    def keep(self, far, hooks=()):
        s = self.s
        if self.fused:
            at = lambda i: s.tile(i, far, s.lo)[0]
            to = lambda i: s.tile(i, far, s.lo)[1]
            run_outer(self.a, self.b, s.sums[0], at, to, self.steps, s.rows, add=s.recv[0], hooks=hooks)
        else:
            s.first_adds(far)


class Tokens:
    def __init__(self, links, refs, rows, f, t, job):
        self.give_buf, self.got, self.sum, self.got_y, self.sum_y, self.final = refs
        self.rows, self.mid, self.y, self.core, self.job = rows, bit_of(f, 2), t // 2, t % 2, job
        core_peer, y_peer, mid_peer = (f, flip(t, 1)), (f, flip(t, 2)), (flip(f, 2), t)
        self.over_core = [
            links.copy(block(self.give_buf, i, rows), block(self.got, i, rows), core_peer) for i in range(4)
        ]
        self.over_y = [
            links.copy(block(self.sum, m * 2 + 1 - self.y, rows), block(self.got_y, m, rows), y_peer)
            for m in range(2)
        ]
        self.over_mid = [links.copy(block(self.sum_y, 1 - self.mid, rows), self.final.at[1], mid_peer)]

    def give(self, hooks=()):
        index = lambda i: (i // 2) * 4 + (i % 2) * 2 + 1 - self.core
        run_token_tiles(self.job, self.give_buf, index, lambda i: i, 4, hooks=hooks)

    def keep(self, far, hooks=()):
        yy = 1 - self.y if far else self.y
        index = lambda i: i * 4 + yy * 2 + self.core
        run_token_tiles(self.job, self.sum, index, lambda i: i * 2 + yy, 2, add=self.got, hooks=hooks)

    def across(self, own):
        m = self.mid if own else 1 - self.mid
        to = self.final.at[0] if own else block(self.sum_y, m, self.rows)
        run_add(block(self.sum, m * 2 + self.y, self.rows), block(self.got_y, m, self.rows), to)


def greet(f, t, masks, top):
    mid = bit_of(f, 2)
    swapped = f + (top - 2) * (mid - bit_of(f, top))
    barrier = pltpu.get_barrier_semaphore()
    peers = [(flip(f, m), t) for m in masks + [2]] + [(f, flip(t, 1)), (f, flip(t, 2))]
    for peer in peers:
        pl.semaphore_signal(barrier, inc=1, device_id=peer, device_id_type=MESH)

    @pl.when(swapped != f)
    def _():
        pl.semaphore_signal(barrier, inc=1, device_id=(swapped, t), device_id_type=MESH)

    pl.semaphore_wait(barrier, len(peers) + (mid + bit_of(f, top)) % 2)
    return swapped


class Swap:
    def __init__(self, links, src, dst, stay, f, t, swapped):
        self.move = links.copy(src, dst, (swapped, t)).copy
        self.copy = pltpu.make_async_copy(src, stay, links.local_sem.at[links.n_local])
        links.n_local += 1
        links.swaps.append(self)
        self.moves, self.stays = swapped != f, swapped == f
        self.started, self.done = False, False

    def start(self):
        self.started = True
        pl.when(self.moves)(self.move.start)
        pl.when(self.stays)(self.copy.start)

    def wait(self):
        self.done = True
        pl.when(self.moves)(self.move.wait_recv)
        pl.when(self.stays)(self.copy.wait)

    def drain(self):
        if self.started and not self.done:
            self.wait()
        if self.started:
            pl.when(self.moves)(self.move.wait_send)


class Plan:
    def __init__(self):
        self.actions, self.waits = {}, {}

    def send(self, name, needs, starts, *copies):
        self.actions[name] = (None, needs, starts)
        self.waits[name] = copies

    def compute(self, name, needs, run):
        self.actions[name] = (True, needs, run)

    def pending(self, name):
        found = []
        for need in self.actions[name][1]:
            found += self.waits.pop(need, ())
        return found

    def starter(self, name):
        pending, starts = self.pending(name), self.actions[name][2]

        def run():
            for c in pending:
                c()
            for start in starts:
                start()

        return run

    def carry_out(self, order):
        i = 0
        while i < len(order):
            name = order[i]
            i += 1
            compute, _, run = self.actions[name]
            if not compute:
                self.starter(name)()
                continue
            for wait in self.pending(name):
                wait()
            n = 1 + order[i:].count(name)
            hooks = []
            for part in range(1, n):
                while order[i] != name:
                    hooks.append((part, n, self.starter(order[i])))
                    i += 1
                i += 1
            run(hooks) if n > 1 else run(())


ORDER = [
    "xs_m", "xs_y", "cast_out", "cast_qkv", "qkv_first", "cast_down", "down1_x", "es_y", "out_swap", "xs_c",
    "down0_x", "qkv_own_zh", "qkv_mid_zh", "out_x", "qkv_own_zhx", "cast_up", "es_m", "qkv_mid_zhx", "es_c",
    "down1_zh", "xs_my", "out_zh", "qkv_own_x", "up_own_x", "qkv_mid_x", "xs_mc", "xs_yc", "out_zhx", "es_yc",
    "xs_myc", "norms_own", "up_own_zh", "up_first", "es_my", "norms_oth", "down1_zhx", "proj_own", "proj_own",
    "es_mc", "proj_oth", "proj_oth", "up_mid_zh", "up_mid_x", "es_myc", "up_own_zhx", "da_own", "da_oth",
    "attn_own", "attn_oth", "up_mid_zhx", "down0_zh", "gout", "gqkv_gf", "gqkv_f", "gqkv_gn", "up_own",
    "up_own", "up_oth", "down0_zhx", "up_oth", "gqkv_kf", "gqkv_on", "gdown_gf", "gdown_f", "branch_g",
    "branch_g", "branch_c", "dh_oth", "dh_oth", "dh_own", "dh_own", "branch_kf", "branch_y", "gqkv_n",
    "gdown_kf", "gdown_on", "gup_gf", "norm_g", "gout_n", "norm_g", "norm_c", "gout_f", "gqkv_kn", "gqkv_add",
    "gqkv_x", "gup_f", "gout_kf", "branch_kn", "norm_kf", "gout_on", "norm_y", "branch_aa", "branch_m",
    "gdown_gn", "gdown_n", "gup_kf", "gup_on", "norm_kn", "gup_gn", "small0", "gout_kn", "small1", "gdown_kn",
    "gup_n", "branch_ab", "gdown_add", "gout_add", "small2", "norm_aa", "norm_m", "norm_ab", "small3",
    "gup_kn", "small4", "gup_add", "gout_x", "gup_x", "small_end",
]

N_HBM = 9


def layer_kernel(
    masks, top, length,
    x, e, up, qkv, down, out, seg, table, e_own, vec,
    *rest,
):
    n_stage = len(masks)
    (xa, n1, n2, g, slope, g_qkv, g_out, g_down, g_up), rest = rest[:N_HBM], rest[N_HBM:]
    stage_refs = []
    for _ in range(4):
        stage_refs.append((rest[:n_stage], rest[n_stage : 2 * n_stage]))
        rest = rest[2 * n_stage :]
    token_refs, rest = [rest[:6], rest[6:12]], rest[12:]
    (up_new, qkv_new, out_new, small), rest = rest[:4], rest[4:]
    (
        ea, upa, qkva, downa, outa, up16, qkv16, out16, p, da, a, dproj, dh, turns, dk, dv,
        sums, qkv_sum, bias_sum, up_bias, starts, small_in,
        send_sem, recv_sem, local_sem,
    ) = rest
    f = lax.axis_index("fsdp")
    t = lax.axis_index("tp")
    mid = bit_of(f, 2)
    rows, d = x.shape
    feat, sub, orow = up.shape[0], down.shape[0], out.shape[0]
    mine = upa.shape[1]
    chunk = 2 * sub
    hi_n = mine // chunk
    swapped = greet(f, t, masks, top)
    links = Links(send_sem, recv_sem, local_sem)
    plan = Plan()

    mid_peer, y_peer, core_peer = (flip(f, 2), t), (f, flip(t, 2)), (f, flip(t, 1))
    qkv_block = lambda i: block(qkva, i, feat)
    up_block = lambda i: block(upa, i, feat)
    half_sub = sub // 2
    out_block = lambda i: block(outa, out_place(i, top), orow)
    tok = lambda buf, m, j: block(buf, m * 4 + j, rows)

    def sends(name, needs, *copies):
        plan.send(name, needs, [c.start for c in copies], *[c.wait_recv for c in copies])

    own_x = links.local(x, tok(xa, mid, t))
    own_e = links.local(e, tok(ea, mid, t))
    for prefix, source, buf, own in (("xs", x, xa, own_x), ("es", e, ea, own_e)):
        for name, needs, m, j, peer in (
            ("m", (), mid, t, mid_peer),
            ("y", (), mid, t, y_peer),
            ("c", (), mid, t, core_peer),
            ("my", ("m",), 1 - mid, t, y_peer),
            ("mc", ("m",), 1 - mid, t, core_peer),
            ("yc", ("y",), mid, flip(t, 2), core_peer),
            ("myc", ("my",), 1 - mid, flip(t, 2), core_peer),
        ):
            ref = tok(buf, m, j)
            c = links.copy(ref if needs else source, ref, peer)
            sends(prefix + "_" + name, [prefix + "_" + n for n in needs], c)
    plan.waits["own_x"], plan.waits["own_e"] = (own_x.wait,), (own_e.wait,)
    own_x.start()
    own_e.start()

    def spreads(name, group, need):
        sends(name + "_x", need, group.copies[1])
        plan.send(name + "_zh", need, [group.high], *([group.copies[masks[0]].wait_recv] if n_stage == 2 else []))
        if n_stage == 2:
            sends(name + "_zhx", [name + "_zh"], group.copies[masks[0] | 1])
        else:
            plan.send(name + "_zhx", [], [group.rest], *[c.wait_recv for c in group.ends() if c is not group.copies[1]])

    first_up = links.copy(up16, up_block(f), mid_peer)
    first_qkv = links.copy(qkv16, qkv_block(f), mid_peer)
    sends("up_first", [], first_up)
    sends("qkv_first", [], first_qkv)
    spreads("up_own", Group(links, up_block, f, t, masks, f), [])
    spreads("up_mid", Group(links, up_block, f, t, masks, flip(f, 2)), ["up_first"])
    spreads("qkv_own", Group(links, qkv_block, f, t, masks, f), [])
    spreads("qkv_mid", Group(links, qkv_block, f, t, masks, flip(f, 2)), ["qkv_first"])
    for h in range(2):
        at = lambda i, h=h: block(downa, ((i // 4) * 2 + i % 2) * 2 + h, half_sub)
        spreads("down" + str(h), Group(links, at, f, t, masks, f), [])
    out_in = Swap(links, out16, out_block(swapped), out_block(f), f, t, swapped)
    plan.send("out_swap", [], [out_in.start], out_in.wait)
    spreads("out", Group(links, out_block, f, t, masks, f), ["out_swap"])
    other_starts = links.copy(starts.at[pl.ds(0, 8)], starts.at[pl.ds(8, 8)], mid_peer)

    segments = seg[0:1, :]
    count = lambda n: jnp.sum((segments < n).astype(f32), axis=1, keepdims=True)
    lane = lax.broadcasted_iota(jnp.int32, (8, 128), 1)
    starts[0:8, :] = jnp.where(lane == 0, count(1), count(2))
    other_starts.start()
    for ref in (sums, qkv_sum, bias_sum):
        ref[...] = jnp.zeros_like(ref)
    for h in range(hi_n):
        at = pl.ds(pl.multiple_of((h * 2 + mid) * chunk, chunk), chunk)
        up_bias[0:1, h * chunk : (h + 1) * chunk] = sum(
            jnp.where(t == j, vec[9 + j : 10 + j, at], 0.0) for j in range(4)
        )
    head = pl.ds(pl.multiple_of((t * 2 + mid) * HD, HD), HD)
    qkv_bias = lambda: jnp.concatenate([vec[6 + c : 7 + c, head] for c in range(3)], axis=1)

    def cast_qkv(hooks):
        run_cast_qkv(qkv, 1 - mid, qkv16)
        run_cast_qkv(qkv, mid, qkv_block(f))

    def cast_up(hooks):
        run_cast(up, lambda i: i * 2 + 1 - mid, hi_n, chunk, up16)
        run_cast(up, lambda i: i * 2 + mid, hi_n, chunk, up_block(f))

    plan.compute("cast_qkv", [], cast_qkv)
    plan.compute("cast_up", [], cast_up)
    down_rows = block(downa, (f // 4) * 2 + f % 2, sub)
    plan.compute("cast_down", [], lambda hooks: run_cast(down, lambda i: i, 2, d // 2, down_rows))
    plan.compute("cast_out", [], lambda hooks: run_cast(out, lambda i: i, 1, d, out16))

    per_seq = length // TILE
    names = lambda prefix, *ends: [prefix + "_" + end for end in ends]
    of_up = names("up", "own_x", "own_zhx", "mid_x", "mid_zhx")
    of_qkv = names("qkv", "own_x", "own_zhx", "mid_x", "mid_zhx")
    of_down = ["down0_x", "down0_zhx", "down1_x", "down1_zhx"]
    of_out = ["out_x", "out_zhx"]
    plan.waits["starts"] = (other_starts.wait_recv,)
    norms = vec
    for which, seq, arrive in (("own", mid, ("c", "y", "yc")), ("oth", 1 - mid, ("m", "mc", "my", "myc"))):
        own = which == "own"
        rotary = Rotary(table, starts, 0 if own else 1)
        index = lambda i, seq=seq: seq * per_seq + i
        es = names("es", *arrive) + ["own_e"]
        plan.compute(
            "norms_" + which,
            names("xs", *arrive) + ["own_x"],
            lambda hooks, index=index: run_norms(norms, xa, n1, n2, index, per_seq, hooks),
        )
        plan.compute(
            "up_" + which,
            of_up,
            lambda hooks, index=index: run_up(up_bias, n2, upa, g, slope, index, per_seq, hooks),
        )
        plan.compute(
            "proj_" + which,
            of_qkv + ["starts"],
            lambda hooks, seq=seq, rotary=rotary: run_project(
                qkv_bias, n1, qkva, rotary, seq, p, turns, per_seq, hooks
            ),
        )

        def back(hooks, index=index):
            for i in range(per_seq):
                at = here(index(i))
                da[at, :] = dot(ea[at, :], outa[...], NT).astype(bf16)

        plan.compute("da_" + which, of_out + es, back)
        plan.compute(
            "attn_" + which,
            [],
            lambda hooks, seq=seq, rotary=rotary: run_attention(
                length, seq, rotary, p, da, turns, a, dproj, dk, dv
            ),
        )
        plan.compute(
            "dh_" + which,
            of_down + es,
            lambda hooks, index=index: run_hidden_grad(ea, downa, slope, dh, bias_sum, index, per_seq, hooks),
        )
    all_es = names("es", "c", "y", "yc", "m", "mc", "my", "myc") + ["own_e"]

    same = lambda i: i
    down_place = lambda i: (i // 4) * 2 + i % 2

    def scatter(name, part, place, height, mids, refs):
        s = Scatter(links, part, place, height, mids, *refs, f, t, masks)
        for far, end in ((True, "_f"), (False, "_n")):
            sends(name + end, [], *[s.copies[0, k, j] for k, j in s.each(far)])
        half = s.n_hi // 2
        sends(name + "_on", [], *[s.copies[1, k - half, j] for k, j in s.each(True)])
        plan.compute(name + "_add", [name + "_on"] if n_stage == 2 else [], lambda hooks: s.finish(n_stage == 2))
        return s

    def outer(name, s, left, right, needs):
        o = Outer(s, left, right)
        plan.compute(name + "_gf", needs, lambda hooks: o.give(True, hooks))
        plan.compute(name + "_gn", needs, lambda hooks: o.give(False, hooks))
        plan.compute(name + "_kf", [name + "_f"], lambda hooks: o.keep(True, hooks))
        plan.compute(name + "_kn", [name + "_n"], lambda hooks: o.keep(False, hooks))

    qkv_s = scatter("gqkv", g_qkv, same, feat, (0, 1), stage_refs[0])
    out_s = scatter("gout", g_out, lambda i: out_place(i, top), orow, (None,), stage_refs[1])
    down_s = scatter("gdown", g_down, down_place, sub, (None,), stage_refs[2])
    up_s = scatter("gup", g_up, same, feat, (0, 1), stage_refs[3])
    outer("gdown", down_s, g, ea, all_es)
    outer("gqkv", qkv_s, n1, dproj, [])
    outer("gup", up_s, n2, dh, [])
    plan.compute("gout", all_es, lambda hooks: run_outer_wide(a, ea, g_out))
    plan.compute("gout_kf", ["gout_f"], lambda hooks: out_s.first_adds(True))
    plan.compute("gout_kn", ["gout_n"], lambda hooks: out_s.first_adds(False))
    out_back = Swap(links, out_s.sums[-1], out_new, out_new, f, t, swapped)
    plan.send("gout_x", [], [out_back.start], out_back.wait)

    def exchange_columns(name, job, dst):
        total = job.sums[-1]
        c = links.copy(block(total, 1 - mid, feat), dst.at[mid], mid_peer)
        stay = links.local(block(total, mid, feat), dst.at[mid])
        plan.send(name, [], [c.start, stay.start], c.wait_recv)

    exchange_columns("gqkv_x", qkv_s, qkv_new)
    exchange_columns("gup_x", up_s, up_new)

    norm_t = Tokens(links, token_refs[0], rows, f, t, run_norm_grad(vec, dh, upa, dproj, qkva, xa, sums, qkv_sum))
    branch_t = Tokens(links, token_refs[1], rows, f, t, run_branch(a, outa, g, downa))
    for name, job, needs in (("norm", norm_t, []), ("branch", branch_t, of_down + of_out)):
        plan.compute(name + "_g", needs, lambda hooks, job=job: job.give(hooks))
        sends(name + "_c", [], *job.over_core)
        plan.compute(name + "_kf", [name + "_c"], lambda hooks, job=job: job.keep(True, hooks))
        plan.compute(name + "_kn", [name + "_c"], lambda hooks, job=job: job.keep(False, hooks))
        sends(name + "_y", [], *job.over_y)
        plan.compute(name + "_aa", [name + "_y"], lambda hooks, job=job: job.across(False))
        plan.compute(name + "_ab", [name + "_y"], lambda hooks, job=job: job.across(True))
        sends(name + "_m", [], *job.over_mid)

    small_peers = [core_peer, y_peer, mid_peer] + [(flip(f, m), t) for m in masks]
    small_copies = [links.copy(small, small_in.at[r], peer) for r, peer in enumerate(small_peers)]

    def small_fill():
        small[...] = jnp.zeros_like(small)
        small[0:4, :] = sums[0:4, :]
        small[4:5, :] = jnp.sum(e_own[...].astype(f32), axis=0, keepdims=True)
        for c in range(3):
            small[5 + c : 6 + c, head] = qkv_sum[0:1, c * HD : (c + 1) * HD]
        for h in range(hi_n):
            at = pl.ds(pl.multiple_of((h * 2 + mid) * chunk, chunk), chunk)
            for j in range(4):
                small[8 + j : 9 + j, at] = jnp.where(t == j, bias_sum[0:1, h * chunk : (h + 1) * chunk], 0.0)
        small_copies[0].start()

    def small_add(r):
        small_copies[r].wait_send()
        small[...] += small_in[r]

    def small_step(r):
        small_add(r - 1)
        small_copies[r].start()

    def small_end(hooks):
        small_add(4)
        for r in range(5, len(small_peers)):
            small_copies[r].start()
            small_copies[r].wait_recv()
            small_add(r)

    plan.send("small0", [], [small_fill], small_copies[0].wait_recv)
    for r in range(1, 5):
        name = "small" + str(r)
        step = functools.partial(small_step, r)
        plan.send(name, ["small" + str(r - 1)], [step], small_copies[r].wait_recv)
    plan.compute("small_end", ["small4"], small_end)

    plan.carry_out(ORDER)
    links.drain()


ANY = pl.BlockSpec(memory_space=pl.ANY)
VMEM = pl.BlockSpec(memory_space=pltpu.VMEM)


def run_layer(masks, top, length, tp, x, e, up, qkv, down, out, seg, table, vec):
    rows, d = x.shape
    tokens = 2 * tp * rows
    mine, wide = up.shape[1] // 2, 3 * HD
    feat, sub, orow = up.shape[0], down.shape[0], out.shape[0]
    n_keys = 1 << len(masks)
    hi_n = n_keys // 2
    shapes = [
        (tokens, d), (tokens, d), (tokens, d), (tokens, mine), (tokens, mine),
        (d, wide), (HD, d), (mine, d), (d, mine),
    ]
    copies = 2 * 7 + 2 * (1 + 2 * (n_keys - 1)) + 2 * (n_keys - 1) + n_keys + 1
    for height, width, mids in ((feat, wide, 2), (orow, d, 1), (sub, d, 1), (feat, mine, 2)):
        for _ in range(2):
            for level in range(len(masks)):
                shapes.append(((hi_n >> level) * mids * height, width))
        copies += (2 * hi_n - 1) * mids + 1
    for _ in range(2):
        shapes += [(4 * rows, d)] * 3 + [(2 * rows, d)] * 2 + [(2, rows, d)]
        copies += 7
    shapes += [(2, feat, mine), (2, feat, wide), (orow, d)]
    n_small = len(masks) + 3
    copies += n_small
    out_shape = [jax.ShapeDtypeStruct(shape, bf16) for shape in shapes]
    out_shape.append(jax.ShapeDtypeStruct((16, d), f32))
    held = [
        (tokens, d), (d, mine), (d, wide), (mine, d), (HD, d), (feat, mine), (feat, wide), (orow, d),
        (tokens, wide), (tokens, HD), (tokens, HD), (tokens, wide), (tokens, mine),
    ]
    result = pl.pallas_call(
        functools.partial(layer_kernel, masks, top, length),
        out_shape=out_shape,
        in_specs=[ANY] * 6 + [VMEM] * 4,
        out_specs=[ANY] * len(shapes) + [VMEM],
        scratch_shapes=[pltpu.VMEM(shape, bf16) for shape in held]
        + [
            pltpu.VMEM(shape, f32)
            for shape in (
                (tokens, 256), (length, HD), (length, HD), (8, d), (8, wide), (8, mine), (8, mine), (16, 128),
                (n_small, 16, d),
            )
        ]
        + [
            pltpu.SemaphoreType.DMA((copies,)),
            pltpu.SemaphoreType.DMA((copies,)),
            pltpu.SemaphoreType.DMA((8,)),
        ],
        compiler_params=pltpu.CompilerParams(
            collective_id=0, has_side_effects=True, vmem_limit_bytes=60 * 2**20
        ),
        name="layer",
    )(x, e, up, qkv, down, out, seg, table, e, vec)
    stage = len(masks)
    at = N_HBM + 2 * stage * 4
    down_new = result[N_HBM + 2 * stage * 3 - 1]
    norm_final, branch_final = result[at + 5], result[at + 11]
    up_new, qkv_new, out_new, small = result[at + 12 : at + 16]
    return norm_final, branch_final, up_new, qkv_new, out_new, down_new, small


def adam_body(rate, decay, w, m, v, grad, m_out, v_out, w_out):
    g = grad[...].astype(f32).reshape(w.shape)
    m_new, v_new, w_new = adam_step(w[...], m[...], v[...], g, rate, decay)
    w_out[...] = w_new
    m_out[...] = m_new
    v_out[...] = v_new


def update_kernel(
    chunk, rates,
    x, e, vec, norm_final, branch_final, qkv_g, out_g, up_g, down_g,
    qw, qm, qv, ow, om, ov, uw, um, uv, dw, dm, dv,
    layer_output, input_grad, qm_o, qv_o, qw_o, om_o, ov_o, ow_o, um_o, uv_o, uw_o, dm_o, dv_o, dw_o,
):
    feat = uw.shape[0]
    rate, rate_out = rates

    def pipeline(body, grid, ins, outs):
        pltpu.emit_pipeline(
            body, grid=grid, in_specs=[s for _, s in ins], out_specs=[s for _, s in outs]
        )(*[r for r, _ in ins], *[r for r, _ in outs])

    body = functools.partial(adam_body, rate, decay_rate)
    spec = pl.BlockSpec((1, feat, HD), lambda c, q: (c, 0, q))
    grad = pl.BlockSpec((1, feat, HD), lambda c, q: (q, 0, c))
    pipeline(
        body, (3, 2), [(qw, spec), (qm, spec), (qv, spec), (qkv_g, grad)], [(qm_o, spec), (qv_o, spec), (qw_o, spec)]
    )
    spec = pl.BlockSpec((feat, chunk), lambda h, q: (0, h * 2 + q))
    grad = pl.BlockSpec((1, feat, chunk), lambda h, q: (q, 0, h))
    pipeline(
        body,
        (uw.shape[1] // chunk // 2, 2),
        [(uw, spec), (um, spec), (uv, spec), (up_g, grad)],
        [(um_o, spec), (uv_o, spec), (uw_o, spec)],
    )
    rows = min(dw.shape[0], 64)
    spec = pl.BlockSpec((rows, dw.shape[1]), lambda i: (i, 0))
    pipeline(
        body,
        (dw.shape[0] // rows,),
        [(dw, spec), (dm, spec), (dv, spec), (down_g, spec)],
        [(dm_o, spec), (dv_o, spec), (dw_o, spec)],
    )
    half = ow.shape[1] // 2
    spec = pl.BlockSpec((ow.shape[0], half), lambda i: (0, i))
    pipeline(
        functools.partial(adam_body, rate_out, decay_rate),
        (2,),
        [(ow, spec), (om, spec), (ov, spec), (out_g, spec)],
        [(om_o, spec), (ov_o, spec), (ow_o, spec)],
    )

    def tokens(x_ref, e_ref, n_ref, b_ref, out_ref, grad_ref):
        stream = x_ref[...].astype(f32)
        bias = vec[4:5, :] + vec[5:6, :]
        out_ref[...] = stream + (b_ref[0].astype(f32) + b_ref[1].astype(f32)) + bias
        scaled = n_ref[0].astype(f32) + n_ref[1].astype(f32)
        centred = stream - jnp.mean(stream, axis=-1, keepdims=True)
        inverse = lax.rsqrt(jnp.mean(centred * centred, axis=-1, keepdims=True) + norm_eps)
        normal = centred * inverse
        grad_ref[...] = e_ref[...].astype(f32) + inverse * (
            scaled
            - jnp.mean(scaled, axis=-1, keepdims=True)
            - normal * jnp.mean(scaled * normal, axis=-1, keepdims=True)
        )

    rows = 64
    d = x.shape[1]
    one = pl.BlockSpec((rows, d), lambda i: (i, 0))
    two = pl.BlockSpec((2, rows, d), lambda i: (0, i, 0))
    pipeline(
        tokens,
        (x.shape[0] // rows,),
        [(x, one), (e, one), (norm_final, two), (branch_final, two)],
        [(layer_output, one), (input_grad, one)],
    )


def run_update(chunk, rates, x, e, vec, finals, grads, weights):
    flat = [w for group in weights for w in group]
    tokens = jax.ShapeDtypeStruct(x.shape, f32)
    out_shape = [tokens, tokens] + [jax.ShapeDtypeStruct(w.shape, f32) for w in flat]
    return pl.pallas_call(
        functools.partial(update_kernel, chunk, rates),
        out_shape=out_shape,
        in_specs=[ANY, ANY, VMEM] + [ANY] * (6 + len(flat)),
        out_specs=[ANY] * len(out_shape),
        compiler_params=pltpu.CompilerParams(vmem_limit_bytes=48 * 2**20),
        name="update",
    )(x, e, vec, *finals, *grads, *flat)


def make_local(fsdp, tp):
    masks = [1 << b for b in range(2, fsdp.bit_length() - 1)] + [1]
    top = fsdp // 2

    def local(
        layer_input,
        out_cotangent,
        segments,
        qkv_weight,
        qkv_first,
        qkv_second,
        out_weight,
        out_first,
        out_second,
        up_weight,
        up_first,
        up_second,
        down_weight,
        down_first,
        down_second,
        small_params,
        small_first,
        small_second,
    ):
        d = layer_input.shape[1]
        length = segments.shape[1]
        chunk = 2 * down_weight.shape[1]
        lanes = np.arange(128)
        rate = 10000.0 ** (-(2.0 * (lanes % (ROT // 2))) / ROT)
        angle = np.arange(length)[:, None] * rate[None]
        rates = np.broadcast_to(rate, angle.shape)
        table = jnp.asarray(np.concatenate([np.cos(angle), np.sin(angle), rates], 1), f32)
        vec = small_params.reshape(-1, d)
        norm_final, branch_final, up_new, qkv_new, out_new, down_new, small = run_layer(
            masks, top, length, tp, layer_input, out_cotangent, up_weight[0], qkv_weight[0], down_weight[0],
            out_weight[0], segments, table, vec,
        )
        weights = (
            (qkv_weight[0], qkv_first[0], qkv_second[0]),
            (out_weight[0], out_first[0], out_second[0]),
            (up_weight[0], up_first[0], up_second[0]),
            (down_weight[0], down_first[0], down_second[0]),
        )
        results = run_update(
            chunk, (d ** (-0.5), 4.0 * d ** (-0.5)), layer_input, out_cotangent, vec, (norm_final, branch_final),
            (qkv_new, out_new, up_new, down_new), weights,
        )
        small_total = jnp.concatenate([small[0:5], small[4:5], small[5:12]]).reshape(1, -1)
        small_updated = adam_step(small_params, small_first, small_second, small_total, rate_vector, 0.0)
        return (*results[:2], *[w[None] for w in results[2:]], *small_updated)

    return local


def solution(mesh):
    tokens = P(("fsdp", "tp"), None)
    inner = P(None, ("tp", "fsdp"), None)
    qkv = P(None, None, "fsdp", "tp")
    up = P(None, "fsdp", "tp")
    weights = (qkv,) * 3 + (inner,) * 3 + (up,) * 3 + (inner,) * 3 + (P(),) * 3
    return jax.shard_map(
        make_local(mesh.shape["fsdp"], mesh.shape["tp"]),
        mesh=mesh,
        in_specs=(tokens, tokens, P("fsdp", None)) + weights,
        out_specs=(tokens, tokens) + weights,
        check_vma=False,
    )
```

time: 534 us -> 438 us (0.82)
  local copies, waits for them, and re-layouts: 42.7 us -> 6.49 us
  other arithmetic: 36.9 us -> 3.25 us
  Pallas kernels: 442 us -> 420 us
    pallas_call x1, Pallas kernels: 442 us -> 394 us  [run_layer(): pl.pallas_call(functools.partial(layer_kernel, masks, top, length), out_s...]
    pallas_call x0 -> x1, Pallas kernels: none -> 26 us  [run_update(): pl.pallas_call(functools.partial(update_kernel, chunk, rates), out_shape=...]
    unnamed x62 -> x26, local copies, waits for them, and re-layouts: 20.3 us -> 3.97 us
    convert_element_type x7 -> x0, local copies, waits for them, and re-layouts: 15.6 us -> none  [the longest x5 12 us: local(): grad.astype(f32)]
    sub x5 -> x1, other arithmetic: 16.1 us -> 1.44 us  [adam_step(): weight - rate * (first_hat / (jnp.sqrt(second_hat) + adam_eps) + decay *...]
    convert_element_type x8 -> x0, other arithmetic: 8.16 us -> none  [the longest x1 2.86 us: local(): down16 = down_weight[0].astype(bf16)]
    select_n x2 -> x0, other arithmetic: 5.61 us -> none  [the longest x1 5.6 us: local(): jnp.where(lane < ROT, jnp.where(lane < half, -1.0, 1.0) * jnp.sin(angle),...]
  transfers between devices with their start and end apart: 1 -> 0, of which waited for: 0 -> 0; matrix products, arithmetic and copies ran while one was open for 5% -> 0% of each run, Pallas kernels for 0% -> 0%
where the time goes in v5:
time: 438 us; the launch traced here: 431 us
  Pallas kernels  420 us (96%)
  local copies, waits for them, and re-layouts  6.49 us (1%)
    pallas_call x1, Pallas kernels, run_layer(): pl.pallas_call(functools.partial(layer_kernel, masks, top, length), out_s...  394 us
    pallas_call x1, Pallas kernels, run_update(): pl.pallas_call(functools.partial(update_kernel, chunk, rates), out_shape=...  26 us

profile of v5, /device:TPU:30, one launch (start us, length us, event | category | flops | bytes accessed | tf_op | source)
XLA Modules:
  0.0 431.4 jit_solution(11798641187872320214)
XLA Ops:
  0.7 0.5 broadcast.21
  1.2 1.8 reduce.3
  3.0 0.7 reshape.76.vec
  3.6 0.0 copy-start.9
  3.6 0.0 copy-start.10
  3.6 0.0 copy-start.11
  3.6 0.0 copy-start.1
  3.6 0.0 copy-start.2
  3.7 0.0 copy-start.3
  3.7 0.0 copy-start.6
  3.7 0.0 copy-start.7
  3.7 394.4 %layer.1 = (bf16[2048,2048]{1,0:T(8,128)(2,1)}, bf16[2048,2048]{1,0:T(8,128)(2,1)}, bf16[2048,2048]{1,0:T(8,128)(2,1)}, bf16[2048,1024]{1,0:T(8,128)(2,1)}, bf16...) custom-call(bf16[256,2048]{1,0:T(8,128)(2,1)} %x.3, ...), custom_call_target="tpu_custom_call" | custom-call | tf_op jit(solution)/shard_map/layer/pallas_call | solution.py:956
  398.1 0.0 copy-start
  398.1 1.0 slice.9
  399.1 0.8 slice.8
  399.9 0.1 copy.36
  400.1 0.0 copy-done.9
  400.1 0.0 copy-done.10
  400.1 0.0 copy-done.11
  400.1 1.4 multiply_subtract_fusion
  401.5 0.0 copy-done.1
  401.5 0.0 copy-done.2
  401.5 0.0 copy-done.3
  401.5 0.0 copy-done.6
  401.5 0.0 copy-done.7
  401.6 0.0 copy-done
  401.6 0.0 copy-start.4
  401.6 1.2 copy-done.4
  402.8 0.0 copy-start.5
  402.8 1.1 copy-done.5
  403.9 0.9 copy-done.8
  404.9 26.0 %update.1 = (f32[256,2048]{1,0:T(8,128)}, f32[256,2048]{1,0:T(8,128)}, f32[3,256,512]{2,1,0:T(8,128)}, f32[3,256,512]{2,1,0:T(8,128)}, f32[3,256,512]{2,1,0:T(8,...) custom-call(bf16[256,2048]{1,0:T(8,128)(2,1)S(1)} %copy-done.1, ...), custom_call_target="tpu_custom_call" | custom-call | tf_op jit(solution)/shard_map/update/pallas_call | solution.py:1070
  (2 shorter events, 0.0 us)
Async XLA Ops:
  3.6 396.4 %copy-start.9 = (f32[1,26624]{1,0:T(1,128)S(1)}, f32[1,26624]{1,0:T(1,128)}, u32[]{:S(2)}) copy-start(f32[1,26624]{1,0:T(1,128)} %param.34) | copy-start | bytes 319492
  3.6 396.4 %copy-start.10 = (f32[1,26624]{1,0:T(1,128)S(1)}, f32[1,26624]{1,0:T(1,128)}, u32[]{:S(2)}) copy-start(f32[1,26624]{1,0:T(1,128)} %param.36) | copy-start | bytes 319492
  3.6 396.4 %copy-start.11 = (f32[1,26624]{1,0:T(1,128)S(1)}, f32[1,26624]{1,0:T(1,128)}, u32[]{:S(2)}) copy-start(f32[1,26624]{1,0:T(1,128)} %param.35) | copy-start | bytes 319492
  3.6 397.9 %copy-start.1 = (bf16[256,2048]{1,0:T(8,128)(2,1)S(1)}, bf16[256,2048]{1,0:T(8,128)(2,1)}, u32[]{:S(2)}) copy-start(bf16[256,2048]{1,0:T(8,128)(2,1)} %x.3) | copy-start | bytes 3145732
  3.6 397.9 %copy-start.2 = (f32[1,64,2048]{2,1,0:T(8,128)S(1)}, f32[1,64,2048]{2,1,0:T(8,128)}, u32[]{:S(2)}) copy-start(f32[1,64,2048]{2,1,0:T(8,128)} %param.25) | copy-start | bytes 1572868
  3.7 397.9 %copy-start.3 = (f32[13,2048]{1,0:T(8,128)S(1)}, f32[13,2048]{1,0:T(8,128)}, u32[]{:S(2)}) copy-start(f32[13,2048]{1,0:T(8,128)} %reshape.76.vec) | copy-start | bytes 319492
  3.7 397.9 %copy-start.6 = (f32[1,64,2048]{2,1,0:T(8,128)S(1)}, f32[1,64,2048]{2,1,0:T(8,128)}, u32[]{:S(2)}) copy-start(f32[1,64,2048]{2,1,0:T(8,128)} %param.26) | copy-start | bytes 1572868
  3.7 397.9 %copy-start.7 = (f32[1,64,2048]{2,1,0:T(8,128)S(1)}, f32[1,64,2048]{2,1,0:T(8,128)}, u32[]{:S(2)}) copy-start(f32[1,64,2048]{2,1,0:T(8,128)} %param.27) | copy-start | bytes 1572868
  398.1 3.5 copy-start
  401.6 1.2 copy-start.4
  402.8 1.1 copy-start.5
  403.9 0.9 copy-start.8
